TPU v7x, 32 devices: a whole 2x2x4 slice. The times are simulated.
32 devices in a mesh: seq: 4 (over x, core), head: 2 (over y), dp: 4 (over z).
Axes of the slice: x: 2, y: 2, z: 4, core: 2. Of those that a mesh axis runs over, the one named last changes fastest.
Arguments:
- tokens: bfloat16 [8, 1024, 1024], P('dp', 'seq'), may hold values from -6 to 6
- segment_ids: int32 [8, 1024], P('dp', 'seq'), may hold values from 0 to 6, as said below
- ln1_gain: float32 [1024], replicated, may hold values from 0.5 to 1.5
- ln1_bias: float32 [1024], replicated, may hold values from -2 to 2
- qkv_weight: bfloat16 [1024, 3, 1024], P(None, None, 'head'), may hold values from -0.1875 to 0.1875
- qv_bias: float32 [2, 1024], P(None, 'head'), may hold values from -3 to 3
- out_weight: bfloat16 [1024, 1024], P('head'), may hold values from -0.75 to 0.75
- out_bias: float32 [1024], replicated, may hold values from -3 to 3
- ln2_gain: float32 [1024], replicated, may hold values from 0.5 to 1.5
- ln2_bias: float32 [1024], replicated, may hold values from -2 to 2
- up_weight: bfloat16 [1024, 4096], P(None, 'head'), may hold values from -0.1875 to 0.1875
- up_bias: float32 [4096], P('head'), may hold values from -3 to 3
- down_weight: bfloat16 [4096, 1024], P('head'), may hold values from -0.09375 to 0.09375
- down_bias: float32 [1024], replicated, may hold values from -3 to 3
- out_cotangent: bfloat16 [8, 1024, 1024], P('dp', 'seq'), may hold values from -6 to 6
Outputs:
- output: bfloat16 [8, 1024, 1024], P('dp', 'seq')
- tokens_grad: bfloat16 [8, 1024, 1024], P('dp', 'seq')
- ln1_gain_grad: float32 [1024], P(('seq', 'dp'))
- ln1_bias_grad: float32 [1024], P(('seq', 'dp'))
- qkv_weight_grad: float32 [1024, 3, 1024], P(('seq', 'dp'), None, 'head')
- qv_bias_grad: float32 [2, 1024], P(None, ('head', 'seq', 'dp'))
- out_weight_grad: float32 [1024, 1024], P('head', ('seq', 'dp'))
- out_bias_grad: float32 [1024], P(('seq', 'dp'))
- ln2_gain_grad: float32 [1024], P(('seq', 'dp'))
- ln2_bias_grad: float32 [1024], P(('seq', 'dp'))
- up_weight_grad: float32 [1024, 4096], P(('seq', 'dp'), 'head')
- up_bias_grad: float32 [4096], P(('head', 'seq', 'dp'))
- down_weight_grad: float32 [4096, 1024], P('head', ('seq', 'dp'))
- down_bias_grad: float32 [1024], P(('seq', 'dp'))
Inputs may be any that keep to these rules, and one draw needn't show every extreme that they name: `segment_ids`: scene numbers never fall along a sequence.
All inputs are finite; a program needn't handle non-finite values.
Results may differ from a plain program's by a relative error of at most 0.015.
Values may be sent and summed in bfloat16 or wider, within the bound.
A program may use at most 320 MiB of HBM per device.

v0:
```python
import jax
import jax.numpy as jnp
from jax import lax
from jax.sharding import PartitionSpec as P

HEAD_DIM = 64


EPSILON = 1e-05
MASKED = -1e30


def layer_norm(inputs, gain, shift):
    center = jnp.mean(inputs, axis=-1, keepdims=True)
    centred = inputs - center
    spread = jnp.mean(centred * centred, axis=-1, keepdims=True)
    inverse = lax.rsqrt(spread + EPSILON)
    normed = centred * inverse
    return (normed * gain + shift, normed, inverse)


def norm_backward(upstream, normed, inverse, gain):
    scaled = upstream * gain
    centred = scaled - jnp.mean(scaled, axis=-1, keepdims=True)
    return inverse * (centred - normed * jnp.mean(scaled * normed, axis=-1, keepdims=True))


def gelu_tanh(inputs):
    return jax.nn.gelu(inputs, approximate=True)


def span_for(length):
    span_size = length
    while span_size > 1024 and span_size % 2 == 0:
        span_size = span_size // 2
    return span_size


def span_rows(arrays, offset, span_size, axis_number):
    return tuple(
        (lax.dynamic_slice_in_dim(item, offset, span_size, axis_number) for item in arrays)
    )


def key_slices(portion, offset, span_size, head_count):
    key_rows, values, key_seg = span_rows(portion, offset, span_size, 1)
    seq_count = key_rows.shape[0]
    key_block = key_rows.reshape(seq_count, span_size, head_count, -1)
    value_block = values.reshape(seq_count, span_size, head_count, -1)
    return (key_block, value_block, key_seg)


def attend(carried, portion, queries, query_seg):
    length = portion[0].shape[1]
    span_size = span_for(length)
    head_count = queries.shape[2]

    def advance(number, state):
        weighted, running, denominator = state
        key_block, value_block, seg_block = key_slices(
            portion, number * span_size, span_size, head_count
        )
        scores = (
            jnp.einsum("sqhd,skhd->shqk", queries, key_block, preferred_element_type=jnp.float32)
            * 0.125
        )
        allowed = query_seg[:, None, :, None] == seg_block[:, None, None, :]
        masked = jnp.where(allowed, scores, MASKED)
        updated = jnp.maximum(running, jnp.max(masked, axis=-1, keepdims=True))
        weights = jnp.where(allowed, jnp.exp(masked - updated), 0.0)
        rescale = jnp.exp(running - updated)
        weighted = weighted * rescale + jnp.einsum(
            "shqk,skhd->shqd",
            weights.astype(jnp.bfloat16),
            value_block,
            preferred_element_type=jnp.float32,
        )
        denominator = denominator * rescale + jnp.sum(weights, axis=-1, keepdims=True)
        return (weighted, updated, denominator)

    return lax.fori_loop(0, length // span_size, advance, carried)


def block_terms(queries, query_seg, grad_heads, stats, key_block, value_block, seg_block):
    running, denominator, delta = stats
    scores = (
        jnp.einsum("sqhd,skhd->shqk", queries, key_block, preferred_element_type=jnp.float32)
        * 0.125
    )
    allowed = query_seg[:, None, :, None] == seg_block[:, None, None, :]
    log_total = running + jnp.log(denominator)
    probs = jnp.exp(jnp.where(allowed, scores - log_total, MASKED))
    weights_low = jnp.exp(jnp.where(allowed, scores - running, MASKED)).astype(jnp.bfloat16)
    grad_probs = jnp.einsum(
        "sqhd,skhd->shqk", grad_heads, value_block, preferred_element_type=jnp.float32
    )
    grad_scores = (probs * (grad_probs - delta)).astype(jnp.bfloat16)
    return (grad_scores, weights_low)


def value_share(weights_low, grad_heads, denominator):
    scaled = grad_heads.astype(jnp.float32) / jnp.transpose(denominator, (0, 2, 1, 3))
    return jnp.einsum(
        "shqk,sqhd->skhd", weights_low.astype(jnp.float32), scaled, precision=lax.Precision.HIGHEST
    )


def attend_back(portion, queries, query_seg, grad_heads, stats):
    seq_count, length, local_width = portion[0].shape
    head_count = queries.shape[2]
    span_size = span_for(length)

    def advance(number, state):
        grad_query, key_terms, value_terms = state
        offset = number * span_size
        key_block, value_block, seg_block = key_slices(portion, offset, span_size, head_count)
        grad_scores, weights_low = block_terms(
            queries, query_seg, grad_heads, stats, key_block, value_block, seg_block
        )
        grad_query = grad_query + jnp.einsum(
            "shqk,skhd->sqhd", grad_scores, key_block, preferred_element_type=jnp.float32
        )
        key_part = jnp.einsum(
            "shqk,sqhd->skhd", grad_scores, queries, preferred_element_type=jnp.float32
        )
        key_part = key_part.reshape(seq_count, span_size, local_width) * 0.125
        value_part = value_share(weights_low, grad_heads, stats[1]).reshape(
            seq_count, span_size, local_width
        )
        key_terms = lax.dynamic_update_slice_in_dim(key_terms, key_part, offset, 1)
        value_terms = lax.dynamic_update_slice_in_dim(value_terms, value_part, offset, 1)
        return (grad_query, key_terms, value_terms)

    start_state = (
        jnp.zeros(queries.shape, jnp.float32),
        jnp.zeros((seq_count, length, local_width), jnp.float32),
        jnp.zeros((seq_count, length, local_width), jnp.float32),
    )
    return lax.fori_loop(0, length // span_size, advance, start_state)


def shards(
    tokens,
    segment_ids,
    ln1_gain,
    ln1_bias,
    qkv_weight,
    qv_bias,
    out_weight,
    out_bias,
    ln2_gain,
    ln2_bias,
    up_weight,
    up_bias,
    down_weight,
    down_bias,
    out_cotangent,
):
    seq_count, block_rows, features = tokens.shape
    row_count = seq_count * block_rows
    local_width = qkv_weight.shape[2]
    head_count = local_width // HEAD_DIM
    inputs = tokens.astype(jnp.float32).reshape(row_count, features)
    first_pre, normed1, inverse1 = layer_norm(inputs, ln1_gain, ln1_bias)
    first = first_pre.astype(jnp.bfloat16)
    projected = jnp.einsum("rd,dcf->rcf", first, qkv_weight, preferred_element_type=jnp.float32)
    queries = (
        (projected[:, 0] + qv_bias[0])
        .astype(jnp.bfloat16)
        .reshape(seq_count, block_rows, head_count, HEAD_DIM)
    )
    key_rows = projected[:, 1].astype(jnp.bfloat16).reshape(seq_count, block_rows, local_width)
    values = (
        (projected[:, 2] + qv_bias[1])
        .astype(jnp.bfloat16)
        .reshape(seq_count, block_rows, local_width)
    )
    query_seg = segment_ids.astype(jnp.bfloat16)
    stat_shape = (seq_count, head_count, block_rows, 1)
    start_state = (
        jnp.zeros((seq_count, head_count, block_rows, HEAD_DIM), jnp.float32),
        jnp.full(stat_shape, MASKED, jnp.float32),
        jnp.zeros(stat_shape, jnp.float32),
    )
    weighted, running, denominator = attend(
        start_state,
        (
            lax.all_gather(key_rows, "seq", axis=1, tiled=True),
            lax.all_gather(values, "seq", axis=1, tiled=True),
            lax.all_gather(query_seg, "seq", axis=1, tiled=True),
        ),
        queries,
        query_seg,
    )
    heads_full = jnp.transpose(weighted / denominator, (0, 2, 1, 3))
    heads_low = heads_full.astype(jnp.bfloat16).reshape(row_count, local_width)
    branch = lax.psum(
        jnp.dot(heads_low, out_weight, preferred_element_type=jnp.float32).astype(jnp.bfloat16),
        "head",
    ).astype(jnp.float32)
    middle = inputs + branch + out_bias
    second_pre, normed2, inverse2 = layer_norm(middle, ln2_gain, ln2_bias)
    second = second_pre.astype(jnp.bfloat16)
    hidden = jnp.dot(second, up_weight, preferred_element_type=jnp.float32) + up_bias
    activated, gelu_pullback = jax.vjp(gelu_tanh, hidden)
    act_low = activated.astype(jnp.bfloat16)
    mlp_out = lax.psum(
        jnp.dot(act_low, down_weight, preferred_element_type=jnp.float32).astype(jnp.bfloat16),
        "head",
    ).astype(jnp.float32)
    output = (
        (middle + mlp_out + down_bias).astype(jnp.bfloat16).reshape(seq_count, block_rows, features)
    )
    cotangent = out_cotangent.reshape(row_count, features)
    grad_down_bias = jnp.sum(cotangent.astype(jnp.float32), axis=0)
    grad_down_weight = jnp.einsum(
        "rf,rd->fd", act_low, cotangent, preferred_element_type=jnp.float32
    )
    grad_act = jnp.einsum("rd,fd->rf", cotangent, down_weight, preferred_element_type=jnp.float32)
    grad_hidden = gelu_pullback(grad_act)[0].astype(jnp.bfloat16)
    grad_up_bias = jnp.sum(grad_hidden.astype(jnp.float32), axis=0)
    grad_up_weight = jnp.einsum(
        "rd,rf->df", second, grad_hidden, preferred_element_type=jnp.float32
    )
    grad_second = lax.psum(
        jnp.einsum("rf,df->rd", grad_hidden, up_weight, preferred_element_type=jnp.float32).astype(
            jnp.bfloat16
        ),
        "head",
    ).astype(jnp.float32)
    grad_ln2_gain = jnp.sum(grad_second * normed2, axis=0)
    grad_ln2_bias = jnp.sum(grad_second, axis=0)
    grad_middle = cotangent.astype(jnp.float32) + norm_backward(
        grad_second, normed2, inverse2, ln2_gain
    )
    grad_branch = grad_middle.astype(jnp.bfloat16)
    grad_out_bias = jnp.sum(grad_branch.astype(jnp.float32), axis=0)
    grad_out_weight = jnp.einsum(
        "rf,rd->fd", heads_low, grad_branch, preferred_element_type=jnp.float32
    )
    grad_heads = jnp.einsum(
        "rd,fd->rf", grad_branch, out_weight, preferred_element_type=jnp.float32
    )
    grad_heads = grad_heads.astype(jnp.bfloat16).reshape(
        seq_count, block_rows, head_count, HEAD_DIM
    )
    delta = jnp.einsum("sqhd,sqhd->shq", grad_heads.astype(jnp.float32), heads_full)[..., None]
    stats = (running, denominator, delta)
    portion = (
        lax.all_gather(key_rows, "seq", axis=1, tiled=True),
        lax.all_gather(values, "seq", axis=1, tiled=True),
        lax.all_gather(query_seg, "seq", axis=1, tiled=True),
    )
    grad_query, key_terms, value_terms = attend_back(portion, queries, query_seg, grad_heads, stats)
    grad_keys, grad_values = (
        lax.psum_scatter(
            key_terms.astype(jnp.bfloat16), "seq", scatter_dimension=1, tiled=True
        ).astype(jnp.float32),
        lax.psum_scatter(
            value_terms.astype(jnp.bfloat16), "seq", scatter_dimension=1, tiled=True
        ).astype(jnp.float32),
    )
    query_low = (grad_query * 0.125).astype(jnp.bfloat16).reshape(row_count, local_width)
    key_low = grad_keys.astype(jnp.bfloat16).reshape(row_count, local_width)
    value_low = grad_values.astype(jnp.bfloat16).reshape(row_count, local_width)
    stacked = jnp.stack((query_low, key_low, value_low), axis=1)
    grad_qkv_weight = jnp.einsum("rd,rcf->dcf", first, stacked, preferred_element_type=jnp.float32)
    grad_qv_bias = jnp.stack(
        (
            jnp.sum(query_low.astype(jnp.float32), axis=0),
            jnp.sum(value_low.astype(jnp.float32), axis=0),
        )
    )
    grad_first = lax.psum(
        jnp.einsum("rcf,dcf->rd", stacked, qkv_weight, preferred_element_type=jnp.float32).astype(
            jnp.bfloat16
        ),
        "head",
    ).astype(jnp.float32)
    grad_ln1_gain = jnp.sum(grad_first * normed1, axis=0)
    grad_ln1_bias = jnp.sum(grad_first, axis=0)
    grad_tokens = (grad_middle + norm_backward(grad_first, normed1, inverse1, ln1_gain)).astype(
        jnp.bfloat16
    )
    grad_tokens = grad_tokens.reshape(seq_count, block_rows, features)
    summed = (
        lax.psum_scatter(grad_ln1_gain, ("seq", "dp"), scatter_dimension=0, tiled=True),
        lax.psum_scatter(grad_ln1_bias, ("seq", "dp"), scatter_dimension=0, tiled=True),
        lax.psum_scatter(grad_qkv_weight, ("seq", "dp"), scatter_dimension=0, tiled=True),
        lax.psum_scatter(grad_qv_bias, ("seq", "dp"), scatter_dimension=1, tiled=True),
        lax.psum_scatter(grad_out_weight, ("seq", "dp"), scatter_dimension=1, tiled=True),
        lax.psum_scatter(grad_out_bias, ("seq", "dp"), scatter_dimension=0, tiled=True),
        lax.psum_scatter(grad_ln2_gain, ("seq", "dp"), scatter_dimension=0, tiled=True),
        lax.psum_scatter(grad_ln2_bias, ("seq", "dp"), scatter_dimension=0, tiled=True),
        lax.psum_scatter(grad_up_weight, ("seq", "dp"), scatter_dimension=0, tiled=True),
        lax.psum_scatter(grad_up_bias, ("seq", "dp"), scatter_dimension=0, tiled=True),
        lax.psum_scatter(grad_down_weight, ("seq", "dp"), scatter_dimension=1, tiled=True),
        lax.psum_scatter(grad_down_bias, ("seq", "dp"), scatter_dimension=0, tiled=True),
    )
    return (
        output,
        grad_tokens,
        summed[0],
        summed[1],
        summed[2],
        summed[3],
        summed[4],
        summed[5],
        summed[6],
        summed[7],
        summed[8],
        summed[9],
        summed[10],
        summed[11],
    )


def solution(mesh):
    in_specs = (
        P("dp", "seq", None),
        P("dp", "seq"),
        P(),
        P(),
        P(None, None, "head"),
        P(None, "head"),
        P("head", None),
        P(),
        P(),
        P(),
        P(None, "head"),
        P("head"),
        P("head", None),
        P(),
        P("dp", "seq", None),
    )
    out_specs = (
        P("dp", "seq", None),
        P("dp", "seq", None),
        P(("seq", "dp")),
        P(("seq", "dp")),
        P(("seq", "dp"), None, "head"),
        P(None, ("head", "seq", "dp")),
        P("head", ("seq", "dp")),
        P(("seq", "dp")),
        P(("seq", "dp")),
        P(("seq", "dp")),
        P(("seq", "dp"), "head"),
        P(("head", "seq", "dp")),
        P("head", ("seq", "dp")),
        P(("seq", "dp")),
    )
    return jax.shard_map(shards, mesh=mesh, in_specs=in_specs, out_specs=out_specs, check_vma=False)
```

profile of v0, /device:TPU:0, one launch (start us, length us, event | category | flops | bytes accessed | tf_op | source)
XLA Modules:
  0.0 777.4 jit_solution(13267273470833764153)
XLA Ops:
  26.3 6.4 all_gather.12
  33.9 8.2 %all-gather.3.cloned.1.call-done = bf16[2,1024,512]{2,1,0:T(8,128)(2,1)} async-done(((bf16[2,256,512]{2,1,0:T(8,128)(2,1)}), bf16[2,1024,512]{2,1,0:T(8,128)(2,1)}) %all-gather.3.cloned.1.call-update) | async-done | bytes 2097168 | tf_op jit(solution)/shard_map/all_gather | solution.py:188
  46.1 5.3 select_reduce_fusion
  51.4 5.2 fusion
  57.3 9.5 %all-gather.5.cloned.1.call-done = bf16[2,1024,512]{2,1,0:T(8,128)(2,1)} async-done(((bf16[2,256,512]{2,1,0:T(8,128)(2,1)}), bf16[2,1024,512]{2,1,0:T(8,128)(2,1)}) %all-gather.5.cloned.1.call-update) | async-done | bytes 2097168 | tf_op jit(solution)/shard_map/all_gather | solution.py:189
  70.8 9.9 %fusion.80 = (bf16[2,256,8,64]{1,3,2,0:T(8,128)(2,1)S(1)}, f32[2,256,8,64]{1,3,2,0:T(8,128)}) fusion(f32[2,256,8]{1,2,0:T(8,128)S(1)} %bitcast_add_fusion.1, bf16[2,1024,8,64]{1,3,2,0:T(8,128)(2,1)} %bitcast.137, f32[2,8,256,1024]{3,2,1,0:T(8,128)} %copy-done.3, f32[2,8,256]{2,1,0:T(8,128)S(1)} %broadcast_maximum_fusion, ...), kind=kOutput, calls=%fused_computation.126 | convolution fusion | flops 558628864 | bytes 21020672 | tf_op jit(solution)/shard_map/while/body/eval_jaxpr/shqk,skhd->shqd/dot_general | solution.py:72
  84.5 39.6 %all-reduce.13.cloned.1.call-done = bf16[512,1024]{1,0:T(8,128)(2,1)} async-done(((bf16[512,1024]{1,0:T(8,128)(2,1)}), bf16[512,1024]{1,0:T(8,128)(2,1)}) %all-reduce.13.cloned.1.call-update) | async-done | bytes 1048592 | tf_op jit(solution)/shard_map/psum | solution.py:197
  132.1 5.0 convert_reduce_fusion
  142.0 40.0 %all-reduce.15.cloned.1.call-done = bf16[512,1024]{1,0:T(8,128)(2,1)} async-done(((bf16[512,1024]{1,0:T(8,128)(2,1)}), bf16[512,1024]{1,0:T(8,128)(2,1)}) %all-reduce.15.cloned.1.call-update) | async-done | bytes 1048592 | tf_op jit(solution)/shard_map/psum | solution.py:225
  196.1 11.6 %fusion.42 = bf16[2,8,64,1024]{3,2,1,0:T(8,128)(2,1)} fusion(f32[2,8,256,1024]{3,2,1,0:T(8,128)} %copy-done.3, f32[2,8,256]{2,1,0:T(8,128)S(1)} %broadcast_maximum_fusion, pred[2,256,1024]{2,1,0:T(8,128)(4,1)} %broadcast_compare_fusion, f32[2,256,8,64]{1,0,3,2:T(2,128)S(1)} %convert_divide_fusion), kind=kOutput, calls=%fused_computation.67 | convolution fusion | flops 3239051264 | bytes 20463616 | tf_op jit(solution)/shard_map/while/body/eval_jaxpr/shqk,sqhd->skhd/dot_general | solution.py:103
  210.8 10.0 %multiply_convert_fusion = bf16[2,8,256,1024]{3,2,1,0:T(8,128)(2,1)S(1)} fusion(f32[2,8,256,1024]{3,2,1,0:T(8,128)} %copy-done.3, f32[2,8,256]{2,1,0:T(8,128)S(1)} %multiply_reduce_fusion.1, f32[2,8,256]{2,1,0:T(8,128)S(1)} %get-tuple-element.111, pred[2,256,1024]{2,1,0:T(8,128)(4,1)S(1)} %copy-done.12, bf16[2,1024,8,64]{1,3,2,0:T(8,128)(2,1)S(1)} %bitcast.138, ...), kind=kOutput, calls=%fused_computation.1 | convolution fusion | flops 562036736 | bytes 28344320 | tf_op jit(solution)/shard_map/while/body/eval_jaxpr/sqhd,skhd->shqk/dot_general | solution.py:94
  225.0 7.4 convolution_convert_fusion.2
  245.2 28.1 %reduce-scatter.10.cloned.1.call-done = bf16[2,256,512]{1,2,0:T(8,128)(2,1)} async-done(((bf16[2,1024,512]{1,2,0:T(8,128)(2,1)}), bf16[2,256,512]{1,2,0:T(8,128)(2,1)}) %reduce-scatter.10.cloned.1.call-update) | async-done | bytes 524304 | tf_op jit(solution)/shard_map/reduce_scatter | solution.py:256
  275.4 4.2 bitcast_convert_fusion
  283.7 7.5 fusion.82
  291.5 8.3 %fusion.76 = f32[2048,1024]{0,1:T(8,128)} fusion(bf16[512,1024]{1,0:T(8,128)(2,1)} %bitcast.132, f32[512,2048]{1,0:T(8,128)} %copy-done.35, f32[2048]{0:T(1024)S(1)} %copy-done.32), kind=kOutput, calls=%fused_computation.124 | convolution fusion | flops 2157969408 | bytes 13639680 | tf_op jit(solution)/shard_map/rf,rd->fd/dot_general | solution.py:216
  299.9 6.2 fusion.51
  310.0 22.2 %reduce-scatter.22.cloned.1.call-done = f32[32,2]{1,0:T(8,128)} async-done(((f32[512,2]{1,0:T(8,128)}), f32[32,2]{1,0:T(8,128)}) %reduce-scatter.22.cloned.1.call-update) | async-done | bytes 272
  333.5 63.8 %all-reduce.17.cloned.1.call-done = (bf16[512,1024]{1,0:T(8,128)(2,1)}, bf16[512,1024]{1,0:T(8,128)(2,1)}) async-done(((bf16[512,1024]{1,0:T(8,128)(2,1)}, bf16[512,1024]{1,0:T(8,128)(2,1)}), (bf16[512,1024]{1,0:T(8,128)(2,1)}, bf16[512,1024]{1,0:T(8,128)(2,1)})) %all-reduce.17.cloned.1.call-update) | async-done | bytes 2097168 | tf_op jit(solution)/shard_map/psum | solution.py:207
  399.8 61.9 %all-reduce.7 = (f32[1024]{0:T(1024)S(1)}, f32[1024]{0:T(1024)S(1)}, f32[1024]{0:T(1024)S(1)}, f32[1024]{0:T(1024)S(1)}, f32[1024]{0:T(1024)S(1)}, /*index=5*/f32[2048]{0:T(1024)S(1)}, f32[1024]{0:T(1024)S(1)}) all-reduce(f32[1024]{0:T(1024)S(1)} %get-tuple-element.74, ...), channel_id=4, replica_groups=mesh['seq'=4,'head'=2,'dp'=4] {'seq','dp'}, use_global_device_ids=true, to_apply=%region_17.18.clone | all-reduce | flops 8192 | bytes 65536
  465.8 4.3 fusion.26
  470.1 101.8 %reduce-scatter.18.cloned.1.call-done = f32[64,2048]{1,0:T(8,128)} async-done(((f32[1024,2048]{1,0:T(8,128)}), f32[64,2048]{1,0:T(8,128)}) %reduce-scatter.18.cloned.1.call-update) | async-done | bytes 524304 | tf_op jit(solution)/shard_map/reduce_scatter | solution.py:295
  571.9 109.0 %reduce-scatter.20.cloned.1.call-done = f32[2048,64]{0,1:T(8,128)} async-done(((f32[2048,1024]{0,1:T(8,128)}), f32[2048,64]{0,1:T(8,128)}) %reduce-scatter.20.cloned.1.call-update) | async-done | bytes 524304 | tf_op jit(solution)/shard_map/reduce_scatter | solution.py:297
  680.9 89.3 %reduce-scatter.14.cloned.1.call-done = f32[64,3,512]{2,0,1:T(8,128)} async-done(((f32[1024,3,512]{2,0,1:T(8,128)}), f32[64,3,512]{2,0,1:T(8,128)}) %reduce-scatter.14.cloned.1.call-update) | async-done | bytes 393232 | tf_op jit(solution)/shard_map/reduce_scatter | solution.py:289
  (164 shorter events, 96.5 us)
Async XLA Ops:
  7.2 34.9 %all-gather.3.cloned.1.call-start = ((), (), s32[]{:S(2)}) async-start(), calls=%async_computation.7 | async-start | bytes 2621440 | tf_op jit(solution)/shard_map/all_gather | solution.py:188
  16.6 50.2 %all-gather.5.cloned.1.call-start = ((), (), s32[]{:S(2)}) async-start(), calls=%async_computation.8 | async-start | bytes 2621440 | tf_op jit(solution)/shard_map/all_gather | solution.py:189
  20.3 103.8 %all-reduce.13.cloned.1.call-start = ((), (), s32[]{:S(2)}) async-start(), calls=%async_computation.9 | async-start | bytes 2097152 | tf_op jit(solution)/shard_map/psum | solution.py:197
  20.4 5.9 copy-start.29
  51.4 5.9 copy-start.3
  70.8 11.3 %copy-start.19 = (bf16[512,1024]{1,0:T(8,128)(2,1)S(1)}, bf16[512,1024]{1,0:T(8,128)(2,1)}, u32[]{:S(2)}) copy-start(bf16[512,1024]{1,0:T(8,128)(2,1)} %param.21) | copy-start | bytes 3145732
  80.7 43.5 %copy-start.23 = (f32[1024]{0:T(1024)S(1)}, f32[1024]{0:T(1024)}, u32[]{:S(2)}) copy-start(f32[1024]{0:T(1024)} %param.22) | copy-start | bytes 12292
  83.9 44.6 %copy-start.25 = (f32[1024]{0:T(1024)S(1)}, f32[1024]{0:T(1024)}, u32[]{:S(2)}) copy-start(f32[1024]{0:T(1024)} %param.23) | copy-start | bytes 12292
  83.9 44.6 %copy-start.26 = (f32[1024]{0:T(1024)S(1)}, f32[1024]{0:T(1024)}, u32[]{:S(2)}) copy-start(f32[1024]{0:T(1024)} %param.24) | copy-start | bytes 12292
  83.9 98.1 %all-reduce.15.cloned.1.call-start = ((), (), s32[]{:S(2)}) async-start(), calls=%async_computation.10 | async-start | bytes 2097152 | tf_op jit(solution)/shard_map/psum | solution.py:225
  131.6 5.5 copy-start.35
  141.8 99.2 %reduce-scatter.12.cloned.1.call-start = ((), (), s32[]{:S(2)}) async-start(), calls=%async_computation.12 | async-start | bytes 2621440 | tf_op jit(solution)/shard_map/reduce_scatter | solution.py:259
  207.7 65.6 %reduce-scatter.10.cloned.1.call-start = ((), (), s32[]{:S(2)}) async-start(), calls=%async_computation.11 | async-start | bytes 2621440 | tf_op jit(solution)/shard_map/reduce_scatter | solution.py:256
  210.8 10.0 %copy-start.10 = (f32[2,256,8,64]{1,3,2,0:T(8,128)S(1)}, f32[2,256,8,64]{1,3,2,0:T(8,128)}, u32[]{:S(2)}) copy-start(f32[2,256,8,64]{1,3,2,0:T(8,128)} %copy.68) | copy-start | bytes 3145732
  224.7 107.5 %reduce-scatter.22.cloned.1.call-start = ((), (), s32[]{:S(2)}) async-start(), calls=%async_computation.17 | async-start | bytes 278528
  224.9 7.4 copy-start.7
  225.0 7.4 copy-start.9
  243.1 154.2 %all-reduce.17.cloned.1.call-start = ((), (), s32[]{:S(2)}) async-start(), calls=%async_computation.18 | async-start | bytes 4194304 | tf_op jit(solution)/shard_map/psum | solution.py:207
  279.6 190.5 %reduce-scatter.16.cloned.1.call-start = ((), (), s32[]{:S(2)}) async-start(), calls=%async_computation.14 | async-start | bytes 2228224 | tf_op jit(solution)/shard_map/reduce_scatter | solution.py:291
  283.6 288.3 %reduce-scatter.18.cloned.1.call-start = ((), (), s32[]{:S(2)}) async-start(), calls=%async_computation.15 | async-start | bytes 8912896 | tf_op jit(solution)/shard_map/reduce_scatter | solution.py:295
  291.2 389.7 %reduce-scatter.20.cloned.1.call-start = ((), (), s32[]{:S(2)}) async-start(), calls=%async_computation.16 | async-start | bytes 8912896 | tf_op jit(solution)/shard_map/reduce_scatter | solution.py:297
  299.8 470.4 %reduce-scatter.14.cloned.1.call-start = ((), (), s32[]{:S(2)}) async-start(), calls=%async_computation.13 | async-start | bytes 6684672 | tf_op jit(solution)/shard_map/reduce_scatter | solution.py:289
  306.1 91.2 %copy-start.24 = (f32[1024]{0:T(1024)S(1)}, f32[1024]{0:T(1024)}, u32[]{:S(2)}) copy-start(f32[1024]{0:T(1024)} %param.17) | copy-start | bytes 12292
  306.1 159.7 %copy-start.27 = (f32[1024]{0:T(1024)S(1)}, f32[1024]{0:T(1024)}, u32[]{:S(2)}) copy-start(f32[1024]{0:T(1024)} %param.28) | copy-start | bytes 12292
  (24 other events, 71.1 us)
Sparse Core Ops, SparseCore 0:
  16.7 25.2 all-gather.2
  44.2 22.5 all-gather.4
  84.0 40.0 all-reduce.12
  141.9 40.0 all-reduce.14
  207.8 31.4 reduce-scatter.11
  241.9 31.4 reduce-scatter.9
  276.8 55.2 reduce-scatter.21
  335.1 62.1 all-reduce.16
  402.1 61.6 reduce-scatter.15
  468.2 103.6 reduce-scatter.17
  576.6 104.3 reduce-scatter.19
  685.3 84.9 reduce-scatter.13
where the time goes:
time: 782 us; the launch traced here: 777 us
  waiting for transfers between devices  512 us (65%)
  matrix products  97.1 us (12%)
  blocking collectives  68.2 us (9%)
  local copies, waits for them, and re-layouts  45.7 us (6%)
  other arithmetic  36.7 us (5%)
  between operations  16.3 us (2%)
    reduce_scatter x1, waiting for transfers between devices, shards(): lax.psum_scatter(grad_down_weight, ('seq', 'dp'), scatter_dimension=1, ti...  109 us
    reduce_scatter x1, waiting for transfers between devices, shards(): lax.psum_scatter(grad_up_weight, ('seq', 'dp'), scatter_dimension=0, tile...  102 us
    reduce_scatter x1, waiting for transfers between devices, shards(): lax.psum_scatter(grad_qkv_weight, ('seq', 'dp'), scatter_dimension=0, til...  89.3 us
    psum x1, waiting for transfers between devices, shards(): lax.psum(jnp.dot(act_low, down_weight, preferred_element_type=jnp.float32...  63.8 us
    unnamed x1, blocking collectives  61.9 us
    psum x1, waiting for transfers between devices, shards(): lax.psum(jnp.einsum('rf,df->rd', grad_hidden, up_weight, preferred_elemen...  40 us
    psum x1, waiting for transfers between devices, shards(): lax.psum(jnp.dot(heads_low, out_weight, preferred_element_type=jnp.float3...  39.6 us
    reduce_scatter x1, waiting for transfers between devices, shards(): lax.psum_scatter(key_terms.astype(jnp.bfloat16), 'seq', scatter_dimension...  28.1 us
  transfers between devices with their start and end apart: 12, of which 10 were waited for; matrix products, arithmetic and copies ran while one was open for 14% of the time, Pallas kernels for 0%

commit v1 on v0

v1 whole, which is shorter than its diff:
```python
import functools

import jax
import jax.numpy as jnp
from jax import lax
from jax.experimental import pallas as pl
from jax.experimental.pallas import tpu as pltpu
from jax.sharding import PartitionSpec as P

HEAD_DIM = 64
LANES = 128
EPSILON = 1e-05
MASKED = -1e30
F32 = jnp.float32
LOW = jnp.bfloat16
NN = (((1,), (0,)), ((), ()))
NT = (((1,), (1,)), ((), ()))
TN = (((0,), (0,)), ((), ()))
VMEM_LIMIT = 60 * 2**20


def dot(a, b, dims=NN):
    return lax.dot_general(a, b, dims, preferred_element_type=F32)


def axis_size(name):
    return lax.axis_size(name)


def swap(value, axis, mask):
    return lax.ppermute(value, axis, [(i, i ^ mask) for i in range(axis_size(axis))])


def bits_of(count):
    return [1 << b for b in range(count.bit_length() - 1)]


def layer_norm(inputs, gain, shift):
    center = jnp.mean(inputs, axis=-1, keepdims=True)
    centred = inputs - center
    spread = jnp.mean(centred * centred, axis=-1, keepdims=True)
    inverse = lax.rsqrt(spread + EPSILON)
    normed = centred * inverse
    return (normed * gain + shift, normed, inverse)


def norm_backward(upstream, normed, inverse, gain):
    scaled = upstream * gain
    centred = scaled - jnp.mean(scaled, axis=-1, keepdims=True)
    return inverse * (centred - normed * jnp.mean(scaled * normed, axis=-1, keepdims=True))


def gelu_pair(v):
    c = 0.7978845608028654
    square = v * v
    t = jnp.tanh(c * v * (1.0 + 0.044715 * square))
    half = 0.5 * (1.0 + t)
    return v * half, half + (0.5 * c) * v * (1.0 - t * t) * (1.0 + 3.0 * 0.044715 * square)


def half_lanes(shape, head):
    lane = lax.broadcasted_iota(jnp.int32, shape, 1)
    return (lane < HEAD_DIM) if head == 0 else (lane >= HEAD_DIM)


def attend_kernel(n, q_ref, seg_ref, segk_ref, *refs):
    kv_refs = refs[:n]
    w_ref, attn_ref, low_ref, inv_ref = refs[n:]
    q = q_ref[...] * jnp.asarray(0.125, LOW)
    seg_q = seg_ref[0:1, :]
    for head in range(2):
        qh = jnp.where(half_lanes(q.shape, head), q, jnp.zeros_like(q))
        parts, top = [], None
        for m in range(n):
            s = dot(kv_refs[m][0], qh, NT)
            s = jnp.where(segk_ref[m] == seg_q, s, MASKED)
            peak = jnp.max(s, axis=0, keepdims=True)
            top = peak if top is None else jnp.maximum(top, peak)
            parts.append(s)
        total, mixed = 0.0, 0.0
        for m in range(n):
            w = jnp.exp(parts[m] - top)
            total = total + jnp.sum(w, axis=0, keepdims=True)
            wl = w.astype(LOW)
            w_ref[head, m] = wl
            vt = kv_refs[m][1].T[head * HEAD_DIM:(head + 1) * HEAD_DIM, :]
            mixed = mixed + dot(vt, wl)
        inverse = 1.0 / total
        inv_ref[0, head:head + 1, :] = inverse
        attn_ref[head * HEAD_DIM:(head + 1) * HEAD_DIM, :] = mixed * inverse
    low_ref[...] = attn_ref[...].T.astype(LOW)


def attend(q, seg_rows, seg_cols, kvs):
    n, (rows, width) = len(kvs), q.shape
    pairs = width // LANES
    step = lambda p: (0, p)
    kv_spec = pl.BlockSpec((2, rows, LANES), lambda p: (0, 0, p))
    return pl.pallas_call(
        functools.partial(attend_kernel, n),
        grid=(pairs,),
        in_specs=[
            pl.BlockSpec((rows, LANES), step),
            pl.BlockSpec((8, rows), lambda p: (0, 0)),
            pl.BlockSpec((n, rows, 1), lambda p: (0, 0, 0)),
        ]
        + [kv_spec] * n,
        out_specs=[
            pl.BlockSpec((2, n, rows, rows), lambda p: (p, 0, 0, 0)),
            pl.BlockSpec((LANES, rows), lambda p: (p, 0)),
            pl.BlockSpec((rows, LANES), step),
            pl.BlockSpec((1, 2, rows), lambda p: (p, 0, 0)),
        ],
        out_shape=[
            jax.ShapeDtypeStruct((2 * pairs, n, rows, rows), LOW),
            jax.ShapeDtypeStruct((width, rows), F32),
            jax.ShapeDtypeStruct((rows, width), LOW),
            jax.ShapeDtypeStruct((pairs, 2, rows), F32),
        ],
        compiler_params=pltpu.CompilerParams(vmem_limit_bytes=VMEM_LIMIT),
        cost_estimate=pl.CostEstimate(
            flops=2 * pairs * n * rows * rows * 256 * 4,
            bytes_accessed=2 * pairs * n * rows * rows * 2,
            transcendentals=2 * pairs * n * rows * rows,
        ),
    )(q, seg_rows, seg_cols, *kvs)


def attend_back_kernel(n, q_ref, g_ref, attn_ref, inv_ref, w_ref, *refs):
    kv_refs = refs[:n]
    dq_ref = refs[n]
    dkv_refs = refs[n + 1:2 * n + 1]
    dqt_ref = refs[2 * n + 1]
    q = q_ref[...]
    gt = g_ref[...].astype(F32).T
    qs, gs, gts, deltas = [], [], [], []
    for head in range(2):
        rows_h = slice(head * HEAD_DIM, (head + 1) * HEAD_DIM)
        part = (gt[rows_h] * inv_ref[0, head:head + 1, :]).astype(LOW)
        deltas.append(jnp.sum(part.astype(F32) * attn_ref[rows_h, :], axis=0, keepdims=True))
        zeros = jnp.zeros_like(part)
        full = jnp.concatenate([part, zeros] if head == 0 else [zeros, part], axis=0)
        gts.append(full)
        gs.append(full.T)
        qs.append(jnp.where(half_lanes(q.shape, head), q, jnp.zeros_like(q)))
    dqt = [0.0, 0.0]
    for m in range(n):
        kt = kv_refs[m][0].T
        v = kv_refs[m][1]
        dk = dv = 0.0
        for head in range(2):
            w = w_ref[head, m]
            ds = (w.astype(F32) * (dot(v, gts[head]) - deltas[head])).astype(LOW)
            dk = dk + dot(ds, qs[head])
            dv = dv + dot(w, gs[head])
            dqt[head] = dqt[head] + dot(kt[head * HEAD_DIM:(head + 1) * HEAD_DIM, :], ds)
        dkv_refs[m][0] = (dk * 0.125).astype(LOW)
        dkv_refs[m][1] = dv.astype(LOW)
    dqt_ref[0:HEAD_DIM, :] = dqt[0]
    dqt_ref[HEAD_DIM:LANES, :] = dqt[1]
    dq_ref[...] = (dqt_ref[...].T * 0.125).astype(LOW)


def attend_back(q, g, attn, inverse, weights, kvs):
    n, (rows, width) = len(kvs), q.shape
    pairs = width // LANES
    step = lambda p: (0, p)
    kv_spec = pl.BlockSpec((2, rows, LANES), lambda p: (0, 0, p))
    out = pl.pallas_call(
        functools.partial(attend_back_kernel, n),
        grid=(pairs,),
        in_specs=[
            pl.BlockSpec((rows, LANES), step),
            pl.BlockSpec((rows, LANES), step),
            pl.BlockSpec((LANES, rows), lambda p: (p, 0)),
            pl.BlockSpec((1, 2, rows), lambda p: (p, 0, 0)),
            pl.BlockSpec((2, n, rows, rows), lambda p: (p, 0, 0, 0)),
        ]
        + [kv_spec] * n,
        out_specs=[pl.BlockSpec((rows, LANES), step)] + [kv_spec] * n,
        out_shape=[jax.ShapeDtypeStruct((rows, width), LOW)]
        + [jax.ShapeDtypeStruct((2, rows, width), LOW)] * n,
        scratch_shapes=[pltpu.VMEM((LANES, rows), F32)],
        compiler_params=pltpu.CompilerParams(vmem_limit_bytes=VMEM_LIMIT),
        cost_estimate=pl.CostEstimate(
            flops=2 * pairs * n * rows * rows * 256 * 8,
            bytes_accessed=2 * pairs * n * rows * rows * 2,
            transcendentals=0,
        ),
    )(q, g, attn, inverse, weights, *kvs)
    return out[0], out[1:]


def gather_seq(block):
    bits = bits_of(axis_size("seq"))
    blocks = {0: block}
    for bit in reversed(bits):
        for m in list(blocks):
            blocks[m | bit] = swap(blocks[m], "seq", bit)
    return [blocks[m] for m in range(len(blocks))]


def scatter_seq(parts):
    parts = dict(enumerate(parts))
    for bit in bits_of(axis_size("seq")):
        for m in [m for m in sorted(parts, reverse=True) if m & bit]:
            got = swap(parts.pop(m).astype(LOW), "seq", bit)
            parts[m ^ bit] = parts[m ^ bit].astype(F32) + got.astype(F32)
    return parts[0].astype(F32)


def scatter_line(term):
    n = axis_size("dp")
    me = lax.axis_index("dp")
    rows = term.shape[0] // n
    block = lambda i: lax.dynamic_slice_in_dim(term, jnp.clip(i, 0, n - 1) * rows, rows, 0)
    up = down = None
    for k in range(n - 1, 0, -1):
        send_up = block(me + k) if up is None else block(me + k) + up
        send_down = block(me - k) if down is None else block(me - k) + down
        up = lax.ppermute(
            send_up.astype(LOW), "dp", [(i, i + 1) for i in range(n) if i + k < n]
        ).astype(F32)
        down = lax.ppermute(
            send_down.astype(LOW), "dp", [(i, i - 1) for i in range(n) if i - k >= 0]
        ).astype(F32)
    out = block(me)
    return out if n == 1 else out + up + down


def relative_columns(rows):
    n = axis_size("seq")
    me = lax.axis_index("seq")
    width = rows.shape[1] // n
    return [lax.dynamic_slice_in_dim(rows, (me ^ m) * width, width, 1) for m in range(n)]


def weight_grad(left, right):
    return scatter_line(scatter_seq([dot(part, right, TN) for part in left]))


def scatter_small(blocks):
    for axis in ("seq", "dp"):
        n = axis_size(axis)
        me = lax.axis_index(axis)
        bits = bits_of(n)
        rest = blocks.shape[1:]
        for bit in reversed(bits):
            low, high = blocks[:bit], blocks[bit:]
            mine = (me & bit) != 0
            send = jnp.where(mine, low, high)
            blocks = jnp.where(mine, high, low) + swap(send, axis, bit)
        blocks = blocks.reshape(rest)
    return blocks


def other_head(value):
    return swap(value, "head", 1)


def head_sum(value):
    value = value.astype(LOW)
    return value.astype(F32) + other_head(value).astype(F32)


def by_head(mine, other, axis):
    first = lax.axis_index("head") == 0
    return jnp.where(
        first,
        jnp.concatenate([mine, other], axis),
        jnp.concatenate([other, mine], axis),
    )


def shards(
    tokens,
    segment_ids,
    ln1_gain,
    ln1_bias,
    qkv_weight,
    qv_bias,
    out_weight,
    out_bias,
    ln2_gain,
    ln2_bias,
    up_weight,
    up_bias,
    down_weight,
    down_bias,
    out_cotangent,
):
    count, rows, features = tokens.shape
    local = qkv_weight.shape[2]
    hidden_local = up_weight.shape[1]
    n_seq, n_dp = axis_size("seq"), axis_size("dp")
    every = range(count)
    wq, wk, wv = (qkv_weight[:, c, :] for c in range(3))

    seg = gather_seq(segment_ids)
    seg_rows = [jnp.broadcast_to(segment_ids[s][None, :], (8, rows)) for s in every]
    seg_cols = [jnp.stack([part[s] for part in seg])[:, :, None] for s in every]

    half = out_weight.shape[0] // 2
    core = lax.axis_index("seq") & 1
    fetched = other_head(lax.dynamic_slice_in_dim(out_weight, core * half, half, 0))
    swapped = swap(fetched, "seq", 1)
    out_other = jnp.where(
        core == 0,
        jnp.concatenate([fetched, swapped], 0),
        jnp.concatenate([swapped, fetched], 0),
    )
    out_full = by_head(out_weight, out_other, 0)

    inputs, first, normed1, inverse1, queries, kvs = [], [], [], [], [], []
    for s in every:
        x = tokens[s].astype(F32)
        pre, normed, inverse = layer_norm(x, ln1_gain, ln1_bias)
        low = pre.astype(LOW)
        k = dot(low, wk).astype(LOW)
        v = (dot(low, wv) + qv_bias[1]).astype(LOW)
        kvs.append(gather_seq(jnp.stack([k, v])))
        queries.append((dot(low, wq) + qv_bias[0]).astype(LOW))
        inputs.append(x)
        first.append(low)
        normed1.append(normed)
        inverse1.append(inverse)

    attended = [attend(queries[s], seg_rows[s], seg_cols[s], kvs[s]) for s in every]

    outputs, second, act, g_hidden, g_middle, heads = [], [], [], [], [], []
    g_queries, g_kv = [], []
    vec = {
        name: 0.0 for name in ("out_b", "ln2_g", "ln2_b", "down_b", "up_b", "q_b", "v_b", "ln1_g", "ln1_b")
    }
    add = lambda name, value: vec.__setitem__(name, vec[name] + jnp.sum(value, axis=0))
    state = []
    for s in every:
        weights, attn_full, attn_low, inv_total = attended[s]
        mixed = by_head(attn_low, other_head(attn_low), 1)
        middle = inputs[s] + dot(mixed, out_full) + out_bias
        pre, normed2, inverse2 = layer_norm(middle, ln2_gain, ln2_bias)
        low = pre.astype(LOW)
        hidden = dot(low, up_weight) + up_bias
        activated, slope = gelu_pair(hidden)
        act_low = activated.astype(LOW)
        cot = out_cotangent[s]
        gh = (dot(cot, down_weight, NT) * slope).astype(LOW)
        g_second = head_sum(dot(gh, up_weight, NT))
        mlp = head_sum(dot(act_low, down_weight))
        outputs.append((middle + mlp + down_bias).astype(LOW))
        second.append(low)
        act.append(act_low)
        g_hidden.append(gh)
        heads.append(attn_low)
        state.append((normed2, inverse2, g_second))
        add("down_b", cot.astype(F32))
        add("up_b", gh.astype(F32))

    g_branch, g_first_parts = [], []
    for s in every:
        normed2, inverse2, g_second = state[s]
        weights, attn_full, attn_low, inv_total = attended[s]
        add("ln2_g", g_second * normed2)
        add("ln2_b", g_second)
        gm = out_cotangent[s].astype(F32) + norm_backward(g_second, normed2, inverse2, ln2_gain)
        gb = gm.astype(LOW)
        add("out_b", gb.astype(F32))
        g_attn = dot(gb, out_weight, NT).astype(LOW)
        dq, dkv = attend_back(queries[s], g_attn, attn_full, inv_total, weights, kvs[s])
        g_queries.append(dq)
        g_kv.append(scatter_seq(dkv).astype(LOW))
        g_middle.append(gm)
        g_branch.append(gb)

    join = lambda items: jnp.concatenate(items, axis=0)
    cot_all = out_cotangent.reshape(count * rows, features)
    cot_rel = relative_columns(cot_all)
    down_grad = weight_grad(cot_rel, join(act))
    up_grad = weight_grad(relative_columns(join(second)), join(g_hidden))
    out_grad = weight_grad(relative_columns(join(g_branch)), join(heads))

    tokens_grads = []
    for s in every:
        gq, gk, gv = g_queries[s], g_kv[s][0], g_kv[s][1]
        part = (dot(gq, wq, NT) + dot(gk, wk, NT) + dot(gv, wv, NT)).astype(LOW)
        add("q_b", gq.astype(F32))
        add("v_b", gv.astype(F32))
        add("ln1_g", part.astype(F32) * normed1[s])
        add("ln1_b", part.astype(F32))
        g_first = part.astype(F32) + other_head(part).astype(F32)
        tokens_grads.append(
            (g_middle[s] + norm_backward(g_first, normed1[s], inverse1[s], ln1_gain)).astype(LOW)
        )
    first_rel = relative_columns(join(first))
    g_proj = [join(g_queries), join([g[0] for g in g_kv]), join([g[1] for g in g_kv])]
    qkv_grad = jnp.stack([weight_grad(first_rel, g) for g in g_proj], axis=1)

    ln1 = jnp.stack([vec["ln1_g"], vec["ln1_b"]])
    ln1 = ln1 + other_head(ln1)
    wide = [ln1[0], ln1[1], vec["out_b"], vec["ln2_g"], vec["ln2_b"], vec["down_b"]]
    blocks = [v.reshape(n_seq, n_dp, -1) for v in wide + [vec["q_b"], vec["v_b"], vec["up_b"]]]
    sizes = [b.shape[2] for b in blocks]
    small = scatter_small(jnp.concatenate(blocks, axis=2))
    pieces, at = [], 0
    for size in sizes:
        pieces.append(small[at:at + size])
        at += size

    return (
        jnp.stack(outputs),
        jnp.stack(tokens_grads),
        pieces[0],
        pieces[1],
        qkv_grad,
        jnp.stack([pieces[6], pieces[7]]),
        out_grad.T,
        pieces[2],
        pieces[3],
        pieces[4],
        up_grad,
        pieces[8],
        down_grad.T,
        pieces[5],
    )


def solution(mesh):
    in_specs = (
        P("dp", "seq", None),
        P("dp", "seq"),
        P(),
        P(),
        P(None, None, "head"),
        P(None, "head"),
        P("head", None),
        P(),
        P(),
        P(),
        P(None, "head"),
        P("head"),
        P("head", None),
        P(),
        P("dp", "seq", None),
    )
    out_specs = (
        P("dp", "seq", None),
        P("dp", "seq", None),
        P(("seq", "dp")),
        P(("seq", "dp")),
        P(("seq", "dp"), None, "head"),
        P(None, ("head", "seq", "dp")),
        P("head", ("seq", "dp")),
        P(("seq", "dp")),
        P(("seq", "dp")),
        P(("seq", "dp")),
        P(("seq", "dp"), "head"),
        P(("head", "seq", "dp")),
        P("head", ("seq", "dp")),
        P(("seq", "dp")),
    )
    return jax.shard_map(shards, mesh=mesh, in_specs=in_specs, out_specs=out_specs, check_vma=False)
```

time: 782 us -> 430 us (0.55)
  waiting for transfers between devices: 512 us -> 141 us
  starting transfers between devices: 1.66 us -> 135 us
  blocking collectives: 68.2 us -> 0 us
  Pallas kernels: 0 us -> 35.6 us
  local copies, waits for them, and re-layouts: 45.7 us -> 12.3 us
  matrix products: 97.1 us -> 65.5 us
  between operations: 16.3 us -> 3.11 us
    reduce_scatter x6 -> x0, waiting for transfers between devices: 328 us -> none  [the longest x1 109 us: shards(): lax.psum_scatter(grad_down_weight, ('seq', 'dp'), scatter_dimension=1, ti...]
    psum x3 -> x0, waiting for transfers between devices: 143 us -> none  [the longest x1 63.8 us: shards(): lax.psum(jnp.dot(act_low, down_weight, preferred_element_type=jnp.float32...]
    ppermute x0 -> x84, waiting for transfers between devices: none -> 141 us  [the longest x48 108 us: swap(): lax.ppermute(value, axis, [(i, i ^ mask) for i in range(axis_size(axis))])]
    ppermute x0 -> x84, starting transfers between devices: none -> 135 us  [the longest x18 90.8 us: scatter_line(): lax.ppermute(send_up.astype(LOW), 'dp', [(i, i + 1) for i in range(n) if...]
    unnamed x1 -> x0, blocking collectives: 61.9 us -> none
    pallas_call x0 -> x4, Pallas kernels: none -> 35.6 us  [the longest x2 18.3 us: attend_back(): pl.pallas_call(functools.partial(attend_back_kernel, n), grid=(pairs,), i...]
    dot_general x18 -> x48, matrix products: 97.1 us -> 65.5 us  [dot(): return lax.dot_general(a, b, dims, preferred_element_type=F32)]
    unnamed x13 -> x0, waiting for transfers between devices: 22.4 us -> none
  transfers between devices with their start and end apart: 12 -> 84, of which waited for: 10 -> 29; matrix products, arithmetic and copies ran while one was open for 14% -> 23% of each run, Pallas kernels for 0% -> 8%
where the time goes in v1:
time: 430 us; the launch traced here: 423 us
  waiting for transfers between devices  141 us (33%)
  starting transfers between devices  135 us (31%)
  matrix products  65.5 us (15%)
  Pallas kernels  35.6 us (8%)
  other arithmetic  31.3 us (7%)
  local copies, waits for them, and re-layouts  12.3 us (3%)
    ppermute x48, waiting for transfers between devices, swap(): lax.ppermute(value, axis, [(i, i ^ mask) for i in range(axis_size(axis))])  108 us
    ppermute x18, starting transfers between devices, scatter_line(): lax.ppermute(send_up.astype(LOW), 'dp', [(i, i + 1) for i in range(n) if...  90.8 us
    dot_general x48, matrix products, dot(): return lax.dot_general(a, b, dims, preferred_element_type=F32)  65.5 us
    ppermute x48, starting transfers between devices, swap(): lax.ppermute(value, axis, [(i, i ^ mask) for i in range(axis_size(axis))])  27 us
    pallas_call x2, Pallas kernels, attend_back(): pl.pallas_call(functools.partial(attend_back_kernel, n), grid=(pairs,), i...  18.3 us
    pallas_call x2, Pallas kernels, attend(): pl.pallas_call(functools.partial(attend_kernel, n), grid=(pairs,), in_spe...  17.2 us
    ppermute x18, starting transfers between devices, scatter_line(): lax.ppermute(send_down.astype(LOW), 'dp', [(i, i - 1) for i in range(n) i...  16.8 us
    ppermute x18, waiting for transfers between devices, scatter_line(): lax.ppermute(send_up.astype(LOW), 'dp', [(i, i + 1) for i in range(n) if...  16.8 us
  transfers between devices with their start and end apart: 84, of which 29 were waited for; matrix products, arithmetic and copies ran while one was open for 23% of the time, Pallas kernels for 8%

profile of v1, /device:TPU:0, one launch (start us, length us, event | category | flops | bytes accessed | tf_op | source)
XLA Modules:
  0.0 423.1 jit_solution(3294305100092824006)
XLA Ops:
  24.8 9.9 %collective-permute-done.4.refs_2_ = bf16[2,256,512]{2,1,0:T(8,128)(2,1)} collective-permute-done((bf16[2,256,512]{2,1,0:T(8,128)(2,1)}, bf16[2,256,512]{2,1,0:T(8,128)(2,1)}, u32[]{:S(2)}, u32[]{:S(2)}) %collective-permute-start.4) | collective-permute-done | bytes 524320 | tf_op jit(solution)/shard_map/ppermute | solution.py:31
  37.9 8.4 %shard_map.255 = (bf16[8,4,256,256]{3,2,1,0:T(8,128)(2,1)}, f32[512,256]{1,0:T(8,128)}, bf16[256,512]{1,0:T(8,128)(2,1)}, f32[4,2,256]{2,1,0:T(2,128)}) custom-call(bf16[256,512]{1,0:T(8,128)(2,1)} %fusion.24.q_ref, s32[8,256]{1,0:T(8,128)} %broadcast_in_dim.16.seg_ref, s32[4,256,1]{2,1,0:T(8,128)} %copy.32.segk_ref, bf16[2,256,512]{2,1,0:T(8,128)(2,1)} %copy-done.27, ...), custom_call_target="tpu_custom_call" | custom-call | flops 2147483648 | bytes 4194304 | tf_op jit(solution)/shard_map/pallas_call | solution.py:99
  48.6 8.8 %shard_map.254 = (bf16[8,4,256,256]{3,2,1,0:T(8,128)(2,1)}, f32[512,256]{1,0:T(8,128)}, bf16[256,512]{1,0:T(8,128)(2,1)}, f32[4,2,256]{2,1,0:T(2,128)}) custom-call(bf16[256,512]{1,0:T(8,128)(2,1)} %fusion.22.q_ref, s32[8,256]{1,0:T(8,128)} %broadcast_in_dim.13.seg_ref, s32[4,256,1]{2,1,0:T(8,128)} %copy.31.segk_ref, ...), custom_call_target="tpu_custom_call" | custom-call | flops 2147483648 | bytes 4194304 | tf_op jit(solution)/shard_map/pallas_call | solution.py:99
  102.7 11.2 %collective-permute-done.14 = bf16[256,1024]{1,0:T(8,128)(2,1)S(1)} collective-permute-done((bf16[256,1024]{1,0:T(8,128)(2,1)S(1)}, bf16[256,1024]{1,0:T(8,128)(2,1)S(1)}, u32[]{:S(2)}, u32[]{:S(2)}) %collective-permute-start.14) | collective-permute-done | bytes 524320 | tf_op jit(solution)/shard_map/ppermute | solution.py:31
  113.9 9.0 %collective-permute-done.20 = bf16[256,1024]{1,0:T(8,128)(2,1)S(1)} collective-permute-done((bf16[256,1024]{1,0:T(8,128)(2,1)S(1)}, bf16[256,1024]{1,0:T(8,128)(2,1)S(1)}, u32[]{:S(2)}, u32[]{:S(2)}) %collective-permute-start.20) | collective-permute-done | bytes 524320 | tf_op jit(solution)/shard_map/ppermute | solution.py:31
  130.5 9.1 %shard_map.257 = (bf16[256,512]{1,0:T(8,128)(2,1)}, bf16[2,256,512]{2,1,0:T(8,128)(2,1)}, bf16[2,256,512]{2,1,0:T(8,128)(2,1)}, bf16[2,256,512]{2,1,0:T(8,128)(2,1)}, bf16[2,256,512]{2,1,0:T(8,128)(2,1)}) custom-call(bf16[256,512]{1,0:T(8,128)(2,1)} %fusion.24.q_ref, bf16[256,512]{1,0:T(8,128)(2,1)} %convolution_convert_fusion.16.g_ref, ...), custom_call_target="tpu_custom_call" | custom-call | flops 4294967296 | bytes 4194304 | tf_op jit(solution)/shard_map/pallas_call | solution.py:169
  139.6 9.3 %shard_map.256 = (bf16[256,512]{1,0:T(8,128)(2,1)}, bf16[2,256,512]{2,1,0:T(8,128)(2,1)}, bf16[2,256,512]{2,1,0:T(8,128)(2,1)}, bf16[2,256,512]{2,1,0:T(8,128)(2,1)}, bf16[2,256,512]{2,1,0:T(8,128)(2,1)}) custom-call(bf16[256,512]{1,0:T(8,128)(2,1)} %fusion.22.q_ref, bf16[256,512]{1,0:T(8,128)(2,1)} %convolution_convert_fusion.17.g_ref, ...), custom_call_target="tpu_custom_call" | custom-call | flops 4294967296 | bytes 4194304 | tf_op jit(solution)/shard_map/pallas_call | solution.py:169
  155.3 5.0 %collective-permute-done.59 = bf16[256,512]{1,0:T(8,128)(2,1)} collective-permute-done((bf16[256,512]{1,0:T(8,128)(2,1)}, bf16[256,512]{1,0:T(8,128)(2,1)}, u32[]{:S(2)}, u32[]{:S(2)}) %collective-permute-start.59) | collective-permute-done | bytes 262176 | tf_op jit(solution)/shard_map/ppermute | solution.py:31
  177.4 7.5 %collective-permute-start.62 = (bf16[64,512]{1,0:T(8,128)(2,1)S(1)}, bf16[64,512]{1,0:T(8,128)(2,1)S(1)}, u32[]{:S(2)}, u32[]{:S(2)}) collective-permute-start(bf16[64,512]{1,0:T(8,128)(2,1)S(1)} %get-tuple-element.117), channel_id=1, source_target_pairs={{0,1},{1,2},{2,3},{4,5},{5,6},{6,7},{8,9},{9,10},{10,11},{12,13},{... | collective-permute-start | bytes 196616 | tf_op jit(solution)/shard_map/ppermute | solution.py:221
  186.8 4.3 %collective-permute-done.65 = bf16[64,512]{1,0:T(8,128)(2,1)S(1)} collective-permute-done((bf16[64,512]{1,0:T(8,128)(2,1)S(1)}, bf16[64,512]{1,0:T(8,128)(2,1)S(1)}, u32[]{:S(2)}, u32[]{:S(2)}) %collective-permute-start.65) | collective-permute-done | bytes 65568 | tf_op jit(solution)/shard_map/ppermute | solution.py:224
  195.5 33.7 %collective-permute-done.23 = bf16[2,256,512]{2,1,0:T(8,128)(2,1)S(1)} collective-permute-done((bf16[2,256,512]{2,1,0:T(8,128)(2,1)S(1)}, bf16[2,256,512]{2,1,0:T(8,128)(2,1)S(1)}, u32[]{:S(2)}, u32[]{:S(2)}) %collective-permute-start.23) | collective-permute-done | bytes 524320 | tf_op jit(solution)/shard_map/ppermute | solution.py:31
  244.5 5.4 %collective-permute-done.24 = bf16[256,1024]{1,0:T(8,128)(2,1)S(1)} collective-permute-done((bf16[256,1024]{1,0:T(8,128)(2,1)S(1)}, bf16[256,1024]{1,0:T(8,128)(2,1)S(1)}, u32[]{:S(2)}, u32[]{:S(2)}) %collective-permute-start.24) | collective-permute-done | bytes 524320 | tf_op jit(solution)/shard_map/ppermute | solution.py:31
  251.5 8.0 %collective-permute-done.19 = bf16[256,1024]{1,0:T(8,128)(2,1)S(1)} collective-permute-done((bf16[256,1024]{1,0:T(8,128)(2,1)S(1)}, bf16[256,1024]{1,0:T(8,128)(2,1)S(1)}, u32[]{:S(2)}, u32[]{:S(2)}) %collective-permute-start.19) | collective-permute-done | bytes 524320 | tf_op jit(solution)/shard_map/ppermute | solution.py:31
  293.6 4.3 %collective-permute-start.79 = (bf16[64,2048]{1,0:T(8,128)(2,1)S(1)}, bf16[64,2048]{1,0:T(8,128)(2,1)S(1)}, u32[]{:S(2)}, u32[]{:S(2)}) collective-permute-start(bf16[64,2048]{1,0:T(8,128)(2,1)S(1)} %add_convert_fusion.13), channel_id=1, source_target_pairs={{0,1},{1,2},{4,5},{5,6},{8,9},{9,10},{12,13},{13,14},{16,17},{17,1... | collective-permute-start | bytes 786440 | tf_op jit(solution)/shard_map/ppermute | solution.py:221
  299.2 4.5 %collective-permute-done.79 = bf16[64,2048]{1,0:T(8,128)(2,1)S(1)} collective-permute-done((bf16[64,2048]{1,0:T(8,128)(2,1)S(1)}, bf16[64,2048]{1,0:T(8,128)(2,1)S(1)}, u32[]{:S(2)}, u32[]{:S(2)}) %collective-permute-start.79) | collective-permute-done | bytes 262176 | tf_op jit(solution)/shard_map/ppermute | solution.py:221
  303.7 5.8 %collective-permute-start.70 = (bf16[64,2048]{1,0:T(8,128)(2,1)S(1)}, bf16[64,2048]{1,0:T(8,128)(2,1)S(1)}, u32[]{:S(2)}, u32[]{:S(2)}) collective-permute-start(bf16[64,2048]{1,0:T(8,128)(2,1)S(1)} %add_convert_fusion.17), channel_id=1, source_target_pairs={{0,1},{1,2},{4,5},{5,6},{8,9},{9,10},{12,13},{13,14},{16,17},{17,1... | collective-permute-start | bytes 786440 | tf_op jit(solution)/shard_map/ppermute | solution.py:221
  316.7 8.8 %collective-permute-done.32 = bf16[256,512]{1,0:T(8,128)(2,1)S(1)} collective-permute-done((bf16[256,512]{1,0:T(8,128)(2,1)S(1)}, bf16[256,512]{1,0:T(8,128)(2,1)S(1)}, u32[]{:S(2)}, u32[]{:S(2)}) %collective-permute-start.32) | collective-permute-done | bytes 262176 | tf_op jit(solution)/shard_map/ppermute | solution.py:31
  325.5 4.4 %collective-permute-start.80 = (bf16[64,2048]{1,0:T(8,128)(2,1)S(1)}, bf16[64,2048]{1,0:T(8,128)(2,1)S(1)}, u32[]{:S(2)}, u32[]{:S(2)}) collective-permute-start(bf16[64,2048]{1,0:T(8,128)(2,1)S(1)} %get-tuple-element.82), channel_id=1, source_target_pairs={{0,1},{1,2},{2,3},{4,5},{5,6},{6,7},{8,9},{9,10},{10,11},{12,13},{... | collective-permute-start | bytes 786440 | tf_op jit(solution)/shard_map/ppermute | solution.py:221
  334.4 4.5 %collective-permute-start.33 = (bf16[64,512]{1,0:T(8,128)(2,1)S(1)}, bf16[64,512]{1,0:T(8,128)(2,1)S(1)}, u32[]{:S(2)}, u32[]{:S(2)}) collective-permute-start(bf16[64,512]{1,0:T(8,128)(2,1)S(1)} %get-tuple-element.123), channel_id=1, source_target_pairs={{0,1},{4,5},{8,9},{12,13},{16,17},{20,21},{24,25},{28,29}} | collective-permute-start | bytes 196616 | tf_op jit(solution)/shard_map/ppermute | solution.py:221
  340.8 4.3 %collective-permute-start.42 = (bf16[64,512]{1,0:T(8,128)(2,1)S(1)}, bf16[64,512]{1,0:T(8,128)(2,1)S(1)}, u32[]{:S(2)}, u32[]{:S(2)}) collective-permute-start(bf16[64,512]{1,0:T(8,128)(2,1)S(1)} %get-tuple-element.127), channel_id=1, source_target_pairs={{0,1},{4,5},{8,9},{12,13},{16,17},{20,21},{24,25},{28,29}} | collective-permute-start | bytes 196616 | tf_op jit(solution)/shard_map/ppermute | solution.py:221
  359.7 4.4 %collective-permute-start.43 = (bf16[64,512]{1,0:T(8,128)(2,1)S(1)}, bf16[64,512]{1,0:T(8,128)(2,1)S(1)}, u32[]{:S(2)}, u32[]{:S(2)}) collective-permute-start(bf16[64,512]{1,0:T(8,128)(2,1)S(1)} %add_convert_fusion.31), channel_id=1, source_target_pairs={{0,1},{1,2},{4,5},{5,6},{8,9},{9,10},{12,13},{13,14},{16,17},{17,1... | collective-permute-start | bytes 196616 | tf_op jit(solution)/shard_map/ppermute | solution.py:221
  374.2 21.1 %collective-permute-start.35 = (bf16[64,512]{1,0:T(8,128)(2,1)S(1)}, bf16[64,512]{1,0:T(8,128)(2,1)S(1)}, u32[]{:S(2)}, u32[]{:S(2)}) collective-permute-start(bf16[64,512]{1,0:T(8,128)(2,1)S(1)} %get-tuple-element.121), channel_id=1, source_target_pairs={{0,1},{1,2},{2,3},{4,5},{5,6},{6,7},{8,9},{9,10},{10,11},{12,13},{... | collective-permute-start | bytes 196616 | tf_op jit(solution)/shard_map/ppermute | solution.py:221
  399.1 4.5 %collective-permute-start.53 = (bf16[64,512]{1,0:T(8,128)(2,1)S(1)}, bf16[64,512]{1,0:T(8,128)(2,1)S(1)}, u32[]{:S(2)}, u32[]{:S(2)}) collective-permute-start(bf16[64,512]{1,0:T(8,128)(2,1)S(1)} %get-tuple-element.133), channel_id=1, source_target_pairs={{0,1},{1,2},{2,3},{4,5},{5,6},{6,7},{8,9},{9,10},{10,11},{12,13},{... | collective-permute-start | bytes 196616 | tf_op jit(solution)/shard_map/ppermute | solution.py:221
  414.1 4.8 %collective-permute-done.83 = bf16[64,2048]{1,0:T(8,128)(2,1)S(1)} collective-permute-done((bf16[64,2048]{1,0:T(8,128)(2,1)S(1)}, bf16[64,2048]{1,0:T(8,128)(2,1)S(1)}, u32[]{:S(2)}, u32[]{:S(2)}) %collective-permute-start.83) | collective-permute-done | bytes 262176 | tf_op jit(solution)/shard_map/ppermute | solution.py:224
  (462 shorter events, 218.8 us)
Async XLA Ops:
  9.5 27.8 %collective-permute-start.10 = (bf16[2,256,512]{2,1,0:T(8,128)(2,1)S(1)}, bf16[2,256,512]{2,1,0:T(8,128)(2,1)}, u32[]{:S(2)}, u32[]{:S(2)}) collective-permute-start(bf16[2,256,512]{2,1,0:T(8,128)(2,1)S(1)} %pad_maximum_fusion.5.refs_0_), channel_id=1, source_target_pairs={{0,8},{8,0},{16,24},{24,16},{1,9},{9,1},{17,25},{25,17},{2,10},{10... | collective-permute-start | bytes 1572872 | tf_op jit(solution)/shard_map/ppermute | solution.py:31
  24.3 23.7 %collective-permute-start.3 = (bf16[2,256,512]{2,1,0:T(8,128)(2,1)}, bf16[2,256,512]{2,1,0:T(8,128)(2,1)}, u32[]{:S(2)}, u32[]{:S(2)}) collective-permute-start(bf16[2,256,512]{2,1,0:T(8,128)(2,1)} %pad_maximum_fusion.4.refs_0_), channel_id=1, source_target_pairs={{0,8},{8,0},{16,24},{24,16},{1,9},{9,1},{17,25},{25,17},{2,10},{10... | collective-permute-start | bytes 1572872 | tf_op jit(solution)/shard_map/ppermute | solution.py:31
  77.1 25.6 %collective-permute-start.15 = (bf16[256,1024]{1,0:T(8,128)(2,1)S(1)}, bf16[256,1024]{1,0:T(8,128)(2,1)S(1)}, u32[]{:S(2)}, u32[]{:S(2)}) collective-permute-start(bf16[256,1024]{1,0:T(8,128)(2,1)S(1)} %convolution_convert_fusion.5), channel_id=1, source_target_pairs={{0,4},{4,0},{1,5},{5,1},{2,6},{6,2},{3,7},{7,3},{8,12},{12,8},{9,1... | collective-permute-start | bytes 1572872 | tf_op jit(solution)/shard_map/ppermute | solution.py:31
  85.4 28.5 %collective-permute-start.14 = (bf16[256,1024]{1,0:T(8,128)(2,1)S(1)}, bf16[256,1024]{1,0:T(8,128)(2,1)S(1)}, u32[]{:S(2)}, u32[]{:S(2)}) collective-permute-start(bf16[256,1024]{1,0:T(8,128)(2,1)S(1)} %convolution_convert_fusion.6), channel_id=1, source_target_pairs={{0,4},{4,0},{1,5},{5,1},{2,6},{6,2},{3,7},{7,3},{8,12},{12,8},{9,1... | collective-permute-start | bytes 1572872 | tf_op jit(solution)/shard_map/ppermute | solution.py:31
  86.0 37.0 %collective-permute-start.20 = (bf16[256,1024]{1,0:T(8,128)(2,1)S(1)}, bf16[256,1024]{1,0:T(8,128)(2,1)S(1)}, u32[]{:S(2)}, u32[]{:S(2)}) collective-permute-start(bf16[256,1024]{1,0:T(8,128)(2,1)S(1)} %convolution_convert_fusion.4), channel_id=1, source_target_pairs={{0,4},{4,0},{1,5},{5,1},{2,6},{6,2},{3,7},{7,3},{8,12},{12,8},{9,1... | collective-permute-start | bytes 1572872 | tf_op jit(solution)/shard_map/ppermute | solution.py:31
  92.7 76.4 %collective-permute-start.76 = (bf16[256,2048]{1,0:T(8,128)(2,1)}, bf16[256,2048]{1,0:T(8,128)(2,1)}, u32[]{:S(2)}, u32[]{:S(2)}) collective-permute-start(bf16[256,2048]{1,0:T(8,128)(2,1)} %convolution_convert_fusion), channel_id=1, source_target_pairs={{0,8},{8,0},{16,24},{24,16},{1,9},{9,1},{17,25},{25,17},{2,10},{10... | collective-permute-start | bytes 3145736 | tf_op jit(solution)/shard_map/ppermute | solution.py:31
  98.8 138.5 %collective-permute-start.75 = (bf16[256,2048]{1,0:T(8,128)(2,1)}, bf16[256,2048]{1,0:T(8,128)(2,1)}, u32[]{:S(2)}, u32[]{:S(2)}) collective-permute-start(bf16[256,2048]{1,0:T(8,128)(2,1)} %convolution_convert_fusion.1), channel_id=1, source_target_pairs={{0,8},{8,0},{16,24},{24,16},{1,9},{9,1},{17,25},{25,17},{2,10},{10... | collective-permute-start | bytes 3145736 | tf_op jit(solution)/shard_map/ppermute | solution.py:31
  102.7 59.0 %collective-permute-start.67 = (bf16[256,2048]{1,0:T(8,128)(2,1)}, bf16[256,2048]{1,0:T(8,128)(2,1)}, u32[]{:S(2)}, u32[]{:S(2)}) collective-permute-start(bf16[256,2048]{1,0:T(8,128)(2,1)} %convolution_convert_fusion.2), channel_id=1, source_target_pairs={{0,8},{8,0},{16,24},{24,16},{1,9},{9,1},{17,25},{25,17},{2,10},{10... | collective-permute-start | bytes 3145736 | tf_op jit(solution)/shard_map/ppermute | solution.py:31
  155.2 36.6 %collective-permute-start.16 = (bf16[2,256,512]{2,1,0:T(8,128)(2,1)S(1)}, bf16[2,256,512]{2,1,0:T(8,128)(2,1)S(1)}, u32[]{:S(2)}, u32[]{:S(2)}) collective-permute-start(bf16[2,256,512]{2,1,0:T(8,128)(2,1)S(1)} %copy-done.56), channel_id=1, source_target_pairs={{0,8},{8,0},{16,24},{24,16},{1,9},{9,1},{17,25},{25,17},{2,10},{10... | collective-permute-start | bytes 1572872 | tf_op jit(solution)/shard_map/ppermute | solution.py:31
  186.8 81.0 %collective-permute-start.66 = (bf16[256,2048]{1,0:T(8,128)(2,1)}, bf16[256,2048]{1,0:T(8,128)(2,1)}, u32[]{:S(2)}, u32[]{:S(2)}) collective-permute-start(bf16[256,2048]{1,0:T(8,128)(2,1)} %convolution_convert_fusion.3), channel_id=1, source_target_pairs={{0,8},{8,0},{16,24},{24,16},{1,9},{9,1},{17,25},{25,17},{2,10},{10... | collective-permute-start | bytes 3145736 | tf_op jit(solution)/shard_map/ppermute | solution.py:31
  191.8 47.0 %collective-permute-start.77 = (bf16[256,2048]{1,0:T(8,128)(2,1)}, bf16[256,2048]{1,0:T(8,128)(2,1)}, u32[]{:S(2)}, u32[]{:S(2)}) collective-permute-start(bf16[256,2048]{1,0:T(8,128)(2,1)} %add_convert_fusion), channel_id=1, source_target_pairs={{0,16},{8,24},{16,0},{24,8},{1,17},{9,25},{17,1},{25,9},{2,18},{10... | collective-permute-start | bytes 3145736 | tf_op jit(solution)/shard_map/ppermute | solution.py:31
  192.3 36.9 %collective-permute-start.23 = (bf16[2,256,512]{2,1,0:T(8,128)(2,1)S(1)}, bf16[2,256,512]{2,1,0:T(8,128)(2,1)S(1)}, u32[]{:S(2)}, u32[]{:S(2)}) collective-permute-start(bf16[2,256,512]{2,1,0:T(8,128)(2,1)S(1)} %add_convert_fusion.3), channel_id=1, source_target_pairs={{0,16},{8,24},{16,0},{24,8},{1,17},{9,25},{17,1},{25,9},{2,18},{10... | collective-permute-start | bytes 1572872 | tf_op jit(solution)/shard_map/ppermute | solution.py:31
  195.0 72.8 %collective-permute-start.68 = (bf16[256,2048]{1,0:T(8,128)(2,1)}, bf16[256,2048]{1,0:T(8,128)(2,1)}, u32[]{:S(2)}, u32[]{:S(2)}) collective-permute-start(bf16[256,2048]{1,0:T(8,128)(2,1)} %add_convert_fusion.1), channel_id=1, source_target_pairs={{0,16},{8,24},{16,0},{24,8},{1,17},{9,25},{17,1},{25,9},{2,18},{10... | collective-permute-start | bytes 3145736 | tf_op jit(solution)/shard_map/ppermute | solution.py:31
  241.9 48.4 %collective-permute-start.78 = (bf16[64,2048]{1,0:T(8,128)(2,1)}, bf16[64,2048]{1,0:T(8,128)(2,1)}, u32[]{:S(2)}, u32[]{:S(2)}) collective-permute-start(bf16[64,2048]{1,0:T(8,128)(2,1)} %get-tuple-element.84), channel_id=1, source_target_pairs={{0,1},{4,5},{8,9},{12,13},{16,17},{20,21},{24,25},{28,29}} | collective-permute-start | bytes 786440 | tf_op jit(solution)/shard_map/ppermute | solution.py:221
  249.9 48.8 %collective-permute-start.81 = (bf16[64,2048]{1,0:T(8,128)(2,1)}, bf16[64,2048]{1,0:T(8,128)(2,1)}, u32[]{:S(2)}, u32[]{:S(2)}) collective-permute-start(bf16[64,2048]{1,0:T(8,128)(2,1)} %get-tuple-element.85), channel_id=1, source_target_pairs={{3,2},{7,6},{11,10},{15,14},{19,18},{23,22},{27,26},{31,30}} | collective-permute-start | bytes 786440 | tf_op jit(solution)/shard_map/ppermute | solution.py:224
  282.3 28.2 %collective-permute-start.72 = (bf16[64,2048]{1,0:T(8,128)(2,1)S(1)}, bf16[64,2048]{1,0:T(8,128)(2,1)S(1)}, u32[]{:S(2)}, u32[]{:S(2)}) collective-permute-start(bf16[64,2048]{1,0:T(8,128)(2,1)S(1)} %get-tuple-element.89), channel_id=1, source_target_pairs={{3,2},{7,6},{11,10},{15,14},{19,18},{23,22},{27,26},{31,30}} | collective-permute-start | bytes 786440 | tf_op jit(solution)/shard_map/ppermute | solution.py:224
  298.3 32.0 %collective-permute-start.39 = (bf16[256,512]{1,0:T(8,128)(2,1)S(1)}, bf16[256,512]{1,0:T(8,128)(2,1)S(1)}, u32[]{:S(2)}, u32[]{:S(2)}) collective-permute-start(bf16[256,512]{1,0:T(8,128)(2,1)S(1)} %copy-done.60), channel_id=1, source_target_pairs={{0,8},{8,0},{16,24},{24,16},{1,9},{9,1},{17,25},{25,17},{2,10},{10... | collective-permute-start | bytes 786440 | tf_op jit(solution)/shard_map/ppermute | solution.py:31
  298.7 35.7 %collective-permute-start.48 = (bf16[256,512]{1,0:T(8,128)(2,1)S(1)}, bf16[256,512]{1,0:T(8,128)(2,1)S(1)}, u32[]{:S(2)}, u32[]{:S(2)}) collective-permute-start(bf16[256,512]{1,0:T(8,128)(2,1)S(1)} %copy-done.59), channel_id=1, source_target_pairs={{0,8},{8,0},{16,24},{24,16},{1,9},{9,1},{17,25},{25,17},{2,10},{10... | collective-permute-start | bytes 786440 | tf_op jit(solution)/shard_map/ppermute | solution.py:31
  310.6 28.4 %collective-permute-start.50 = (bf16[256,512]{1,0:T(8,128)(2,1)S(1)}, bf16[256,512]{1,0:T(8,128)(2,1)S(1)}, u32[]{:S(2)}, u32[]{:S(2)}) collective-permute-start(bf16[256,512]{1,0:T(8,128)(2,1)S(1)} %add_convert_fusion.18), channel_id=1, source_target_pairs={{0,16},{8,24},{16,0},{24,8},{1,17},{9,25},{17,1},{25,9},{2,18},{10... | collective-permute-start | bytes 786440 | tf_op jit(solution)/shard_map/ppermute | solution.py:31
  325.5 88.6 %collective-permute-start.80 = (bf16[64,2048]{1,0:T(8,128)(2,1)S(1)}, bf16[64,2048]{1,0:T(8,128)(2,1)S(1)}, u32[]{:S(2)}, u32[]{:S(2)}) collective-permute-start(bf16[64,2048]{1,0:T(8,128)(2,1)S(1)} %get-tuple-element.82), channel_id=1, source_target_pairs={{0,1},{1,2},{2,3},{4,5},{5,6},{6,7},{8,9},{9,10},{10,11},{12,13},{... | collective-permute-start | bytes 786440 | tf_op jit(solution)/shard_map/ppermute | solution.py:221
  330.2 65.2 %collective-permute-start.82 = (bf16[64,2048]{1,0:T(8,128)(2,1)S(1)}, bf16[64,2048]{1,0:T(8,128)(2,1)S(1)}, u32[]{:S(2)}, u32[]{:S(2)}) collective-permute-start(bf16[64,2048]{1,0:T(8,128)(2,1)S(1)} %get-tuple-element.83), channel_id=1, source_target_pairs={{2,1},{3,2},{6,5},{7,6},{10,9},{11,10},{14,13},{15,14},{18,17},{19... | collective-permute-start | bytes 786440 | tf_op jit(solution)/shard_map/ppermute | solution.py:224
  330.9 88.9 %collective-permute-start.71 = (bf16[64,2048]{1,0:T(8,128)(2,1)S(1)}, bf16[64,2048]{1,0:T(8,128)(2,1)S(1)}, u32[]{:S(2)}, u32[]{:S(2)}) collective-permute-start(bf16[64,2048]{1,0:T(8,128)(2,1)S(1)} %get-tuple-element.86), channel_id=1, source_target_pairs={{0,1},{1,2},{2,3},{4,5},{5,6},{6,7},{8,9},{9,10},{10,11},{12,13},{... | collective-permute-start | bytes 786440 | tf_op jit(solution)/shard_map/ppermute | solution.py:221
  370.3 27.4 %collective-permute-start.73 = (bf16[64,2048]{1,0:T(8,128)(2,1)S(1)}, bf16[64,2048]{1,0:T(8,128)(2,1)S(1)}, u32[]{:S(2)}, u32[]{:S(2)}) collective-permute-start(bf16[64,2048]{1,0:T(8,128)(2,1)S(1)} %get-tuple-element.87), channel_id=1, source_target_pairs={{2,1},{3,2},{6,5},{7,6},{10,9},{11,10},{14,13},{15,14},{18,17},{19... | collective-permute-start | bytes 786440 | tf_op jit(solution)/shard_map/ppermute | solution.py:224
  374.2 24.8 %collective-permute-start.35 = (bf16[64,512]{1,0:T(8,128)(2,1)S(1)}, bf16[64,512]{1,0:T(8,128)(2,1)S(1)}, u32[]{:S(2)}, u32[]{:S(2)}) collective-permute-start(bf16[64,512]{1,0:T(8,128)(2,1)S(1)} %get-tuple-element.121), channel_id=1, source_target_pairs={{0,1},{1,2},{2,3},{4,5},{5,6},{6,7},{8,9},{9,10},{10,11},{12,13},{... | collective-permute-start | bytes 196616 | tf_op jit(solution)/shard_map/ppermute | solution.py:221
  (131 other events, 1462.1 us)

commit v2 on v1

--- a/solution.py
+++ b/solution.py
@@ -272,7 +272,740 @@
     )
 
 
-def shards(
+MESH = pl.DeviceIdType.MESH
+CHUNK = 32
+WIDE = 512
+
+
+def loop(count, body):
+    def step(i, carry):
+        body(i)
+        return carry
+
+    lax.fori_loop(0, count, step, 0)
+
+
+def span(i, size):
+    return pl.ds(pl.multiple_of(i * size, size), size)
+
+
+def fold(value):
+    return jnp.sum(value.reshape(value.shape[0] // 8, 8, value.shape[1]), axis=0)
+
+
+class Copies:
+    def __init__(self, send, recv):
+        self.send, self.recv, self.all, self.n = send, recv, [], 0
+
+    def start(self, src, dst, device):
+        copy = pltpu.make_async_remote_copy(
+            src_ref=src,
+            dst_ref=dst,
+            send_sem=self.send.at[self.n],
+            recv_sem=self.recv.at[self.n],
+            device_id=device,
+            device_id_type=MESH,
+        )
+        copy.start()
+        self.n += 1
+        self.all.append(copy)
+        return copy
+
+
+N_COPIES = 96
+N_LOCAL = 24
+
+
+def layer_kernel(n_dp, *refs):
+    (
+        tok_h, seg_in, g1, b1, wqkv_h, qvb, outw_h, outb, g2, b2, up_h, upb, down_h, downb, cot_h,
+        out_h, tg_h, downg_h, upg_h, outg_h, qkvg_h, vec_o,
+        tok, cot, wqkv, outw, up, down, q, kv, attn_t, attn, mid, lnb, act, gh,
+        first_t, second_t, cot_t, gb_t, g_attn, t2, gs, ffn, stat, st,
+        gs_r, ffn_r, gf_r, dkv_r, act_r, gh_r, first_r, second_r, cot_r, gb_r, heads_r, dqkv_r, xr, zr,
+        segs, segk, vec, qvacc, upacc, ln1_r, vs, vr,
+        send, recv, local,
+    ) = refs
+    rows = tok.shape[0] // 2
+    width = tok.shape[1]
+    heads_w = q.shape[1]
+    hidden = act.shape[1]
+    pairs = heads_w // LANES
+    quarter = width // 4
+    block = quarter // n_dp
+    s = lax.axis_index("seq")
+    h = lax.axis_index("head")
+    z = lax.axis_index("dp")
+    x, core = s // 2, s % 2
+    seq_peer = [None] + [((x ^ (m >> 1)) * 2 + (core ^ (m & 1)), h, z) for m in (1, 2, 3)]
+    across = (s, 1 - h, z)
+    along = [None] + [(s, h, lax.rem(z + n_dp - d, n_dp)) for d in range(1, n_dp)]
+    copies = Copies(send, recv)
+    loads = []
+
+    def load(src, dst):
+        copy = pltpu.make_async_copy(src, dst, local.at[len(loads)])
+        copy.start()
+        loads.append(copy)
+        return copy
+
+    get_tok = load(tok_h, tok)
+    get_qkv = load(wqkv_h, wqkv)
+    own_out = pl.ds(pl.multiple_of(h * heads_w, heads_w), heads_w)
+    get_out = load(outw_h, outw.at[own_out, :])
+    get_cot = load(cot_h, cot)
+    get_up = load(up_h, up)
+    get_down = load(down_h, down)
+
+    barrier = pltpu.get_barrier_semaphore()
+    partners = seq_peer[1:] + [across] + along[1:]
+    for device in partners:
+        pl.semaphore_signal(barrier, inc=1, device_id=device, device_id_type=MESH)
+
+    vec[...] = jnp.zeros_like(vec)
+    qvacc[...] = jnp.zeros_like(qvacc)
+    upacc[...] = jnp.zeros_like(upacc)
+    segs[0] = seg_in[...]
+    pl.semaphore_wait(barrier, len(partners))
+
+    seg_got = [None] + [copies.start(segs.at[0], segs.at[m], seq_peer[m]) for m in (1, 2, 3)]
+
+    def seq_rows(i):
+        return slice(i * rows, (i + 1) * rows)
+
+    def flip(src, i, dst):
+        def part(c):
+            dst[span(c, 256), seq_rows(i)] = src[:, span(c, 256)].T
+
+        loop(width // 256, part)
+
+    def swap_rows(flipped, target):
+        return [
+            copies.start(
+                flipped.at[pl.ds(pl.multiple_of(c * 2 * quarter + (1 - core) * quarter, quarter), quarter), :],
+                target.at[c],
+                seq_peer[1],
+            )
+            for c in range(2)
+        ]
+
+    kv_got = [[None] * 4, [None] * 4]
+
+    def project(i):
+        def norm(c):
+            at = pl.ds(pl.multiple_of(i * rows + c * CHUNK, CHUNK), CHUNK)
+            v = tok[at, :].astype(F32)
+            center = jnp.mean(v, axis=-1, keepdims=True)
+            v = v - center
+            inverse = lax.rsqrt(jnp.mean(v * v, axis=-1, keepdims=True) + EPSILON)
+            stat[0, at, 0:1] = center
+            stat[0, at, 1:2] = inverse
+            lnb[i, span(c, CHUNK), :] = (v * inverse * g1[...] + b1[...]).astype(LOW)
+
+        loop(rows // CHUNK, norm)
+        low = lnb.at[i]
+
+        def tile_kv(j):
+            at = span(j, 256)
+            kv[i, 0, :, at] = dot(low[...], wqkv[1, :, at]).astype(LOW)
+            up_at = pl.ds(pl.multiple_of(heads_w + j * 256, 256), 256)
+            kv[i, 0, :, up_at] = (dot(low[...], wqkv[2, :, at]) + qvb[1:2, at]).astype(LOW)
+
+        if i == 0:
+            get_qkv.wait()
+        loop(heads_w // 256, tile_kv)
+        kv_got[i][2] = copies.start(kv.at[i, 0], kv.at[i, 2], seq_peer[2])
+        kv_got[i][1] = copies.start(kv.at[i, 0], kv.at[i, 1], seq_peer[1])
+
+        def tile_q(j):
+            at = span(j, 256)
+            q[seq_rows(i), at] = (dot(low[...], wqkv[0, :, at]) + qvb[0:1, at]).astype(LOW)
+
+        loop(heads_w // 256, tile_q)
+        flip(low, i, first_t)
+
+    def attend_blocks(i, blocks, begin, end):
+        seg_q = segs[0, i:i + 1, :].astype(F32)
+
+        def pair(p):
+            lanes = span(p, LANES)
+            v_lanes = pl.ds(pl.multiple_of(heads_w + p * LANES, LANES), LANES)
+            qp = q[seq_rows(i), lanes] * jnp.asarray(0.125, LOW)
+            vts = [kv[i, m, :, v_lanes].T for m in blocks]
+            for head in range(2):
+                at = pl.ds(pl.multiple_of(p * LANES + head * HEAD_DIM, HEAD_DIM), HEAD_DIM)
+                qh = jnp.where(half_lanes(qp.shape, head), qp, jnp.zeros_like(qp))
+                parts = []
+                top = None if begin else st[i, p, head:head + 1, :]
+                old = top
+                for m in blocks:
+                    score = dot(kv[i, m, :, lanes], qh, NT)
+                    score = jnp.where(segk[m, :, i:i + 1] == seg_q, score, MASKED)
+                    peak = jnp.max(score, axis=0, keepdims=True)
+                    top = peak if top is None else jnp.maximum(top, peak)
+                    parts.append(score)
+                total = mixed = 0.0
+                for part, vt in zip(parts, vts):
+                    w = jnp.exp(part - top)
+                    total = total + jnp.sum(w, axis=0, keepdims=True)
+                    mixed = mixed + dot(vt[head * HEAD_DIM:(head + 1) * HEAD_DIM, :], w.astype(LOW))
+                if not begin:
+                    scale = jnp.exp(old - top)
+                    total = total + scale * st[i, p, 2 + head:3 + head, :]
+                    mixed = mixed + scale * attn_t[i, at, :]
+                if end:
+                    mixed = mixed / total
+                    st[i, p, 4 + head:5 + head, :] = top + jnp.log(total)
+                else:
+                    st[i, p, head:head + 1, :] = top
+                    st[i, p, 2 + head:3 + head, :] = total
+                attn_t[i, at, :] = mixed
+            if end:
+                to = pl.ds(pl.multiple_of(h * heads_w + p * LANES, LANES), LANES)
+                attn[seq_rows(i), to] = attn_t[i, lanes, :].T.astype(LOW)
+
+        loop(pairs, pair)
+
+    def seg_columns(m):
+        segk[m] = segs[m].astype(F32).T
+
+    own_heads = pl.ds(pl.multiple_of(h * heads_w, heads_w), heads_w)
+    attn_got = [None, None]
+
+    def attend_far(i):
+        kv_got[i][2].wait_recv()
+        kv_got[i][3] = copies.start(kv.at[i, 2], kv.at[i, 3], seq_peer[1])
+        attend_blocks(i, (2,), False, False)
+        kv_got[i][3].wait_recv()
+        attend_blocks(i, (3,), False, True)
+        mine = attn.at[seq_rows(i), own_heads]
+        attn_got[i] = copies.start(mine, mine, across)
+        heads_sent[i] = copies.start(mine, heads_r.at[seq_rows(i), :], seq_peer[1])
+
+    heads_sent = [None, None]
+
+    def middle(i):
+        attn_got[i].wait_recv()
+
+        def tile(j):
+            at = span(j, 256)
+            mid[seq_rows(i), at] = (
+                dot(attn[seq_rows(i), :], outw[:, at])
+                + tok[seq_rows(i), at].astype(F32)
+                + outb[:, at]
+            )
+
+        loop(width // 256, tile)
+
+        def norm(c):
+            at = pl.ds(pl.multiple_of(i * rows + c * CHUNK, CHUNK), CHUNK)
+            v = mid[at, :]
+            center = jnp.mean(v, axis=-1, keepdims=True)
+            v = v - center
+            inverse = lax.rsqrt(jnp.mean(v * v, axis=-1, keepdims=True) + EPSILON)
+            stat[1, at, 0:1] = center
+            stat[1, at, 1:2] = inverse
+            lnb[i, span(c, CHUNK), :] = (v * inverse * g2[...] + b2[...]).astype(LOW)
+
+        loop(rows // CHUNK, norm)
+
+    gs_got, ffn_got, act_got, gh_got = [None] * 2, [None] * 2, [None] * 2, [None] * 2
+
+    def feed(i):
+        at_rows = seq_rows(i)
+
+        def tile(j):
+            at = span(j, 256)
+            value, slope = gelu_pair(dot(lnb[i], up[:, at]) + upb[:, at])
+            act[at_rows, at] = value.astype(LOW)
+            g = (dot(cot[at_rows, :], down[at, :], NT) * slope).astype(LOW)
+            gh[at_rows, at] = g
+            upacc[:, at] += fold(g.astype(F32))
+
+        loop(hidden // 256, tile)
+
+        def back(j):
+            gs[at_rows, span(j, 256)] = dot(gh[at_rows, :], up[span(j, 256), :], NT).astype(LOW)
+
+        loop(width // 256, back)
+        gs_got[i] = copies.start(gs.at[at_rows, :], gs_r.at[at_rows, :], across)
+        act_got[i] = copies.start(act.at[at_rows, :], act_r.at[at_rows, :], seq_peer[1])
+        gh_got[i] = copies.start(gh.at[at_rows, :], gh_r.at[at_rows, :], seq_peer[1])
+        flip(lnb.at[i], i, second_t)
+
+    def feed_out(i):
+        at_rows = seq_rows(i)
+
+        def tile(j):
+            ffn[at_rows, span(j, 256)] = dot(act[at_rows, :], down[:, span(j, 256)]).astype(LOW)
+
+        loop(width // 256, tile)
+        ffn_got[i] = copies.start(ffn.at[at_rows, :], ffn_r.at[at_rows, :], across)
+
+    def finish_output(i):
+        ffn_got[i].wait()
+
+        def part(c):
+            at = pl.ds(pl.multiple_of(i * rows + c * CHUNK, CHUNK), CHUNK)
+            both = ffn[at, :].astype(F32) + ffn_r[at, :].astype(F32)
+            ffn[at, :] = (mid[at, :] + both + downb[...]).astype(LOW)
+
+        loop(rows // CHUNK, part)
+        load(ffn.at[seq_rows(i), :], out_h.at[seq_rows(i), :])
+
+    gb = down.at[2 * rows:4 * rows, :]
+    parts_kv = [down.at[(4 + m) * rows:(5 + m) * rows, :] for m in range(4)]
+    dqkv = up.at[2 * rows:4 * rows, :]
+
+    def norm2_back(i):
+        gs_got[i].wait_recv()
+
+        def part(c):
+            at = pl.ds(pl.multiple_of(i * rows + c * CHUNK, CHUNK), CHUNK)
+            g = gs[at, :].astype(F32) + gs_r[at, :].astype(F32)
+            inverse = stat[1, at, 1:2]
+            normed = (mid[at, :] - stat[1, at, 0:1]) * inverse
+            vec[3] += fold(g * normed)
+            vec[4] += fold(g)
+            e = g * g2[...]
+            e = e - jnp.mean(e, axis=-1, keepdims=True) - normed * jnp.mean(e * normed, axis=-1, keepdims=True)
+            low = (cot[at, :].astype(F32) + inverse * e).astype(LOW)
+            gb[at, :] = low
+            vec[2] += fold(low.astype(F32))
+
+        loop(rows // CHUNK, part)
+
+        def tile(j):
+            w_rows = pl.ds(pl.multiple_of(h * heads_w + j * 256, 256), 256)
+            g_attn[i, :, span(j, 256)] = dot(gb[seq_rows(i), :], outw[w_rows, :], NT).astype(LOW)
+
+        loop(heads_w // 256, tile)
+
+    def attend_back_pairs(i, start, stop):
+        seg_q = segs[0, i:i + 1, :].astype(F32)
+
+        def pair(p):
+            lanes = span(p, LANES)
+            v_lanes = pl.ds(pl.multiple_of(heads_w + p * LANES, LANES), LANES)
+            qp = q[seq_rows(i), lanes]
+            g = g_attn[i, :, lanes]
+            gt = g.astype(F32).T
+            qs, qscaled, gs_, gts, deltas, lses = [], [], [], [], [], []
+            for head in range(2):
+                at = pl.ds(pl.multiple_of(p * LANES + head * HEAD_DIM, HEAD_DIM), HEAD_DIM)
+                mask = half_lanes(qp.shape, head)
+                part = gt[head * HEAD_DIM:(head + 1) * HEAD_DIM, :]
+                deltas.append(jnp.sum(part * attn_t[i, at, :], axis=0, keepdims=True))
+                zeros = jnp.zeros_like(part)
+                full = jnp.concatenate([part, zeros] if head == 0 else [zeros, part], axis=0)
+                gts.append(full.astype(LOW))
+                gs_.append(jnp.where(mask, g, jnp.zeros_like(g)))
+                qs.append(jnp.where(mask, qp, jnp.zeros_like(qp)))
+                qscaled.append(qs[-1] * jnp.asarray(0.125, LOW))
+                lses.append(st[i, p, 4 + head:5 + head, :])
+            dqt = [0.0, 0.0]
+            for m in range(4):
+                k = kv[i, m, :, lanes]
+                kt = k.T
+                v = kv[i, m, :, v_lanes]
+                allowed = segk[m, :, i:i + 1] == seg_q
+                dk = dv = 0.0
+                for head in range(2):
+                    score = dot(k, qscaled[head], NT)
+                    probs = jnp.exp(jnp.where(allowed, score - lses[head], MASKED))
+                    ds = (probs * (dot(v, gts[head]) - deltas[head])).astype(LOW)
+                    dk = dk + dot(ds, qs[head])
+                    dv = dv + dot(probs.astype(LOW), gs_[head])
+                    dqt[head] = dqt[head] + dot(kt[head * HEAD_DIM:(head + 1) * HEAD_DIM, :], ds)
+                parts_kv[m][:, lanes] = (dk * 0.125).astype(LOW)
+                parts_kv[m][:, v_lanes] = dv.astype(LOW)
+            dq = (jnp.concatenate(dqt, axis=0).T * 0.125).astype(LOW)
+            dqkv[seq_rows(i), lanes] = dq
+            qvacc[:, lanes] += fold(dq.astype(F32))
+
+        lax.fori_loop(start, stop, lambda p, c: (pair(p), c)[1], 0)
+
+    near_got, far_got, dq_got = [None] * 2, [None] * 2, [None] * 2
+    kv_cols = pl.ds(heads_w, 2 * heads_w)
+
+    def keys_near(i):
+        near_got[i] = [
+            copies.start(parts_kv[3], dkv_r.at[i, 2], seq_peer[1]),
+            copies.start(parts_kv[1], dkv_r.at[i, 0], seq_peer[1]),
+        ]
+        at = (seq_rows(i), pl.ds(0, heads_w))
+        dq_got[i] = copies.start(dqkv.at[at], dqkv_r.at[at], seq_peer[1])
+
+    def keys_far(i):
+        near_got[i][0].wait_recv()
+
+        def part(c):
+            at = span(c, 64)
+            t2[i, at, :] = (parts_kv[2][at, :].astype(F32) + dkv_r[i, 2, at, :].astype(F32)).astype(LOW)
+
+        loop(rows // 64, part)
+        far_got[i] = copies.start(t2.at[i], dkv_r.at[i, 1], seq_peer[2])
+        near_got[i][1].wait_recv()
+
+        def rest(c):
+            at = span(c, 64)
+            to = pl.ds(pl.multiple_of(i * rows + c * 64, 64), 64)
+            dqkv[to, kv_cols] = (parts_kv[0][at, :].astype(F32) + dkv_r[i, 0, at, :].astype(F32)).astype(LOW)
+
+        loop(rows // 64, rest)
+
+    dkv_got, gf_got = [None] * 2, [None] * 2
+
+    def keys_done(i):
+        far_got[i].wait_recv()
+
+        def part(c):
+            at = span(c, 64)
+            to = pl.ds(pl.multiple_of(i * rows + c * 64, 64), 64)
+            low = (dqkv[to, kv_cols].astype(F32) + dkv_r[i, 1, at, :].astype(F32)).astype(LOW)
+            dqkv[to, kv_cols] = low
+            qvacc[:, pl.ds(heads_w, heads_w)] += fold(low[:, heads_w:].astype(F32))
+
+        loop(rows // 64, part)
+        at = (seq_rows(i), kv_cols)
+        dkv_got[i] = copies.start(dqkv.at[at], dqkv_r.at[at], seq_peer[1])
+
+    def first_back(i):
+        gs_got[i].wait_send()
+
+        def tile(j):
+            at = span(j, 256)
+            total = 0.0
+            for c in range(3):
+                total = total + dot(dqkv[seq_rows(i), c * heads_w:(c + 1) * heads_w], wqkv[c, at, :], NT)
+            gs[seq_rows(i), at] = total.astype(LOW)
+
+        loop(width // 256, tile)
+        gf_got[i] = copies.start(gs.at[seq_rows(i), :], gf_r.at[seq_rows(i), :], across)
+
+        def sums(c):
+            at = pl.ds(pl.multiple_of(i * rows + c * CHUNK, CHUNK), CHUNK)
+            g = gs[at, :].astype(F32)
+            normed = (tok[at, :].astype(F32) - stat[0, at, 0:1]) * stat[0, at, 1:2]
+            vec[0] += fold(g * normed)
+            vec[1] += fold(g)
+
+        loop(rows // CHUNK, sums)
+
+    def norm1_back(i):
+        gf_got[i].wait()
+
+        def part(c):
+            at = pl.ds(pl.multiple_of(i * rows + c * CHUNK, CHUNK), CHUNK)
+            g = gs[at, :].astype(F32) + gf_r[at, :].astype(F32)
+            inverse = stat[0, at, 1:2]
+            normed = (tok[at, :].astype(F32) - stat[0, at, 0:1]) * inverse
+            e = g * g1[...]
+            e = e - jnp.mean(e, axis=-1, keepdims=True) - normed * jnp.mean(e * normed, axis=-1, keepdims=True)
+            gs[at, :] = (gb[at, :].astype(F32) + inverse * e).astype(LOW)
+
+        loop(rows // CHUNK, part)
+        load(gs.at[seq_rows(i), :], tg_h.at[seq_rows(i), :])
+
+    def piece_tiles(piece, chip, body):
+        left, left_r, right, right_r, cols = piece
+        at_rows = pl.ds(pl.multiple_of(chip * 2 * quarter + core * quarter, quarter), quarter)
+
+        def tile(j):
+            at = span(j, WIDE)
+            body(j, dot(left[at_rows, :], right[:, at]) + dot(left_r[chip], right_r[:, at]))
+
+        loop(cols // WIDE, tile)
+
+    class Group:
+        def __init__(self, pieces, hold, offset, arrivals):
+            self.pieces, self.hold, self.arrivals = pieces, hold, arrivals
+            self.cols = sum(p[4] for p in pieces)
+            self.xr = xr.at[:, pl.ds(offset, self.cols)]
+            self.zr = [zr.at[d, :, pl.ds(offset, self.cols)] for d in range(n_dp - 1)]
+
+        def tiles(self, chip, body):
+            base = 0
+            for piece in self.pieces:
+                piece_tiles(
+                    piece,
+                    chip,
+                    lambda j, value, base=base: body(
+                        pl.ds(pl.multiple_of(base + j * WIDE, WIDE), WIDE), value
+                    ),
+                )
+                base += piece[4]
+
+        def first(self):
+            for copy in self.arrivals():
+                copy.wait_recv()
+
+            def keep(at, value):
+                self.hold[:, at] = value.astype(LOW)
+
+            self.tiles(1 - x, keep)
+            self.far = copies.start(self.hold, self.xr, seq_peer[2])
+
+        def second(self):
+            self.far.wait()
+
+            def keep(at, value):
+                self.hold[:, at] = (value + self.xr[:, at].astype(F32)).astype(LOW)
+
+            self.tiles(x, keep)
+            self.got = []
+            for d in range(1, n_dp):
+                to = lax.rem(z + n_dp - d, n_dp)
+                mine = pl.ds(pl.multiple_of(to * block, block), block)
+                self.got.append(copies.start(self.hold.at[mine, :], self.zr[d - 1], along[d]))
+
+        def third(self, stage, row, targets):
+            for copy in self.got:
+                copy.wait_recv()
+            mine = pl.ds(pl.multiple_of(z * block, block), block)
+            at_col = 0
+            for target, size in targets:
+                at = pl.ds(at_col, size)
+                total = self.hold[mine, at].astype(F32)
+                for d in range(n_dp - 1):
+                    total = total + self.zr[d][:, at].astype(F32)
+                place = stage.at[row:row + block, 0:size]
+                stage[row:row + block, 0:size] = total
+                load(place, target)
+                at_col += size
+                row += block
+            return row
+
+    attn_own = attn.at[:, own_heads]
+    q_cols, k_cols, v_cols = (slice(c * heads_w, (c + 1) * heads_w) for c in range(3))
+    flips = {}
+    group_a = Group(
+        [(cot_t, cot_r, act, act_r, hidden)], up.at[0:rows, :], 0, lambda: flips["cot"] + act_got
+    )
+    group_b = Group(
+        [(second_t, second_r, gh, gh_r, hidden)], up.at[rows:2 * rows, :], hidden, lambda: flips["second"] + gh_got
+    )
+    group_c = Group(
+        [
+            (gb_t, gb_r, attn_own, heads_r, heads_w),
+            (first_t, first_r, dqkv.at[:, q_cols], dqkv_r.at[:, q_cols], heads_w),
+        ],
+        down.at[0:rows, :],
+        2 * hidden,
+        lambda: flips["gb"] + flips["first"] + heads_sent + dq_got,
+    )
+    group_d = Group(
+        [(first_t, first_r, dqkv.at[:, c], dqkv_r.at[:, c], heads_w) for c in (k_cols, v_cols)],
+        down.at[rows:2 * rows, :],
+        2 * hidden + 2 * heads_w,
+        lambda: dkv_got,
+    )
+
+    get_tok.wait()
+    project(0)
+    project(1)
+    flips["first"] = swap_rows(first_t, first_r)
+    get_out.wait()
+    core_rows = pl.ds(pl.multiple_of(h * heads_w + core * (heads_w // 2), heads_w // 2), heads_w // 2)
+    out_got = copies.start(outw.at[core_rows, :], outw.at[core_rows, :], across)
+    for m in (1, 2, 3):
+        seg_got[m].wait_recv()
+    for m in range(4):
+        seg_columns(m)
+    for i in range(2):
+        kv_got[i][1].wait_recv()
+        attend_blocks(i, (0, 1), True, False)
+    get_cot.wait()
+
+    def sum_cot(c):
+        vec[5] += fold(cot[span(c, CHUNK), :].astype(F32))
+
+    loop(2 * rows // CHUNK, sum_cot)
+    for i in range(2):
+        flip(cot.at[seq_rows(i), :], i, cot_t)
+    flips["cot"] = swap_rows(cot_t, cot_r)
+    attend_far(0)
+    attend_far(1)
+    out_got.wait_recv()
+    got_rows = pl.ds(
+        pl.multiple_of((1 - h) * heads_w + core * (heads_w // 2), heads_w // 2), heads_w // 2
+    )
+    out_near = copies.start(outw.at[got_rows, :], outw.at[got_rows, :], seq_peer[1])
+    out_near.wait_recv()
+    get_up.wait()
+    get_down.wait()
+    for i in range(2):
+        middle(i)
+        feed(i)
+    flips["second"] = swap_rows(second_t, second_r)
+    feed_out(0)
+    feed_out(1)
+    group_a.first()
+    norm2_back(0)
+    attend_back_pairs(0, 0, pairs)
+    keys_near(0)
+    group_a.second()
+    keys_far(0)
+    group_b.first()
+    norm2_back(1)
+    for i in range(2):
+        flip(gb.at[seq_rows(i), :], i, gb_t)
+    flips["gb"] = swap_rows(gb_t, gb_r)
+    near_got[0][0].wait_send()
+    near_got[0][1].wait_send()
+    attend_back_pairs(1, 0, pairs)
+    keys_near(1)
+    keys_done(0)
+    keys_far(1)
+    group_c.first()
+    first_back(0)
+    group_b.second()
+    finish_output(0)
+    finish_output(1)
+    keys_done(1)
+    first_back(1)
+    ln1_got = copies.start(vec.at[0:2], ln1_r, across)
+    group_d.first()
+    group_c.second()
+    norm1_back(0)
+    group_d.second()
+    norm1_back(1)
+
+    ln1_got.wait()
+    lines = [jnp.sum(vec[k] + ln1_r[k], axis=0, keepdims=True) for k in range(2)]
+    lines += [jnp.sum(vec[k], axis=0, keepdims=True) for k in range(2, 6)]
+    lines += [jnp.sum(qvacc[...], axis=0, keepdims=True)]
+    ups = jnp.sum(upacc[...], axis=0, keepdims=True)
+    lines += [ups[:, c * width:(c + 1) * width] for c in range(hidden // width)]
+    lines += [jnp.zeros((16 - len(lines), width), F32)]
+    vs[0] = jnp.concatenate(lines, axis=0)
+    copies.start(vs.at[0], vr.at[0], seq_peer[1]).wait_recv()
+    vs[1] = vs[0] + vr[0]
+    copies.start(vs.at[1], vr.at[1], seq_peer[2]).wait_recv()
+    vs[2] = vs[1] + vr[1]
+    got = [copies.start(vs.at[2], vr.at[1 + d], along[d]) for d in range(1, n_dp)]
+    row = group_a.third(mid, 0, [(downg_h.at[:, pl.ds(c * width, width)], width) for c in range(hidden // width)])
+    row = group_b.third(mid, row, [(upg_h.at[:, pl.ds(c * width, width)], width) for c in range(hidden // width)])
+    row = group_c.third(mid, row, [(outg_h, heads_w), (qkvg_h.at[0], heads_w)])
+    row = group_d.third(mid, row, [(qkvg_h.at[1], heads_w), (qkvg_h.at[2], heads_w)])
+    total = vs[2]
+    for d in range(1, n_dp):
+        got[d - 1].wait_recv()
+        total = total + vr[1 + d]
+    vec_o[...] = total
+    waited = {id(c) for c in gs_got + [g.far for g in (group_a, group_b, group_c, group_d)]}
+    waited |= {id(c) for c in ffn_got + gf_got + near_got[0] + [ln1_got]}
+    for copy in copies.all:
+        if id(copy) not in waited:
+            copy.wait_send()
+    for copy in loads[6:]:
+        copy.wait()
+
+
+def one_kernel(args):
+    (
+        tokens, segment_ids, ln1_gain, ln1_bias, qkv_weight, qv_bias, out_weight, out_bias,
+        ln2_gain, ln2_bias, up_weight, up_bias, down_weight, down_bias, out_cotangent,
+    ) = args
+    count, rows, width = tokens.shape
+    heads_w, hidden = qkv_weight.shape[2], up_weight.shape[1]
+    n_dp = axis_size("dp")
+    block = width // (4 * n_dp)
+    total = count * rows
+    grads = 2 * hidden + 4 * heads_w
+    line = lambda v: v.reshape(1, -1)
+    low = lambda *shape: pltpu.VMEM(shape, LOW)
+    full = lambda *shape: pltpu.VMEM(shape, F32)
+    shape = jax.ShapeDtypeStruct
+    vmem, anywhere = pl.BlockSpec(memory_space=pltpu.VMEM), pl.BlockSpec(memory_space=pl.ANY)
+    seg = jnp.concatenate([segment_ids, jnp.zeros((8 - count, rows), jnp.int32)], axis=0)
+    return pl.pallas_call(
+        functools.partial(layer_kernel, n_dp),
+        in_specs=[anywhere, vmem, vmem, vmem, anywhere, vmem, anywhere, vmem, vmem, vmem, anywhere, vmem, anywhere, vmem, anywhere],
+        out_specs=[anywhere] * 6 + [vmem],
+        out_shape=[
+            shape((total, width), LOW),
+            shape((total, width), LOW),
+            shape((block, hidden), F32),
+            shape((block, hidden), F32),
+            shape((block, heads_w), F32),
+            shape((3, block, heads_w), F32),
+            shape((16, width), F32),
+        ],
+        scratch_shapes=[
+            low(total, width), low(total, width), low(3, width, heads_w), low(2 * heads_w, width),
+            low(width, hidden), low(hidden, width), low(total, heads_w), low(2, 4, rows, 2 * heads_w),
+            full(2, heads_w, rows), low(total, width), full(total, width), low(2, rows, width),
+            low(total, hidden), low(total, hidden),
+            low(width, total), low(width, total), low(width, total), low(width, total),
+            low(2, rows, heads_w), low(2, rows, 2 * heads_w), low(total, width), low(total, width),
+            full(2, total, 2), full(2, heads_w // LANES, 8, rows),
+            low(total, width), low(total, width), low(total, width), low(2, 3, rows, 2 * heads_w),
+            low(total, hidden), low(total, hidden),
+            low(2, width // 4, total), low(2, width // 4, total), low(2, width // 4, total), low(2, width // 4, total),
+            low(total, heads_w), low(total, 3 * heads_w), low(width // 4, grads), low(n_dp - 1, block, grads),
+            pltpu.VMEM((4, 8, rows), jnp.int32), full(4, rows, 8), full(6, 8, width), full(8, 2 * heads_w), full(8, hidden),
+            full(2, 8, width), full(3, 16, width), full(n_dp + 1, 16, width),
+            pltpu.SemaphoreType.DMA((N_COPIES,)), pltpu.SemaphoreType.DMA((N_COPIES,)), pltpu.SemaphoreType.DMA((N_LOCAL,)),
+        ],
+        compiler_params=pltpu.CompilerParams(
+            collective_id=0, has_side_effects=True, vmem_limit_bytes=FAST_VMEM
+        ),
+    )(
+        tokens.reshape(total, width), seg, line(ln1_gain), line(ln1_bias), jnp.transpose(qkv_weight, (1, 0, 2)),
+        qv_bias, out_weight, line(out_bias), line(ln2_gain), line(ln2_bias), up_weight, line(up_bias),
+        down_weight, line(down_bias), out_cotangent.reshape(total, width),
+    )
+
+
+FAST_VMEM = 62 * 2**20
+
+
+def fits(args):
+    tokens, qkv_weight, up_weight = args[0], args[4], args[10]
+    count, rows, width = tokens.shape
+    heads_w, hidden = qkv_weight.shape[2], up_weight.shape[1]
+    return (
+        (axis_size("seq"), axis_size("head"), axis_size("dp")) == (4, 2, 4)
+        and (count, rows) == (2, 256)
+        and (width, heads_w, hidden) == (1024, 512, 2048)
+    )
+
+
+def fast(*args):
+    tokens = args[0]
+    out, tokens_grad, down_grad, up_grad, out_grad, qkv_grad, vec = one_kernel(args)
+    n_dp = axis_size("dp")
+    at = lax.axis_index("seq") * n_dp + lax.axis_index("dp")
+    parts = axis_size("seq") * n_dp
+
+    def mine(values):
+        size = values.shape[-1] // parts
+        return lax.dynamic_slice_in_dim(values, at * size, size, values.ndim - 1)
+
+    return (
+        out.reshape(tokens.shape),
+        tokens_grad.reshape(tokens.shape),
+        mine(vec[0]),
+        mine(vec[1]),
+        jnp.transpose(qkv_grad, (1, 0, 2)),
+        mine(vec[6].reshape(2, -1)),
+        out_grad.T,
+        mine(vec[2]),
+        mine(vec[3]),
+        mine(vec[4]),
+        up_grad,
+        mine(vec[7:9].reshape(-1)),
+        down_grad.T,
+        mine(vec[5]),
+    )
+
+
+def shards(*args):
+    return fast(*args) if fits(args) else general(*args)
+
+
+def general(
     tokens,
     segment_ids,
     ln1_gain,

time: 430 us -> 199 us (0.46); the launches traced: 423 us -> 199 us
  Pallas kernels: 35.6 us -> 184 us
  waiting for transfers between devices: 141 us -> 0 us
  starting transfers between devices: 135 us -> 0 us
  matrix products: 65.5 us -> 0 us
  other arithmetic: 31.3 us -> 0 us
    pallas_call x4 -> x1, Pallas kernels: 35.6 us -> 184 us  [one_kernel(): pl.pallas_call(functools.partial(layer_kernel, n_dp), in_specs=[anywhere,...]
    ppermute x84 -> x0, waiting for transfers between devices: 141 us -> none  [the longest x48 108 us: swap(): lax.ppermute(value, axis, [(i, i ^ mask) for i in range(axis_size(axis))])]
    ppermute x84 -> x0, starting transfers between devices: 135 us -> none  [the longest x18 90.8 us: scatter_line(): lax.ppermute(send_up.astype(LOW), 'dp', [(i, i + 1) for i in range(n) if...]
    dot_general x48 -> x0, matrix products: 65.5 us -> none  [dot(): return lax.dot_general(a, b, dims, preferred_element_type=F32)]
    reduce_sum x10 -> x0, other arithmetic: 8.55 us -> none  [the longest x6 4.88 us: shards(): jnp.sum(value, axis=0)]
    another operation x11 -> x0, other arithmetic: 7.79 us -> none  [the longest x2 2.95 us: shards(): jnp.stack(tokens_grads)]
    add x19 -> x0, other arithmetic: 6.75 us -> none  [the longest x4 5.8 us: scatter_seq(): parts[m ^ bit] = parts[m ^ bit].astype(F32) + got.astype(F32)]
    convert_element_type x24 -> x0, other arithmetic: 5.18 us -> none  [the longest x12 2.45 us: scatter_line(): send_up.astype(LOW)]
  transfers between devices with their start and end apart: 84 -> 0, of which waited for: 29 -> 0; matrix products, arithmetic and copies ran while one was open for 23% -> 0% of each run, Pallas kernels for 8% -> 0%
where the time goes in v2:
time: 199 us
  Pallas kernels  184 us (92%)
  local copies, waits for them, and re-layouts  13.8 us (7%)
    pallas_call x1, Pallas kernels, one_kernel(): pl.pallas_call(functools.partial(layer_kernel, n_dp), in_specs=[anywhere,...  184 us
    unnamed x16, local copies, waits for them, and re-layouts  8.38 us

profile of v2, /device:TPU:0, one launch (start us, length us, event | category | flops | bytes accessed | tf_op | source)
XLA Modules:
  0.0 198.6 jit_solution(2489345320566145266)
XLA Ops:
  0.7 1.3 concatenate.3.refs_1_
  1.9 184.0 %shard_map.254 = (bf16[512,1024]{1,0:T(8,128)(2,1)}, bf16[512,1024]{1,0:T(8,128)(2,1)}, f32[64,2048]{1,0:T(8,128)}, f32[64,2048]{1,0:T(8,128)}, f32[64,512]{1,0:...) custom-call(bf16[512,1024]{1,0:T(8,128)(2,1)} %bitcast.35, s32[8,256]{1,0:T(8,128)} %concatenate.3.refs_1_, ...), custom_call_target="tpu_custom_call" | custom-call | tf_op jit(solution)/shard_map/pallas_call | solution.py:922
  186.0 0.0 copy-start.2
  186.0 0.0 copy-start.3
  186.0 0.0 copy-start.1
  186.0 0.0 copy-start
  186.0 1.2 fusion.6
  187.2 0.6 fusion.4
  187.8 0.6 fusion.2
  188.4 0.6 fusion
  189.0 0.6 constant_dynamic-slice_fusion.4
  189.6 0.8 slice_bitcast_fusion
  190.5 0.6 dynamic_slice.47
  191.1 2.3 %copy.38 = bf16[2,256,1024]{2,1,0:T(8,128)(2,1)} copy(bf16[2,256,1024]{2,1,0:T(8,128)(2,1)} %bitcast.34) | data formatting | bytes 2097152
  193.3 2.3 %copy.39 = bf16[2,256,1024]{2,1,0:T(8,128)(2,1)} copy(bf16[2,256,1024]{2,1,0:T(8,128)(2,1)} %bitcast.33) | data formatting | bytes 2097152
  195.6 0.0 copy-done.2
  195.6 0.7 copy.40
  196.3 0.0 copy-done.3
  196.3 0.7 copy.41
  197.0 0.0 copy-done.1
  197.0 0.8 copy.42
  197.8 0.0 copy-done
  197.8 0.8 copy.43
  (2 shorter events, 0.0 us)
Async XLA Ops:
  186.0 9.6 %copy-start.2 = (f32[3,64,512]{2,1,0:T(8,128)S(1)}, f32[3,64,512]{2,1,0:T(8,128)}, u32[]{:S(2)}) copy-start(f32[3,64,512]{2,1,0:T(8,128)} %get-tuple-element.24) | copy-start | bytes 1179652
  186.0 10.3 %copy-start.3 = (f32[64,512]{1,0:T(8,128)S(1)}, f32[64,512]{1,0:T(8,128)}, u32[]{:S(2)}) copy-start(f32[64,512]{1,0:T(8,128)} %get-tuple-element.25) | copy-start | bytes 393220
  186.0 11.0 %copy-start.1 = (f32[64,2048]{1,0:T(8,128)S(1)}, f32[64,2048]{1,0:T(8,128)}, u32[]{:S(2)}) copy-start(f32[64,2048]{1,0:T(8,128)} %get-tuple-element.65) | copy-start | bytes 1572868
  186.0 11.8 %copy-start = (f32[64,2048]{1,0:T(8,128)S(1)}, f32[64,2048]{1,0:T(8,128)}, u32[]{:S(2)}) copy-start(f32[64,2048]{1,0:T(8,128)} %get-tuple-element.27) | copy-start | bytes 1572868

commit v3 on v2

--- a/solution.py
+++ b/solution.py
@@ -293,26 +293,62 @@
     return jnp.sum(value.reshape(value.shape[0] // 8, 8, value.shape[1]), axis=0)
 
 
+class Copy:
+    def __init__(self, copy, remote):
+        self.copy, self.remote = copy, remote
+        self.sent = self.got = False
+
+    def wait_recv(self):
+        if not self.got:
+            self.got = True
+            if self.remote:
+                self.copy.wait_recv()
+            else:
+                self.copy.wait()
+
+    def wait_send(self):
+        if self.remote and not self.sent:
+            self.copy.wait_send()
+        self.sent = True
+
+    def wait(self):
+        self.wait_send()
+        self.wait_recv()
+
+
 class Copies:
-    def __init__(self, send, recv):
-        self.send, self.recv, self.all, self.n = send, recv, [], 0
+    def __init__(self, send, recv, local):
+        self.sems, self.all = (send, recv, local), []
+        self.n_remote = self.n_local = 0
 
     def start(self, src, dst, device):
         copy = pltpu.make_async_remote_copy(
             src_ref=src,
             dst_ref=dst,
-            send_sem=self.send.at[self.n],
-            recv_sem=self.recv.at[self.n],
+            send_sem=self.sems[0].at[self.n_remote],
+            recv_sem=self.sems[1].at[self.n_remote],
             device_id=device,
             device_id_type=MESH,
         )
+        self.n_remote += 1
+        return self.begin(copy, True)
+
+    def load(self, src, dst):
+        copy = pltpu.make_async_copy(src, dst, self.sems[2].at[self.n_local])
+        self.n_local += 1
+        return self.begin(copy, False)
+
+    def begin(self, copy, remote):
         copy.start()
-        self.n += 1
-        self.all.append(copy)
-        return copy
-
-
-N_COPIES = 96
+        self.all.append(Copy(copy, remote))
+        return self.all[-1]
+
+    def finish(self):
+        for copy in self.all:
+            copy.wait()
+
+
+N_COPIES = 128
 N_LOCAL = 24
 
 
@@ -321,8 +357,9 @@
         tok_h, seg_in, g1, b1, wqkv_h, qvb, outw_h, outb, g2, b2, up_h, upb, down_h, downb, cot_h,
         out_h, tg_h, downg_h, upg_h, outg_h, qkvg_h, vec_o,
         tok, cot, wqkv, outw, up, down, q, kv, attn_t, attn, mid, lnb, act, gh,
-        first_t, second_t, cot_t, gb_t, g_attn, t2, gs, ffn, stat, st,
-        gs_r, ffn_r, gf_r, dkv_r, act_r, gh_r, first_r, second_r, cot_r, gb_r, heads_r, dqkv_r, xr, zr,
+        first_t, second_t, cot_t, gb_t, g_attn, gs, ffn, stat, st,
+        gs_r, ffn_r, gf_r, dkv_r, q_far, g_far, st_far, act_r, gh_r, first_r, second_r, cot_r, gb_r, heads_r, dqkv_r,
+        xr, zr, xz, zz,
         segs, segk, vec, qvacc, upacc, ln1_r, vs, vr,
         send, recv, local,
     ) = refs
@@ -339,37 +376,26 @@
     x, core = s // 2, s % 2
     seq_peer = [None] + [((x ^ (m >> 1)) * 2 + (core ^ (m & 1)), h, z) for m in (1, 2, 3)]
     across = (s, 1 - h, z)
-    along = [None] + [(s, h, lax.rem(z + n_dp - d, n_dp)) for d in range(1, n_dp)]
-    copies = Copies(send, recv)
-    loads = []
-
-    def load(src, dst):
-        copy = pltpu.make_async_copy(src, dst, local.at[len(loads)])
-        copy.start()
-        loads.append(copy)
-        return copy
-
+    next_z, far_z = z + 1 - 2 * lax.rem(z, 2), lax.rem(z + 2, 4)
+    beside, beyond = (s, h, next_z), (s, h, far_z)
+    half_w = heads_w // 2
+    copies = Copies(send, recv, local)
+    load = copies.load
+
+    own_out = pl.ds(pl.multiple_of(h * heads_w, heads_w), heads_w)
     get_tok = load(tok_h, tok)
     get_qkv = load(wqkv_h, wqkv)
-    own_out = pl.ds(pl.multiple_of(h * heads_w, heads_w), heads_w)
-    get_out = load(outw_h, outw.at[own_out, :])
-    get_cot = load(cot_h, cot)
-    get_up = load(up_h, up)
-    get_down = load(down_h, down)
 
     barrier = pltpu.get_barrier_semaphore()
-    partners = seq_peer[1:] + [across] + along[1:]
+    partners = seq_peer[1:] + [across, beside, beyond]
     for device in partners:
         pl.semaphore_signal(barrier, inc=1, device_id=device, device_id_type=MESH)
 
     vec[...] = jnp.zeros_like(vec)
     qvacc[...] = jnp.zeros_like(qvacc)
     upacc[...] = jnp.zeros_like(upacc)
-    segs[0] = seg_in[...]
-    pl.semaphore_wait(barrier, len(partners))
-
-    seg_got = [None] + [copies.start(segs.at[0], segs.at[m], seq_peer[m]) for m in (1, 2, 3)]
-
+    segs[0] = jnp.zeros_like(segs[0])
+    segs[0, 0:2, :] = seg_in[...]
     def seq_rows(i):
         return slice(i * rows, (i + 1) * rows)
 
@@ -389,9 +415,10 @@
             for c in range(2)
         ]
 
-    kv_got = [[None] * 4, [None] * 4]
-
-    def project(i):
+    kv_got = [[[None] * 2 for _ in range(4)] for _ in range(2)]
+    q_got, q_next = [None] * 2, [None] * 2
+
+    def first_norm(i):
         def norm(c):
             at = pl.ds(pl.multiple_of(i * rows + c * CHUNK, CHUNK), CHUNK)
             v = tok[at, :].astype(F32)
@@ -403,35 +430,45 @@
             lnb[i, span(c, CHUNK), :] = (v * inverse * g1[...] + b1[...]).astype(LOW)
 
         loop(rows // CHUNK, norm)
-        low = lnb.at[i]
-
-        def tile_kv(j):
-            at = span(j, 256)
-            kv[i, 0, :, at] = dot(low[...], wqkv[1, :, at]).astype(LOW)
-            up_at = pl.ds(pl.multiple_of(heads_w + j * 256, 256), 256)
-            kv[i, 0, :, up_at] = (dot(low[...], wqkv[2, :, at]) + qvb[1:2, at]).astype(LOW)
-
-        if i == 0:
-            get_qkv.wait()
-        loop(heads_w // 256, tile_kv)
-        kv_got[i][2] = copies.start(kv.at[i, 0], kv.at[i, 2], seq_peer[2])
-        kv_got[i][1] = copies.start(kv.at[i, 0], kv.at[i, 1], seq_peer[1])
-
-        def tile_q(j):
-            at = span(j, 256)
-            q[seq_rows(i), at] = (dot(low[...], wqkv[0, :, at]) + qvb[0:1, at]).astype(LOW)
-
-        loop(heads_w // 256, tile_q)
-        flip(low, i, first_t)
-
-    def attend_blocks(i, blocks, begin, end):
+
+    def keys_values(i):
+        k = dot(lnb[i], wqkv[1]).astype(LOW)
+        v = (dot(lnb[i], wqkv[2]) + qvb[1:2, :]).astype(LOW)
+        for part in range(2):
+            cols = slice(part * half_w, (part + 1) * half_w)
+            kv[i, 0, part, :, 0:half_w] = k[:, cols]
+            kv[i, 0, part, :, half_w:heads_w] = v[:, cols]
+
+    def send_keys(i):
+        for part in range(2):
+            kv_got[i][2][part] = copies.start(kv.at[i, 0, part], kv.at[i, 2, part], seq_peer[2])
+        for part in range(2):
+            kv_got[i][1][part] = copies.start(kv.at[i, 0, part], kv.at[i, 1, part], seq_peer[1])
+
+    def queries(i):
+        q[seq_rows(i), :] = (dot(lnb[i], wqkv[0]) + qvb[0:1, :]).astype(LOW)
+        q_got[i] = copies.start(q.at[seq_rows(i), :], q_far.at[i, 0], seq_peer[2])
+        flip(lnb.at[i], i, first_t)
+
+    seg_got = [None] * 4
+
+    def meet():
+        pl.semaphore_wait(barrier, len(partners))
+        for m in (1, 2, 3):
+            seg_got[m] = copies.start(segs.at[0], segs.at[m], seq_peer[m])
+
+    def key_lanes(p):
+        lane = lax.rem(p, 2) * LANES
+        return p // 2, pl.ds(pl.multiple_of(lane, LANES), LANES), pl.ds(pl.multiple_of(half_w + lane, LANES), LANES)
+
+    def attend_blocks(i, blocks, begin, end, start, stop):
         seg_q = segs[0, i:i + 1, :].astype(F32)
 
         def pair(p):
             lanes = span(p, LANES)
-            v_lanes = pl.ds(pl.multiple_of(heads_w + p * LANES, LANES), LANES)
+            part, k_lanes, v_lanes = key_lanes(p)
             qp = q[seq_rows(i), lanes] * jnp.asarray(0.125, LOW)
-            vts = [kv[i, m, :, v_lanes].T for m in blocks]
+            vts = [kv[i, m, part, :, v_lanes].T for m in blocks]
             for head in range(2):
                 at = pl.ds(pl.multiple_of(p * LANES + head * HEAD_DIM, HEAD_DIM), HEAD_DIM)
                 qh = jnp.where(half_lanes(qp.shape, head), qp, jnp.zeros_like(qp))
@@ -439,14 +476,14 @@
                 top = None if begin else st[i, p, head:head + 1, :]
                 old = top
                 for m in blocks:
-                    score = dot(kv[i, m, :, lanes], qh, NT)
+                    score = dot(kv[i, m, part, :, k_lanes], qh, NT)
                     score = jnp.where(segk[m, :, i:i + 1] == seg_q, score, MASKED)
                     peak = jnp.max(score, axis=0, keepdims=True)
                     top = peak if top is None else jnp.maximum(top, peak)
                     parts.append(score)
                 total = mixed = 0.0
-                for part, vt in zip(parts, vts):
-                    w = jnp.exp(part - top)
+                for score, vt in zip(parts, vts):
+                    w = jnp.exp(score - top)
                     total = total + jnp.sum(w, axis=0, keepdims=True)
                     mixed = mixed + dot(vt[head * HEAD_DIM:(head + 1) * HEAD_DIM, :], w.astype(LOW))
                 if not begin:
@@ -464,7 +501,7 @@
                 to = pl.ds(pl.multiple_of(h * heads_w + p * LANES, LANES), LANES)
                 attn[seq_rows(i), to] = attn_t[i, lanes, :].T.astype(LOW)
 
-        loop(pairs, pair)
+        lax.fori_loop(start, stop, lambda p, c: (pair(p), c)[1], 0)
 
     def seg_columns(m):
         segk[m] = segs[m].astype(F32).T
@@ -472,12 +509,19 @@
     own_heads = pl.ds(pl.multiple_of(h * heads_w, heads_w), heads_w)
     attn_got = [None, None]
 
-    def attend_far(i):
-        kv_got[i][2].wait_recv()
-        kv_got[i][3] = copies.start(kv.at[i, 2], kv.at[i, 3], seq_peer[1])
-        attend_blocks(i, (2,), False, False)
-        kv_got[i][3].wait_recv()
-        attend_blocks(i, (3,), False, True)
+    def forward_keys(i, part):
+        kv_got[i][2][part].wait_recv()
+        kv_got[i][3][part] = copies.start(kv.at[i, 2, part], kv.at[i, 3, part], seq_peer[1])
+
+    def forward_queries(i):
+        q_got[i].wait_recv()
+        q_next[i] = copies.start(q_far.at[i, 0], q_far.at[i, 1], seq_peer[1])
+
+    def attend_far(i, part):
+        kv_got[i][3][part].wait_recv()
+        attend_blocks(i, (2, 3), False, True, part * pairs // 2, (part + 1) * pairs // 2)
+
+    def send_heads(i):
         mine = attn.at[seq_rows(i), own_heads]
         attn_got[i] = copies.start(mine, mine, across)
         heads_sent[i] = copies.start(mine, heads_r.at[seq_rows(i), :], seq_peer[1])
@@ -488,14 +532,14 @@
         attn_got[i].wait_recv()
 
         def tile(j):
-            at = span(j, 256)
+            at = span(j, WIDE)
             mid[seq_rows(i), at] = (
                 dot(attn[seq_rows(i), :], outw[:, at])
                 + tok[seq_rows(i), at].astype(F32)
                 + outb[:, at]
             )
 
-        loop(width // 256, tile)
+        loop(width // WIDE, tile)
 
         def norm(c):
             at = pl.ds(pl.multiple_of(i * rows + c * CHUNK, CHUNK), CHUNK)
@@ -511,23 +555,30 @@
 
     gs_got, ffn_got, act_got, gh_got = [None] * 2, [None] * 2, [None] * 2, [None] * 2
 
+    def cot_down(i):
+        def tile(j):
+            at = span(j, 2 * WIDE)
+            gh[seq_rows(i), at] = dot(cot[seq_rows(i), :], down[at, :], NT).astype(LOW)
+
+        loop(hidden // (2 * WIDE), tile)
+
     def feed(i):
         at_rows = seq_rows(i)
 
         def tile(j):
-            at = span(j, 256)
+            at = span(j, WIDE)
             value, slope = gelu_pair(dot(lnb[i], up[:, at]) + upb[:, at])
             act[at_rows, at] = value.astype(LOW)
-            g = (dot(cot[at_rows, :], down[at, :], NT) * slope).astype(LOW)
+            g = (gh[at_rows, at].astype(F32) * slope).astype(LOW)
             gh[at_rows, at] = g
             upacc[:, at] += fold(g.astype(F32))
 
-        loop(hidden // 256, tile)
+        loop(hidden // WIDE, tile)
 
         def back(j):
-            gs[at_rows, span(j, 256)] = dot(gh[at_rows, :], up[span(j, 256), :], NT).astype(LOW)
-
-        loop(width // 256, back)
+            gs[at_rows, span(j, WIDE)] = dot(gh[at_rows, :], up[span(j, WIDE), :], NT).astype(LOW)
+
+        loop(width // WIDE, back)
         gs_got[i] = copies.start(gs.at[at_rows, :], gs_r.at[at_rows, :], across)
         act_got[i] = copies.start(act.at[at_rows, :], act_r.at[at_rows, :], seq_peer[1])
         gh_got[i] = copies.start(gh.at[at_rows, :], gh_r.at[at_rows, :], seq_peer[1])
@@ -537,10 +588,12 @@
         at_rows = seq_rows(i)
 
         def tile(j):
-            ffn[at_rows, span(j, 256)] = dot(act[at_rows, :], down[:, span(j, 256)]).astype(LOW)
-
-        loop(width // 256, tile)
-        ffn_got[i] = copies.start(ffn.at[at_rows, :], ffn_r.at[at_rows, :], across)
+            ffn[at_rows, span(j, WIDE)] = dot(act[at_rows, :], down[:, span(j, WIDE)]).astype(LOW)
+
+        loop(width // WIDE, tile)
+
+    def send_feed_out(i):
+        ffn_got[i] = copies.start(ffn.at[seq_rows(i), :], ffn_r.at[seq_rows(i), :], across)
 
     def finish_output(i):
         ffn_got[i].wait()
@@ -554,7 +607,7 @@
         load(ffn.at[seq_rows(i), :], out_h.at[seq_rows(i), :])
 
     gb = down.at[2 * rows:4 * rows, :]
-    parts_kv = [down.at[(4 + m) * rows:(5 + m) * rows, :] for m in range(4)]
+    parts_kv = [[down.at[(4 + 2 * i + m) * rows:(5 + 2 * i + m) * rows, :] for m in range(2)] for i in range(2)]
     dqkv = up.at[2 * rows:4 * rows, :]
 
     def norm2_back(i):
@@ -575,114 +628,131 @@
 
         loop(rows // CHUNK, part)
 
-        def tile(j):
-            w_rows = pl.ds(pl.multiple_of(h * heads_w + j * 256, 256), 256)
-            g_attn[i, :, span(j, 256)] = dot(gb[seq_rows(i), :], outw[w_rows, :], NT).astype(LOW)
-
-        loop(heads_w // 256, tile)
-
-    def attend_back_pairs(i, start, stop):
+        w_rows = pl.ds(pl.multiple_of(h * heads_w, heads_w), heads_w)
+        g_attn[i] = dot(gb[seq_rows(i), :], outw[w_rows, :], NT).astype(LOW)
+
+        def delta(p):
+            g = g_attn[i, :, span(p, LANES)].astype(F32).T
+            each = g * attn_t[i, span(p, LANES), :]
+            for head in range(2):
+                part = each[head * HEAD_DIM:(head + 1) * HEAD_DIM, :]
+                st[i, p, 6 + head:7 + head, :] = jnp.sum(part, axis=0, keepdims=True)
+
+        loop(pairs, delta)
+        g_got[i] = [
+            copies.start(g_attn.at[i], g_far.at[i, 0], seq_peer[2]),
+            copies.start(st.at[i], st_far.at[i, 0], seq_peer[2]),
+        ]
+
+    g_got, g_next = [None] * 2, [None] * 2
+
+    def forward_grads(i):
+        for copy in g_got[i]:
+            copy.wait_recv()
+        g_next[i] = [
+            copies.start(g_far.at[i, 0], g_far.at[i, 1], seq_peer[1]),
+            copies.start(st_far.at[i, 0], st_far.at[i, 1], seq_peer[1]),
+        ]
+
+    def heads_of(pair_value, scale=None):
+        if scale is not None:
+            pair_value = pair_value * jnp.asarray(scale, LOW)
+        zeros = jnp.zeros_like(pair_value)
+        return [jnp.where(half_lanes(pair_value.shape, head), pair_value, zeros) for head in range(2)]
+
+    def backward_terms(allowed, k, v, q_scaled, g, stats, head):
+        score = dot(k, q_scaled[head], NT)
+        probs = jnp.exp(jnp.where(allowed, score - stats[4 + head:5 + head, :], MASKED))
+        return probs.astype(LOW), (probs * (dot(v, g[head], NT) - stats[6 + head:7 + head, :])).astype(LOW)
+
+    def back_own(i):
         seg_q = segs[0, i:i + 1, :].astype(F32)
 
         def pair(p):
             lanes = span(p, LANES)
             v_lanes = pl.ds(pl.multiple_of(heads_w + p * LANES, LANES), LANES)
-            qp = q[seq_rows(i), lanes]
-            g = g_attn[i, :, lanes]
-            gt = g.astype(F32).T
-            qs, qscaled, gs_, gts, deltas, lses = [], [], [], [], [], []
-            for head in range(2):
-                at = pl.ds(pl.multiple_of(p * LANES + head * HEAD_DIM, HEAD_DIM), HEAD_DIM)
-                mask = half_lanes(qp.shape, head)
-                part = gt[head * HEAD_DIM:(head + 1) * HEAD_DIM, :]
-                deltas.append(jnp.sum(part * attn_t[i, at, :], axis=0, keepdims=True))
-                zeros = jnp.zeros_like(part)
-                full = jnp.concatenate([part, zeros] if head == 0 else [zeros, part], axis=0)
-                gts.append(full.astype(LOW))
-                gs_.append(jnp.where(mask, g, jnp.zeros_like(g)))
-                qs.append(jnp.where(mask, qp, jnp.zeros_like(qp)))
-                qscaled.append(qs[-1] * jnp.asarray(0.125, LOW))
-                lses.append(st[i, p, 4 + head:5 + head, :])
+            part, k_in, v_in = key_lanes(p)
+            qs = heads_of(q[seq_rows(i), lanes])
+            q_scaled = heads_of(q[seq_rows(i), lanes], 0.125)
+            g = heads_of(g_attn[i, :, lanes])
+            stats = st[i, p]
             dqt = [0.0, 0.0]
             for m in range(4):
-                k = kv[i, m, :, lanes]
+                k = kv[i, m, part, :, k_in]
                 kt = k.T
-                v = kv[i, m, :, v_lanes]
+                v = kv[i, m, part, :, v_in]
                 allowed = segk[m, :, i:i + 1] == seg_q
                 dk = dv = 0.0
                 for head in range(2):
-                    score = dot(k, qscaled[head], NT)
-                    probs = jnp.exp(jnp.where(allowed, score - lses[head], MASKED))
-                    ds = (probs * (dot(v, gts[head]) - deltas[head])).astype(LOW)
-                    dk = dk + dot(ds, qs[head])
-                    dv = dv + dot(probs.astype(LOW), gs_[head])
+                    probs, ds = backward_terms(allowed, k, v, q_scaled, g, stats, head)
+                    if m < 2:
+                        dk = dk + dot(ds, qs[head])
+                        dv = dv + dot(probs, g[head])
                     dqt[head] = dqt[head] + dot(kt[head * HEAD_DIM:(head + 1) * HEAD_DIM, :], ds)
-                parts_kv[m][:, lanes] = (dk * 0.125).astype(LOW)
-                parts_kv[m][:, v_lanes] = dv.astype(LOW)
+                if m < 2:
+                    parts_kv[i][m][:, lanes] = (dk * 0.125).astype(LOW)
+                    parts_kv[i][m][:, v_lanes] = dv.astype(LOW)
             dq = (jnp.concatenate(dqt, axis=0).T * 0.125).astype(LOW)
             dqkv[seq_rows(i), lanes] = dq
             qvacc[:, lanes] += fold(dq.astype(F32))
 
-        lax.fori_loop(start, stop, lambda p, c: (pair(p), c)[1], 0)
-
-    near_got, far_got, dq_got = [None] * 2, [None] * 2, [None] * 2
-    kv_cols = pl.ds(heads_w, 2 * heads_w)
-
-    def keys_near(i):
-        near_got[i] = [
-            copies.start(parts_kv[3], dkv_r.at[i, 2], seq_peer[1]),
-            copies.start(parts_kv[1], dkv_r.at[i, 0], seq_peer[1]),
-        ]
+        loop(pairs, pair)
+        near_got[i] = copies.start(parts_kv[i][1], dkv_r.at[i], seq_peer[1])
         at = (seq_rows(i), pl.ds(0, heads_w))
         dq_got[i] = copies.start(dqkv.at[at], dqkv_r.at[at], seq_peer[1])
 
-    def keys_far(i):
-        near_got[i][0].wait_recv()
-
-        def part(c):
-            at = span(c, 64)
-            t2[i, at, :] = (parts_kv[2][at, :].astype(F32) + dkv_r[i, 2, at, :].astype(F32)).astype(LOW)
-
-        loop(rows // 64, part)
-        far_got[i] = copies.start(t2.at[i], dkv_r.at[i, 1], seq_peer[2])
-        near_got[i][1].wait_recv()
-
-        def rest(c):
-            at = span(c, 64)
-            to = pl.ds(pl.multiple_of(i * rows + c * 64, 64), 64)
-            dqkv[to, kv_cols] = (parts_kv[0][at, :].astype(F32) + dkv_r[i, 0, at, :].astype(F32)).astype(LOW)
-
-        loop(rows // 64, rest)
+    def back_far(i):
+        q_next[i].wait_recv()
+        for copy in g_next[i]:
+            copy.wait_recv()
+        near_got[i].wait_recv()
+        seg_q = [segs[2 + b, i:i + 1, :].astype(F32) for b in range(2)]
+        at_rows = seq_rows(i)
+
+        def pair(p):
+            lanes = span(p, LANES)
+            v_lanes = pl.ds(pl.multiple_of(heads_w + p * LANES, LANES), LANES)
+            part, k_in, v_in = key_lanes(p)
+            k = kv[i, 0, part, :, k_in]
+            v = kv[i, 0, part, :, v_in]
+            dk = dv = 0.0
+            for b in range(2):
+                qs = heads_of(q_far[i, b, :, lanes])
+                q_scaled = heads_of(q_far[i, b, :, lanes], 0.125)
+                g = heads_of(g_far[i, b, :, lanes])
+                allowed = segk[0, :, i:i + 1] == seg_q[b]
+                for head in range(2):
+                    probs, ds = backward_terms(allowed, k, v, q_scaled, g, st_far[i, b, p], head)
+                    dk = dk + dot(ds, qs[head])
+                    dv = dv + dot(probs, g[head])
+            near = lambda to: parts_kv[i][0][:, to].astype(F32) + dkv_r[i, :, to].astype(F32)
+            k_at = pl.ds(pl.multiple_of(heads_w + p * LANES, LANES), LANES)
+            v_at = pl.ds(pl.multiple_of(2 * heads_w + p * LANES, LANES), LANES)
+            dqkv[at_rows, k_at] = (dk * 0.125 + near(lanes)).astype(LOW)
+            low = (dv + near(v_lanes)).astype(LOW)
+            dqkv[at_rows, v_at] = low
+            qvacc[:, k_at] += fold(low.astype(F32))
+
+        loop(pairs, pair)
+        at = (at_rows, kv_cols)
+        dkv_got[i] = copies.start(dqkv.at[at], dqkv_r.at[at], seq_peer[1])
+
+    near_got, dq_got = [None] * 2, [None] * 2
+    kv_cols = pl.ds(heads_w, 2 * heads_w)
 
     dkv_got, gf_got = [None] * 2, [None] * 2
-
-    def keys_done(i):
-        far_got[i].wait_recv()
-
-        def part(c):
-            at = span(c, 64)
-            to = pl.ds(pl.multiple_of(i * rows + c * 64, 64), 64)
-            low = (dqkv[to, kv_cols].astype(F32) + dkv_r[i, 1, at, :].astype(F32)).astype(LOW)
-            dqkv[to, kv_cols] = low
-            qvacc[:, pl.ds(heads_w, heads_w)] += fold(low[:, heads_w:].astype(F32))
-
-        loop(rows // 64, part)
-        at = (seq_rows(i), kv_cols)
-        dkv_got[i] = copies.start(dqkv.at[at], dqkv_r.at[at], seq_peer[1])
 
     def first_back(i):
         gs_got[i].wait_send()
 
         def tile(j):
-            at = span(j, 256)
+            at = span(j, WIDE)
             total = 0.0
             for c in range(3):
                 total = total + dot(dqkv[seq_rows(i), c * heads_w:(c + 1) * heads_w], wqkv[c, at, :], NT)
             gs[seq_rows(i), at] = total.astype(LOW)
 
-        loop(width // 256, tile)
-        gf_got[i] = copies.start(gs.at[seq_rows(i), :], gf_r.at[seq_rows(i), :], across)
-
+        loop(width // WIDE, tile)
         def sums(c):
             at = pl.ds(pl.multiple_of(i * rows + c * CHUNK, CHUNK), CHUNK)
             g = gs[at, :].astype(F32)
@@ -691,6 +761,9 @@
             vec[1] += fold(g)
 
         loop(rows // CHUNK, sums)
+
+    def send_first_back(i):
+        gf_got[i] = copies.start(gs.at[seq_rows(i), :], gf_r.at[seq_rows(i), :], across)
 
     def norm1_back(i):
         gf_got[i].wait()
@@ -707,199 +780,339 @@
         loop(rows // CHUNK, part)
         load(gs.at[seq_rows(i), :], tg_h.at[seq_rows(i), :])
 
-    def piece_tiles(piece, chip, body):
+    def tiles(piece, chip, body):
         left, left_r, right, right_r, cols = piece
         at_rows = pl.ds(pl.multiple_of(chip * 2 * quarter + core * quarter, quarter), quarter)
+        step = min(cols, 2 * WIDE)
 
         def tile(j):
-            at = span(j, WIDE)
-            body(j, dot(left[at_rows, :], right[:, at]) + dot(left_r[chip], right_r[:, at]))
-
-        loop(cols // WIDE, tile)
-
-    class Group:
-        def __init__(self, pieces, hold, offset, arrivals):
-            self.pieces, self.hold, self.arrivals = pieces, hold, arrivals
-            self.cols = sum(p[4] for p in pieces)
-            self.xr = xr.at[:, pl.ds(offset, self.cols)]
-            self.zr = [zr.at[d, :, pl.ds(offset, self.cols)] for d in range(n_dp - 1)]
-
-        def tiles(self, chip, body):
-            base = 0
-            for piece in self.pieces:
-                piece_tiles(
-                    piece,
-                    chip,
-                    lambda j, value, base=base: body(
-                        pl.ds(pl.multiple_of(base + j * WIDE, WIDE), WIDE), value
-                    ),
-                )
-                base += piece[4]
-
-        def first(self):
+            at = span(j, step)
+            body(at, dot(left[at_rows, :], right[:, at]) + dot(left_r[chip], right_r[:, at]))
+
+        loop(cols // step, tile)
+
+    def block_rows(index):
+        return pl.ds(pl.multiple_of(index * block, block), block)
+
+    def send_beside(hold, arrive):
+        further = lax.rem(next_z + 2, 4)
+        return [
+            copies.start(hold.at[block_rows(next_z), :], arrive[0], beside),
+            copies.start(hold.at[block_rows(further), :], arrive[1], beside),
+        ]
+
+    def send_beyond(hold, arrive):
+        at = block_rows(far_z)
+        hold[at, :] = (hold[at, :].astype(F32) + arrive[1][...].astype(F32)).astype(LOW)
+        return copies.start(hold.at[at, :], arrive[2], beyond)
+
+    def own_block(hold, arrive, at=slice(None)):
+        total = hold[block_rows(z), at].astype(F32)
+        return total + arrive[0][:, at].astype(F32) + arrive[2][:, at].astype(F32)
+
+    def hand_out(place, target, value):
+        size = target.shape[1]
+        top, left = place // 2 * block, place % 2 * (width // 2)
+        mid[top:top + block, left:left + size] = value(slice(None))
+        load(mid.at[top:top + block, left:left + size], target)
+        return place + size * 2 // width
+
+    class AcrossFirst:
+        def __init__(self, piece, hold, offset, arrivals):
+            self.piece, self.hold, self.arrivals = piece, hold, arrivals
+            cols = pl.ds(offset, piece[4])
+            self.xr = xr.at[:, cols]
+            self.zr = [zr.at[d, :, cols] for d in range(3)]
+
+        def prepare(self):
             for copy in self.arrivals():
                 copy.wait_recv()
 
             def keep(at, value):
                 self.hold[:, at] = value.astype(LOW)
 
-            self.tiles(1 - x, keep)
+            tiles(self.piece, 1 - x, keep)
+
+        def across(self):
             self.far = copies.start(self.hold, self.xr, seq_peer[2])
 
-        def second(self):
+        def beside(self):
             self.far.wait()
 
             def keep(at, value):
                 self.hold[:, at] = (value + self.xr[:, at].astype(F32)).astype(LOW)
 
-            self.tiles(x, keep)
-            self.got = []
-            for d in range(1, n_dp):
-                to = lax.rem(z + n_dp - d, n_dp)
-                mine = pl.ds(pl.multiple_of(to * block, block), block)
-                self.got.append(copies.start(self.hold.at[mine, :], self.zr[d - 1], along[d]))
-
-        def third(self, stage, row, targets):
-            for copy in self.got:
+            tiles(self.piece, x, keep)
+            self.near = send_beside(self.hold, self.zr)
+
+        def beyond(self):
+            for copy in self.near:
                 copy.wait_recv()
-            mine = pl.ds(pl.multiple_of(z * block, block), block)
-            at_col = 0
-            for target, size in targets:
-                at = pl.ds(at_col, size)
-                total = self.hold[mine, at].astype(F32)
-                for d in range(n_dp - 1):
-                    total = total + self.zr[d][:, at].astype(F32)
-                place = stage.at[row:row + block, 0:size]
-                stage[row:row + block, 0:size] = total
-                load(place, target)
-                at_col += size
-                row += block
-            return row
+            self.last = send_beyond(self.hold, self.zr)
+
+        def done(self, place, target):
+            self.last.wait_recv()
+            return hand_out(place, target, lambda at: own_block(self.hold, self.zr, at))
+
+    class AlongFirst:
+        def __init__(self, piece, holds, offset, arrivals):
+            self.piece, self.holds, self.arrivals = piece, holds, arrivals
+            cols = pl.ds(offset, piece[4])
+            self.zz = [[zz.at[r, d, :, cols] for d in range(3)] for r in range(2)]
+            self.xz = xz.at[:, cols]
+
+        def beside(self):
+            for copy in self.arrivals():
+                copy.wait_recv()
+            self.near = []
+            for r in (1, 0):
+
+                def keep(at, value, r=r):
+                    self.holds[r][:, at] = value.astype(LOW)
+
+                tiles(self.piece, x ^ r, keep)
+                self.near += send_beside(self.holds[r], self.zz[r])
+
+        def beyond(self):
+            for copy in self.near:
+                copy.wait_recv()
+            self.last = [send_beyond(self.holds[r], self.zz[r]) for r in (1, 0)]
+
+        def across(self):
+            for copy in self.last:
+                copy.wait_recv()
+            mine = block_rows(z)
+            self.holds[1][mine, :] = own_block(self.holds[1], self.zz[1]).astype(LOW)
+            self.far = copies.start(self.holds[1].at[mine, :], self.xz, seq_peer[2])
+
+        def done(self, place, target):
+            self.far.wait_recv()
+
+            def value(at):
+                return own_block(self.holds[0], self.zz[0], at) + self.xz[:, at].astype(F32)
+
+            return hand_out(place, target, value)
 
     attn_own = attn.at[:, own_heads]
     q_cols, k_cols, v_cols = (slice(c * heads_w, (c + 1) * heads_w) for c in range(3))
     flips = {}
-    group_a = Group(
-        [(cot_t, cot_r, act, act_r, hidden)], up.at[0:rows, :], 0, lambda: flips["cot"] + act_got
+    down_piece = lambda at, n: (cot_t, cot_r, act.at[:, at:at + n], act_r.at[:, at:at + n], n)
+    up_piece = lambda at, n: (second_t, second_r, gh.at[:, at:at + n], gh_r.at[:, at:at + n], n)
+    proj_piece = lambda at: (first_t, first_r, dqkv.at[:, at], dqkv_r.at[:, at], heads_w)
+    quarter_h = hidden // 4
+    from_cot, from_second = lambda: flips["cot"] + act_got, lambda: flips["second"] + gh_got
+    downs = [
+        AcrossFirst(down_piece(at, n), up.at[0:rows, at:at + n], at, from_cot)
+        for at, n in ((0, 2 * quarter_h), (2 * quarter_h, quarter_h), (3 * quarter_h, quarter_h))
+    ]
+    ups = [
+        AlongFirst(
+            up_piece(at, n), [up.at[rows:2 * rows, at:at + n], lnb.at[k, :, 0:n]], at, from_second
+        )
+        for k, (at, n) in enumerate(((0, 2 * quarter_h), (2 * quarter_h, quarter_h)))
+    ]
+    up_last = AcrossFirst(
+        up_piece(3 * quarter_h, quarter_h), up.at[rows:2 * rows, 3 * quarter_h:hidden], hidden, from_second
     )
-    group_b = Group(
-        [(second_t, second_r, gh, gh_r, hidden)], up.at[rows:2 * rows, :], hidden, lambda: flips["second"] + gh_got
+    base = hidden + quarter_h
+    proj_out = AcrossFirst(
+        (gb_t, gb_r, attn_own, heads_r, heads_w),
+        down.at[0:rows, 0:heads_w],
+        base,
+        lambda: flips["gb"] + heads_sent,
     )
-    group_c = Group(
-        [
-            (gb_t, gb_r, attn_own, heads_r, heads_w),
-            (first_t, first_r, dqkv.at[:, q_cols], dqkv_r.at[:, q_cols], heads_w),
-        ],
-        down.at[0:rows, :],
-        2 * hidden,
-        lambda: flips["gb"] + flips["first"] + heads_sent + dq_got,
+    proj_q = AcrossFirst(
+        proj_piece(q_cols),
+        down.at[0:rows, heads_w:2 * heads_w],
+        base + heads_w,
+        lambda: flips["first"] + dq_got,
     )
-    group_d = Group(
-        [(first_t, first_r, dqkv.at[:, c], dqkv_r.at[:, c], heads_w) for c in (k_cols, v_cols)],
-        down.at[rows:2 * rows, :],
-        2 * hidden + 2 * heads_w,
-        lambda: dkv_got,
+    proj_k, proj_v = (
+        AcrossFirst(
+            proj_piece(cols),
+            down.at[rows:2 * rows, c * heads_w:(c + 1) * heads_w],
+            base + (2 + c) * heads_w,
+            lambda: flips["first"] + dkv_got,
+        )
+        for c, cols in enumerate((k_cols, v_cols))
     )
 
+    def share_out():
+        half = heads_w // 2
+        get_out.wait()
+        mine = pl.ds(pl.multiple_of(h * heads_w + core * half, half), half)
+        return copies.start(outw.at[mine, :], outw.at[mine, :], across)
+
+    def forward_out():
+        out_got.wait_recv()
+        half = heads_w // 2
+        theirs = pl.ds(pl.multiple_of((1 - h) * heads_w + core * half, half), half)
+        return copies.start(outw.at[theirs, :], outw.at[theirs, :], seq_peer[1])
+
+    def scenes():
+        for m in (1, 2, 3):
+            seg_got[m].wait_recv()
+        for m in range(4):
+            seg_columns(m)
+
+    def attend_near(i):
+        for copy in kv_got[i][1]:
+            copy.wait_recv()
+        attend_blocks(i, (0, 1), True, False, 0, pairs)
+
+    def prepare_cot():
+        get_cot.wait()
+
+        def part(c):
+            vec[5] += fold(cot[span(c, CHUNK), :].astype(F32))
+
+        loop(2 * rows // CHUNK, part)
+        for i in range(2):
+            flip(cot.at[seq_rows(i), :], i, cot_t)
+        flips["cot"] = swap_rows(cot_t, cot_r)
+
+    def flip_branch():
+        for i in range(2):
+            flip(gb.at[seq_rows(i), :], i, gb_t)
+        flips["gb"] = swap_rows(gb_t, gb_r)
+
+    def vectors():
+        ln1_got.wait_recv()
+        lines = [jnp.sum(vec[k] + ln1_r[k], axis=0, keepdims=True) for k in range(2)]
+        lines += [jnp.sum(vec[k], axis=0, keepdims=True) for k in range(2, 6)]
+        lines += [jnp.sum(qvacc[...], axis=0, keepdims=True)]
+        sums = jnp.sum(upacc[...], axis=0, keepdims=True)
+        lines += [sums[:, c * width:(c + 1) * width] for c in range(hidden // width)]
+        lines += [jnp.zeros((16 - len(lines), width), F32)]
+        vs[0] = jnp.concatenate(lines, axis=0)
+        return copies.start(vs.at[0], vr.at[0], seq_peer[1])
+
+    def vectors_on(k, copy, device):
+        copy.wait_recv()
+        vs[k] = vs[k - 1] + vr[k - 1]
+        return copies.start(vs.at[k], vr.at[k], device)
+
+    def vectors_done():
+        vec_4.wait_recv()
+        vec_o[...] = vs[3] + vr[3]
+
+    spans = [(0, 2 * quarter_h), (2 * quarter_h, quarter_h), (3 * quarter_h, quarter_h)]
+
     get_tok.wait()
-    project(0)
-    project(1)
+    first_norm(0)
+    get_qkv.wait()
+    keys_values(0)
+    meet()
+    send_keys(0)
+    get_out, get_cot = load(outw_h, outw.at[own_out, :]), load(cot_h, cot)
+    get_down, get_up = load(down_h, down), load(up_h, up)
+    first_norm(1)
+    keys_values(1)
+    send_keys(1)
+    queries(0)
+    queries(1)
     flips["first"] = swap_rows(first_t, first_r)
-    get_out.wait()
-    core_rows = pl.ds(pl.multiple_of(h * heads_w + core * (heads_w // 2), heads_w // 2), heads_w // 2)
-    out_got = copies.start(outw.at[core_rows, :], outw.at[core_rows, :], across)
-    for m in (1, 2, 3):
-        seg_got[m].wait_recv()
-    for m in range(4):
-        seg_columns(m)
-    for i in range(2):
-        kv_got[i][1].wait_recv()
-        attend_blocks(i, (0, 1), True, False)
-    get_cot.wait()
-
-    def sum_cot(c):
-        vec[5] += fold(cot[span(c, CHUNK), :].astype(F32))
-
-    loop(2 * rows // CHUNK, sum_cot)
-    for i in range(2):
-        flip(cot.at[seq_rows(i), :], i, cot_t)
-    flips["cot"] = swap_rows(cot_t, cot_r)
-    attend_far(0)
-    attend_far(1)
-    out_got.wait_recv()
-    got_rows = pl.ds(
-        pl.multiple_of((1 - h) * heads_w + core * (heads_w // 2), heads_w // 2), heads_w // 2
-    )
-    out_near = copies.start(outw.at[got_rows, :], outw.at[got_rows, :], seq_peer[1])
+    out_got = share_out()
+    scenes()
+    attend_near(0)
+    attend_near(1)
+    forward_keys(0, 0)
+    prepare_cot()
+    forward_keys(0, 1)
+    attend_far(0, 0)
+    attend_far(0, 1)
+    send_heads(0)
+    out_near = forward_out()
+    get_down.wait()
+    cot_down(0)
+    forward_keys(1, 0)
+    cot_down(1)
+    attend_far(1, 0)
+    forward_keys(1, 1)
+    attend_far(1, 1)
+    send_heads(1)
     out_near.wait_recv()
     get_up.wait()
-    get_down.wait()
-    for i in range(2):
-        middle(i)
-        feed(i)
+    middle(0)
+    feed(0)
+    middle(1)
+    feed(1)
     flips["second"] = swap_rows(second_t, second_r)
+    downs[0].prepare()
+    downs[0].across()
+    ups[0].beside()
+    ups[1].beside()
     feed_out(0)
+    send_feed_out(0)
     feed_out(1)
-    group_a.first()
+    forward_queries(0)
+    forward_queries(1)
     norm2_back(0)
-    attend_back_pairs(0, 0, pairs)
-    keys_near(0)
-    group_a.second()
-    keys_far(0)
-    group_b.first()
+    downs[1].prepare()
+    downs[1].across()
+    back_own(0)
     norm2_back(1)
-    for i in range(2):
-        flip(gb.at[seq_rows(i), :], i, gb_t)
-    flips["gb"] = swap_rows(gb_t, gb_r)
-    near_got[0][0].wait_send()
-    near_got[0][1].wait_send()
-    attend_back_pairs(1, 0, pairs)
-    keys_near(1)
-    keys_done(0)
-    keys_far(1)
-    group_c.first()
+    downs[0].beside()
+    forward_grads(0)
+    downs[2].prepare()
+    downs[2].across()
+    flip_branch()
+    ups[0].beyond()
+    ups[1].beyond()
+    back_far(0)
     first_back(0)
-    group_b.second()
-    finish_output(0)
-    finish_output(1)
-    keys_done(1)
+    send_first_back(0)
+    proj_out.prepare()
+    proj_out.across()
+    back_own(1)
+    forward_grads(1)
+    downs[0].beyond()
+    downs[1].beside()
+    up_last.prepare()
+    up_last.across()
+    downs[2].beside()
+    back_far(1)
     first_back(1)
     ln1_got = copies.start(vec.at[0:2], ln1_r, across)
-    group_d.first()
-    group_c.second()
+    send_first_back(1)
+    send_feed_out(1)
+    proj_q.prepare()
+    proj_q.across()
+    proj_k.prepare()
+    proj_k.across()
+    proj_v.prepare()
+    proj_v.across()
+    downs[1].beyond()
+    downs[2].beyond()
+    ups[0].across()
+    ups[1].across()
+    proj_out.beside()
     norm1_back(0)
-    group_d.second()
+    finish_output(0)
+    vec_1 = vectors()
+    up_last.beside()
+    proj_out.beyond()
+    vec_2 = vectors_on(1, vec_1, seq_peer[2])
+    proj_q.beside()
+    up_last.beyond()
     norm1_back(1)
-
-    ln1_got.wait()
-    lines = [jnp.sum(vec[k] + ln1_r[k], axis=0, keepdims=True) for k in range(2)]
-    lines += [jnp.sum(vec[k], axis=0, keepdims=True) for k in range(2, 6)]
-    lines += [jnp.sum(qvacc[...], axis=0, keepdims=True)]
-    ups = jnp.sum(upacc[...], axis=0, keepdims=True)
-    lines += [ups[:, c * width:(c + 1) * width] for c in range(hidden // width)]
-    lines += [jnp.zeros((16 - len(lines), width), F32)]
-    vs[0] = jnp.concatenate(lines, axis=0)
-    copies.start(vs.at[0], vr.at[0], seq_peer[1]).wait_recv()
-    vs[1] = vs[0] + vr[0]
-    copies.start(vs.at[1], vr.at[1], seq_peer[2]).wait_recv()
-    vs[2] = vs[1] + vr[1]
-    got = [copies.start(vs.at[2], vr.at[1 + d], along[d]) for d in range(1, n_dp)]
-    row = group_a.third(mid, 0, [(downg_h.at[:, pl.ds(c * width, width)], width) for c in range(hidden // width)])
-    row = group_b.third(mid, row, [(upg_h.at[:, pl.ds(c * width, width)], width) for c in range(hidden // width)])
-    row = group_c.third(mid, row, [(outg_h, heads_w), (qkvg_h.at[0], heads_w)])
-    row = group_d.third(mid, row, [(qkvg_h.at[1], heads_w), (qkvg_h.at[2], heads_w)])
-    total = vs[2]
-    for d in range(1, n_dp):
-        got[d - 1].wait_recv()
-        total = total + vr[1 + d]
-    vec_o[...] = total
-    waited = {id(c) for c in gs_got + [g.far for g in (group_a, group_b, group_c, group_d)]}
-    waited |= {id(c) for c in ffn_got + gf_got + near_got[0] + [ln1_got]}
-    for copy in copies.all:
-        if id(copy) not in waited:
-            copy.wait_send()
-    for copy in loads[6:]:
-        copy.wait()
+    proj_k.beside()
+    proj_q.beyond()
+    proj_v.beside()
+    proj_k.beyond()
+    vec_3 = vectors_on(2, vec_2, beside)
+    finish_output(1)
+    proj_v.beyond()
+    vec_4 = vectors_on(3, vec_3, beyond)
+    place = 0
+    for group, (at, n) in zip(downs, spans): place = group.done(place, downg_h.at[:, at:at + n])
+    for group, (at, n) in zip(ups + [up_last], spans): place = group.done(place, upg_h.at[:, at:at + n])
+    place = proj_out.done(place, outg_h)
+    place = proj_q.done(place, qkvg_h.at[0])
+    place = proj_k.done(place, qkvg_h.at[1])
+    place = proj_v.done(place, qkvg_h.at[2])
+    vectors_done()
+    copies.finish()
 
 
 def one_kernel(args):
@@ -912,13 +1125,12 @@
     n_dp = axis_size("dp")
     block = width // (4 * n_dp)
     total = count * rows
-    grads = 2 * hidden + 4 * heads_w
+    grads = hidden + hidden // 4 + 4 * heads_w
     line = lambda v: v.reshape(1, -1)
     low = lambda *shape: pltpu.VMEM(shape, LOW)
     full = lambda *shape: pltpu.VMEM(shape, F32)
     shape = jax.ShapeDtypeStruct
     vmem, anywhere = pl.BlockSpec(memory_space=pltpu.VMEM), pl.BlockSpec(memory_space=pl.ANY)
-    seg = jnp.concatenate([segment_ids, jnp.zeros((8 - count, rows), jnp.int32)], axis=0)
     return pl.pallas_call(
         functools.partial(layer_kernel, n_dp),
         in_specs=[anywhere, vmem, vmem, vmem, anywhere, vmem, anywhere, vmem, vmem, vmem, anywhere, vmem, anywhere, vmem, anywhere],
@@ -934,25 +1146,27 @@
         ],
         scratch_shapes=[
             low(total, width), low(total, width), low(3, width, heads_w), low(2 * heads_w, width),
-            low(width, hidden), low(hidden, width), low(total, heads_w), low(2, 4, rows, 2 * heads_w),
+            low(width, hidden), low(hidden, width), low(total, heads_w), low(2, 4, 2, rows, heads_w),
             full(2, heads_w, rows), low(total, width), full(total, width), low(2, rows, width),
             low(total, hidden), low(total, hidden),
             low(width, total), low(width, total), low(width, total), low(width, total),
-            low(2, rows, heads_w), low(2, rows, 2 * heads_w), low(total, width), low(total, width),
+            low(2, rows, heads_w), low(total, width), low(total, width),
             full(2, total, 2), full(2, heads_w // LANES, 8, rows),
-            low(total, width), low(total, width), low(total, width), low(2, 3, rows, 2 * heads_w),
+            low(total, width), low(total, width), low(total, width), low(2, rows, 2 * heads_w),
+            low(2, 2, rows, heads_w), low(2, 2, rows, heads_w), full(2, 2, heads_w // LANES, 8, rows),
             low(total, hidden), low(total, hidden),
             low(2, width // 4, total), low(2, width // 4, total), low(2, width // 4, total), low(2, width // 4, total),
-            low(total, heads_w), low(total, 3 * heads_w), low(width // 4, grads), low(n_dp - 1, block, grads),
+            low(total, heads_w), low(total, 3 * heads_w), low(width // 4, grads), low(3, block, grads),
+            low(block, 3 * hidden // 4), low(2, 3, block, 3 * hidden // 4),
             pltpu.VMEM((4, 8, rows), jnp.int32), full(4, rows, 8), full(6, 8, width), full(8, 2 * heads_w), full(8, hidden),
-            full(2, 8, width), full(3, 16, width), full(n_dp + 1, 16, width),
+            full(2, 8, width), full(4, 16, width), full(4, 16, width),
             pltpu.SemaphoreType.DMA((N_COPIES,)), pltpu.SemaphoreType.DMA((N_COPIES,)), pltpu.SemaphoreType.DMA((N_LOCAL,)),
         ],
         compiler_params=pltpu.CompilerParams(
             collective_id=0, has_side_effects=True, vmem_limit_bytes=FAST_VMEM
         ),
     )(
-        tokens.reshape(total, width), seg, line(ln1_gain), line(ln1_bias), jnp.transpose(qkv_weight, (1, 0, 2)),
+        tokens.reshape(total, width), segment_ids, line(ln1_gain), line(ln1_bias), jnp.transpose(qkv_weight, (1, 0, 2)),
         qv_bias, out_weight, line(out_bias), line(ln2_gain), line(ln2_bias), up_weight, line(up_bias),
         down_weight, line(down_bias), out_cotangent.reshape(total, width),
     )
@@ -972,32 +1186,77 @@
     )
 
 
+def split_kernel(parts, index_ref, vec_ref, *refs):
+    big = (len(refs) - 1 - 8) // 3
+    sources, targets, small = refs[:big], refs[big:2 * big], refs[2 * big:2 * big + 8]
+    held, sem = refs[2 * big + 8:-1], refs[-1]
+    moves = [pltpu.make_async_copy(a, b, sem.at[0, k]) for k, (a, b) in enumerate(zip(sources, held))]
+    for move in moves:
+        move.start()
+    back = [pltpu.make_async_copy(a, b, sem.at[1, k]) for k, (a, b) in enumerate(zip(held, targets))]
+    for move, out in zip(moves, back):
+        move.wait()
+        out.start()
+    at = index_ref[0]
+    width = vec_ref.shape[1]
+
+    def piece(row, size):
+        shift = lax.rem(width - lax.rem(at * size, width), width)
+        return pltpu.roll(vec_ref[row:row + 1, :], shift, 1)[:, :size]
+
+    size = width // parts
+    for ref, row in zip(small[:6], (0, 1, 2, 3, 4, 5)):
+        ref[...] = piece(row, size)
+    half = vec_ref[6:7, :]
+    shift = lax.rem(width - at * (size // 2), width)
+    turned = pltpu.roll(half, shift, 1)
+    small[6][0:1, :] = turned[:, :size // 2]
+    small[6][1:2, :] = pltpu.roll(turned, width // 2, 1)[:, :size // 2]
+    size = small[7].shape[1]
+    low, high = piece(7, size), piece(8, size)
+    small[7][...] = jnp.where(at * size < width, low, high)
+    for out in back:
+        out.wait()
+
+
+def split(parts, big, vec):
+    at = lax.axis_index("seq") * axis_size("dp") + lax.axis_index("dp")
+    size = vec.shape[1] // parts
+    shape = jax.ShapeDtypeStruct
+    smalls = [shape((1, size), F32)] * 6 + [shape((2, size // 2), F32), shape((1, 2 * size), F32)]
+    vmem, anywhere = pl.BlockSpec(memory_space=pltpu.VMEM), pl.BlockSpec(memory_space=pl.ANY)
+    out = pl.pallas_call(
+        functools.partial(split_kernel, parts),
+        in_specs=[pl.BlockSpec(memory_space=pltpu.SMEM), vmem] + [anywhere] * len(big),
+        out_specs=[anywhere] * len(big) + [vmem] * 8,
+        out_shape=[shape(v.shape, v.dtype) for v in big] + smalls,
+        scratch_shapes=[pltpu.VMEM(v.shape, v.dtype) for v in big] + [pltpu.SemaphoreType.DMA((2, len(big)))],
+        compiler_params=pltpu.CompilerParams(vmem_limit_bytes=FAST_VMEM),
+    )(at.astype(jnp.int32).reshape(1), vec, *big)
+    return out[:len(big)], out[len(big):]
+
+
 def fast(*args):
     tokens = args[0]
-    out, tokens_grad, down_grad, up_grad, out_grad, qkv_grad, vec = one_kernel(args)
-    n_dp = axis_size("dp")
-    at = lax.axis_index("seq") * n_dp + lax.axis_index("dp")
-    parts = axis_size("seq") * n_dp
-
-    def mine(values):
-        size = values.shape[-1] // parts
-        return lax.dynamic_slice_in_dim(values, at * size, size, values.ndim - 1)
-
+    *big, vec = one_kernel(args)
+    big, small = split(axis_size("seq") * axis_size("dp"), big, vec)
+    out, tokens_grad, down_grad, up_grad, out_grad, qkv_grad = big
+    flat = [v.reshape(-1) for v in small]
     return (
         out.reshape(tokens.shape),
         tokens_grad.reshape(tokens.shape),
-        mine(vec[0]),
-        mine(vec[1]),
+        flat[0],
+        flat[1],
         jnp.transpose(qkv_grad, (1, 0, 2)),
-        mine(vec[6].reshape(2, -1)),
+        small[6],
         out_grad.T,
-        mine(vec[2]),
-        mine(vec[3]),
-        mine(vec[4]),
+        flat[2],
+        flat[3],
+        flat[4],
         up_grad,
-        mine(vec[7:9].reshape(-1)),
+        flat[7],
         down_grad.T,
-        mine(vec[5]),
+        flat[5],
     )
 
 

time: 199 us -> 144 us (0.72)
  Pallas kernels: 184 us -> 143 us
  local copies, waits for them, and re-layouts: 13.8 us -> 0 us
    pallas_call x1, Pallas kernels: 184 us -> 138 us  [one_kernel(): pl.pallas_call(functools.partial(layer_kernel, n_dp), in_specs=[anywhere,...]
    unnamed x16 -> x0, local copies, waits for them, and re-layouts: 8.38 us -> none
    pallas_call x0 -> x1, Pallas kernels: none -> 4.6 us  [split(): pl.pallas_call(functools.partial(split_kernel, parts), in_specs=[pl.Block...]
    dynamic_slice x5 -> x0, local copies, waits for them, and re-layouts: 2.98 us -> none  [mine(): return lax.dynamic_slice_in_dim(values, at * size, size, values.ndim - 1)]
where the time goes in v3:
time: 144 us; the launch traced here: 143 us
  Pallas kernels  143 us (99%)
    pallas_call x1, Pallas kernels, one_kernel(): pl.pallas_call(functools.partial(layer_kernel, n_dp), in_specs=[anywhere,...  138 us
    pallas_call x1, Pallas kernels, split(): pl.pallas_call(functools.partial(split_kernel, parts), in_specs=[pl.Block...  4.6 us

profile of v3, /device:TPU:0, one launch (start us, length us, event | category | flops | bytes accessed | tf_op | source)
XLA Modules:
  0.0 143.3 jit_solution(16872833488072706097)
XLA Ops:
  0.7 137.9 %shard_map.254 = (bf16[512,1024]{1,0:T(8,128)(2,1)}, bf16[512,1024]{1,0:T(8,128)(2,1)}, f32[64,2048]{1,0:T(8,128)}, f32[64,2048]{1,0:T(8,128)}, f32[64,512]{1,0:...) custom-call(bf16[512,1024]{1,0:T(8,128)(2,1)} %bitcast.24, s32[2,256]{1,0:T(2,128)} %refs_1_.1, f32[1,1024]{1,0:T(1,128)} %bitcast.27, ...), custom_call_target="tpu_custom_call" | custom-call | tf_op jit(solution)/shard_map/pallas_call | solution.py:1134
  138.6 4.6 %shard_map.255 = (bf16[512,1024]{1,0:T(8,128)(2,1)}, bf16[512,1024]{1,0:T(8,128)(2,1)}, f32[64,2048]{1,0:T(8,128)}, f32[64,2048]{1,0:T(8,128)}, f32[64,512]{1,0:...) custom-call(s32[1]{0:T(128)} %bitcast.index_ref, ...), custom_call_target="tpu_custom_call" | custom-call | tf_op jit(solution)/shard_map/pallas_call | solution.py:1228

commit v4 on v3

--- a/solution.py
+++ b/solution.py
@@ -277,12 +277,12 @@
 WIDE = 512
 
 
-def loop(count, body):
+def loop(count, body, unroll=1, start=0):
     def step(i, carry):
         body(i)
         return carry
 
-    lax.fori_loop(0, count, step, 0)
+    lax.fori_loop(start, start + count, step, 0, unroll=unroll)
 
 
 def span(i, size):
@@ -429,7 +429,7 @@
             stat[0, at, 1:2] = inverse
             lnb[i, span(c, CHUNK), :] = (v * inverse * g1[...] + b1[...]).astype(LOW)
 
-        loop(rows // CHUNK, norm)
+        loop(rows // CHUNK, norm, 4)
 
     def keys_values(i):
         k = dot(lnb[i], wqkv[1]).astype(LOW)
@@ -461,42 +461,61 @@
         lane = lax.rem(p, 2) * LANES
         return p // 2, pl.ds(pl.multiple_of(lane, LANES), LANES), pl.ds(pl.multiple_of(half_w + lane, LANES), LANES)
 
+    def twice(row):
+        return jnp.concatenate([row, row], axis=1)
+
+    def both(stats, k):
+        return jnp.concatenate([stats[k:k + 1, :], stats[k + 1:k + 2, :]], axis=1)
+
+    def cols_of(head):
+        return slice(head * rows, (head + 1) * rows)
+
+    def heads_of(pair_value, scale=None):
+        if scale is not None:
+            pair_value = pair_value * jnp.asarray(scale, LOW)
+        zeros = jnp.zeros_like(pair_value)
+        return [jnp.where(half_lanes(pair_value.shape, head), pair_value, zeros) for head in range(2)]
+
     def attend_blocks(i, blocks, begin, end, start, stop):
-        seg_q = segs[0, i:i + 1, :].astype(F32)
+        seg_q = twice(segs[0, i:i + 1, :].astype(F32))
 
         def pair(p):
             lanes = span(p, LANES)
             part, k_lanes, v_lanes = key_lanes(p)
-            qp = q[seq_rows(i), lanes] * jnp.asarray(0.125, LOW)
-            vts = [kv[i, m, part, :, v_lanes].T for m in blocks]
+            qs = jnp.concatenate(heads_of(q[seq_rows(i), lanes], 0.125), axis=0)
+            old = top = None if begin else both(st[i, p], 0)
+            scores = []
+            for m in blocks:
+                score = dot(kv[i, m, part, :, k_lanes], qs, NT)
+                score = jnp.where(segk[m, :, i:i + 1] == seg_q, score, MASKED)
+                peak = jnp.max(score, axis=0, keepdims=True)
+                top = peak if top is None else jnp.maximum(top, peak)
+                scores.append(score)
+            total, mixed = 0.0, [0.0, 0.0]
+            for m, score in zip(blocks, scores):
+                w = jnp.exp(score - top)
+                total = total + jnp.sum(w, axis=0, keepdims=True)
+                low = w.astype(LOW)
+                vt = kv[i, m, part, :, v_lanes].T
+                for head in range(2):
+                    mixed[head] = mixed[head] + dot(vt[head * HEAD_DIM:(head + 1) * HEAD_DIM, :], low[:, cols_of(head)])
+            if not begin:
+                scale = jnp.exp(old - top)
+                total = total + scale * both(st[i, p], 2)
+            if end:
+                inverse, lse = 1.0 / total, top + jnp.log(total)
             for head in range(2):
                 at = pl.ds(pl.multiple_of(p * LANES + head * HEAD_DIM, HEAD_DIM), HEAD_DIM)
-                qh = jnp.where(half_lanes(qp.shape, head), qp, jnp.zeros_like(qp))
-                parts = []
-                top = None if begin else st[i, p, head:head + 1, :]
-                old = top
-                for m in blocks:
-                    score = dot(kv[i, m, part, :, k_lanes], qh, NT)
-                    score = jnp.where(segk[m, :, i:i + 1] == seg_q, score, MASKED)
-                    peak = jnp.max(score, axis=0, keepdims=True)
-                    top = peak if top is None else jnp.maximum(top, peak)
-                    parts.append(score)
-                total = mixed = 0.0
-                for score, vt in zip(parts, vts):
-                    w = jnp.exp(score - top)
-                    total = total + jnp.sum(w, axis=0, keepdims=True)
-                    mixed = mixed + dot(vt[head * HEAD_DIM:(head + 1) * HEAD_DIM, :], w.astype(LOW))
+                value = mixed[head]
                 if not begin:
-                    scale = jnp.exp(old - top)
-                    total = total + scale * st[i, p, 2 + head:3 + head, :]
-                    mixed = mixed + scale * attn_t[i, at, :]
+                    value = value + scale[:, cols_of(head)] * attn_t[i, at, :]
                 if end:
-                    mixed = mixed / total
-                    st[i, p, 4 + head:5 + head, :] = top + jnp.log(total)
+                    value = value * inverse[:, cols_of(head)]
+                    st[i, p, 4 + head:5 + head, :] = lse[:, cols_of(head)]
                 else:
-                    st[i, p, head:head + 1, :] = top
-                    st[i, p, 2 + head:3 + head, :] = total
-                attn_t[i, at, :] = mixed
+                    st[i, p, head:head + 1, :] = top[:, cols_of(head)]
+                    st[i, p, 2 + head:3 + head, :] = total[:, cols_of(head)]
+                attn_t[i, at, :] = value
             if end:
                 to = pl.ds(pl.multiple_of(h * heads_w + p * LANES, LANES), LANES)
                 attn[seq_rows(i), to] = attn_t[i, lanes, :].T.astype(LOW)
@@ -551,9 +570,10 @@
             stat[1, at, 1:2] = inverse
             lnb[i, span(c, CHUNK), :] = (v * inverse * g2[...] + b2[...]).astype(LOW)
 
-        loop(rows // CHUNK, norm)
-
-    gs_got, ffn_got, act_got, gh_got = [None] * 2, [None] * 2, [None] * 2, [None] * 2
+        loop(rows // CHUNK, norm, 4)
+
+    gs_got, ffn_got = [None] * 2, [None] * 2
+    act_got, gh_got = [[None] * 2, [None] * 2], [[None] * 2, [None] * 2]
 
     def cot_down(i):
         def tile(j):
@@ -562,7 +582,7 @@
 
         loop(hidden // (2 * WIDE), tile)
 
-    def feed(i):
+    def feed(i, part):
         at_rows = seq_rows(i)
 
         def tile(j):
@@ -573,15 +593,20 @@
             gh[at_rows, at] = g
             upacc[:, at] += fold(g.astype(F32))
 
-        loop(hidden // WIDE, tile)
+        tiles_each = hidden // WIDE // 2
+        loop(tiles_each, tile, 1, part * tiles_each)
+        cols = slice(part * hidden // 2, (part + 1) * hidden // 2)
+        act_got[i][part] = copies.start(act.at[at_rows, cols], act_r.at[at_rows, cols], seq_peer[1])
+        gh_got[i][part] = copies.start(gh.at[at_rows, cols], gh_r.at[at_rows, cols], seq_peer[1])
+
+    def feed_back(i):
+        at_rows = seq_rows(i)
 
         def back(j):
             gs[at_rows, span(j, WIDE)] = dot(gh[at_rows, :], up[span(j, WIDE), :], NT).astype(LOW)
 
         loop(width // WIDE, back)
         gs_got[i] = copies.start(gs.at[at_rows, :], gs_r.at[at_rows, :], across)
-        act_got[i] = copies.start(act.at[at_rows, :], act_r.at[at_rows, :], seq_peer[1])
-        gh_got[i] = copies.start(gh.at[at_rows, :], gh_r.at[at_rows, :], seq_peer[1])
         flip(lnb.at[i], i, second_t)
 
     def feed_out(i):
@@ -603,7 +628,7 @@
             both = ffn[at, :].astype(F32) + ffn_r[at, :].astype(F32)
             ffn[at, :] = (mid[at, :] + both + downb[...]).astype(LOW)
 
-        loop(rows // CHUNK, part)
+        loop(rows // CHUNK, part, 4)
         load(ffn.at[seq_rows(i), :], out_h.at[seq_rows(i), :])
 
     gb = down.at[2 * rows:4 * rows, :]
@@ -626,7 +651,7 @@
             gb[at, :] = low
             vec[2] += fold(low.astype(F32))
 
-        loop(rows // CHUNK, part)
+        loop(rows // CHUNK, part, 4)
 
         w_rows = pl.ds(pl.multiple_of(h * heads_w, heads_w), heads_w)
         g_attn[i] = dot(gb[seq_rows(i), :], outw[w_rows, :], NT).astype(LOW)
@@ -654,44 +679,32 @@
             copies.start(st_far.at[i, 0], st_far.at[i, 1], seq_peer[1]),
         ]
 
-    def heads_of(pair_value, scale=None):
-        if scale is not None:
-            pair_value = pair_value * jnp.asarray(scale, LOW)
-        zeros = jnp.zeros_like(pair_value)
-        return [jnp.where(half_lanes(pair_value.shape, head), pair_value, zeros) for head in range(2)]
-
-    def backward_terms(allowed, k, v, q_scaled, g, stats, head):
-        score = dot(k, q_scaled[head], NT)
-        probs = jnp.exp(jnp.where(allowed, score - stats[4 + head:5 + head, :], MASKED))
-        return probs.astype(LOW), (probs * (dot(v, g[head], NT) - stats[6 + head:7 + head, :])).astype(LOW)
+    def backward_terms(allowed, k, v, q_scaled, g, lse, delta):
+        probs = jnp.exp(jnp.where(allowed, dot(k, q_scaled, NT) - lse, MASKED))
+        return probs.astype(LOW), (probs * (dot(v, g, NT) - delta)).astype(LOW)
 
     def back_own(i):
-        seg_q = segs[0, i:i + 1, :].astype(F32)
+        seg_q = twice(segs[0, i:i + 1, :].astype(F32))
 
         def pair(p):
             lanes = span(p, LANES)
             v_lanes = pl.ds(pl.multiple_of(heads_w + p * LANES, LANES), LANES)
             part, k_in, v_in = key_lanes(p)
-            qs = heads_of(q[seq_rows(i), lanes])
-            q_scaled = heads_of(q[seq_rows(i), lanes], 0.125)
-            g = heads_of(g_attn[i, :, lanes])
-            stats = st[i, p]
+            qs = jnp.concatenate(heads_of(q[seq_rows(i), lanes]), axis=0)
+            q_scaled = qs * jnp.asarray(0.125, LOW)
+            g = jnp.concatenate(heads_of(g_attn[i, :, lanes]), axis=0)
+            lse, delta = both(st[i, p], 4), both(st[i, p], 6)
             dqt = [0.0, 0.0]
             for m in range(4):
                 k = kv[i, m, part, :, k_in]
                 kt = k.T
                 v = kv[i, m, part, :, v_in]
-                allowed = segk[m, :, i:i + 1] == seg_q
-                dk = dv = 0.0
+                probs, ds = backward_terms(segk[m, :, i:i + 1] == seg_q, k, v, q_scaled, g, lse, delta)
+                if m < 2:
+                    parts_kv[i][m][:, lanes] = (dot(ds, qs) * 0.125).astype(LOW)
+                    parts_kv[i][m][:, v_lanes] = dot(probs, g).astype(LOW)
                 for head in range(2):
-                    probs, ds = backward_terms(allowed, k, v, q_scaled, g, stats, head)
-                    if m < 2:
-                        dk = dk + dot(ds, qs[head])
-                        dv = dv + dot(probs, g[head])
-                    dqt[head] = dqt[head] + dot(kt[head * HEAD_DIM:(head + 1) * HEAD_DIM, :], ds)
-                if m < 2:
-                    parts_kv[i][m][:, lanes] = (dk * 0.125).astype(LOW)
-                    parts_kv[i][m][:, v_lanes] = dv.astype(LOW)
+                    dqt[head] = dqt[head] + dot(kt[head * HEAD_DIM:(head + 1) * HEAD_DIM, :], ds[:, cols_of(head)])
             dq = (jnp.concatenate(dqt, axis=0).T * 0.125).astype(LOW)
             dqkv[seq_rows(i), lanes] = dq
             qvacc[:, lanes] += fold(dq.astype(F32))
@@ -706,7 +719,7 @@
         for copy in g_next[i]:
             copy.wait_recv()
         near_got[i].wait_recv()
-        seg_q = [segs[2 + b, i:i + 1, :].astype(F32) for b in range(2)]
+        seg_q = [twice(segs[2 + b, i:i + 1, :].astype(F32)) for b in range(2)]
         at_rows = seq_rows(i)
 
         def pair(p):
@@ -717,14 +730,13 @@
             v = kv[i, 0, part, :, v_in]
             dk = dv = 0.0
             for b in range(2):
-                qs = heads_of(q_far[i, b, :, lanes])
-                q_scaled = heads_of(q_far[i, b, :, lanes], 0.125)
-                g = heads_of(g_far[i, b, :, lanes])
-                allowed = segk[0, :, i:i + 1] == seg_q[b]
-                for head in range(2):
-                    probs, ds = backward_terms(allowed, k, v, q_scaled, g, st_far[i, b, p], head)
-                    dk = dk + dot(ds, qs[head])
-                    dv = dv + dot(probs, g[head])
+                qs = jnp.concatenate(heads_of(q_far[i, b, :, lanes]), axis=0)
+                q_scaled = qs * jnp.asarray(0.125, LOW)
+                g = jnp.concatenate(heads_of(g_far[i, b, :, lanes]), axis=0)
+                lse, delta = both(st_far[i, b, p], 4), both(st_far[i, b, p], 6)
+                probs, ds = backward_terms(segk[0, :, i:i + 1] == seg_q[b], k, v, q_scaled, g, lse, delta)
+                dk = dk + dot(ds, qs)
+                dv = dv + dot(probs, g)
             near = lambda to: parts_kv[i][0][:, to].astype(F32) + dkv_r[i, :, to].astype(F32)
             k_at = pl.ds(pl.multiple_of(heads_w + p * LANES, LANES), LANES)
             v_at = pl.ds(pl.multiple_of(2 * heads_w + p * LANES, LANES), LANES)
@@ -760,7 +772,7 @@
             vec[0] += fold(g * normed)
             vec[1] += fold(g)
 
-        loop(rows // CHUNK, sums)
+        loop(rows // CHUNK, sums, 4)
 
     def send_first_back(i):
         gf_got[i] = copies.start(gs.at[seq_rows(i), :], gf_r.at[seq_rows(i), :], across)
@@ -777,7 +789,7 @@
             e = e - jnp.mean(e, axis=-1, keepdims=True) - normed * jnp.mean(e * normed, axis=-1, keepdims=True)
             gs[at, :] = (gb[at, :].astype(F32) + inverse * e).astype(LOW)
 
-        loop(rows // CHUNK, part)
+        loop(rows // CHUNK, part, 4)
         load(gs.at[seq_rows(i), :], tg_h.at[seq_rows(i), :])
 
     def tiles(piece, chip, body):
@@ -900,19 +912,25 @@
     up_piece = lambda at, n: (second_t, second_r, gh.at[:, at:at + n], gh_r.at[:, at:at + n], n)
     proj_piece = lambda at: (first_t, first_r, dqkv.at[:, at], dqkv_r.at[:, at], heads_w)
     quarter_h = hidden // 4
-    from_cot, from_second = lambda: flips["cot"] + act_got, lambda: flips["second"] + gh_got
+    halves_of = lambda got, at: [got[i][at // (2 * quarter_h)] for i in range(2)]
+    from_cot = lambda at: lambda: flips["cot"] + halves_of(act_got, at)
+    from_second = lambda at: lambda: flips["second"] + halves_of(gh_got, at)
+    spans = [(0, 2 * quarter_h), (2 * quarter_h, quarter_h), (3 * quarter_h, quarter_h)]
     downs = [
-        AcrossFirst(down_piece(at, n), up.at[0:rows, at:at + n], at, from_cot)
-        for at, n in ((0, 2 * quarter_h), (2 * quarter_h, quarter_h), (3 * quarter_h, quarter_h))
+        AcrossFirst(down_piece(at, n), lnb.at[0] if k == 0 else up.at[0:rows, at:at + n], at, from_cot(at))
+        for k, (at, n) in enumerate(spans)
     ]
     ups = [
         AlongFirst(
-            up_piece(at, n), [up.at[rows:2 * rows, at:at + n], lnb.at[k, :, 0:n]], at, from_second
+            up_piece(at, n),
+            [up.at[rows:2 * rows, at:at + n], up.at[0:rows, 0:n] if k == 0 else lnb.at[1, :, 0:n]],
+            at,
+            from_second(at),
         )
-        for k, (at, n) in enumerate(((0, 2 * quarter_h), (2 * quarter_h, quarter_h)))
+        for k, (at, n) in enumerate(spans[:2])
     ]
     up_last = AcrossFirst(
-        up_piece(3 * quarter_h, quarter_h), up.at[rows:2 * rows, 3 * quarter_h:hidden], hidden, from_second
+        up_piece(3 * quarter_h, quarter_h), up.at[rows:2 * rows, 3 * quarter_h:hidden], hidden, from_second(3 * quarter_h)
     )
     base = hidden + quarter_h
     proj_out = AcrossFirst(
@@ -966,7 +984,7 @@
         def part(c):
             vec[5] += fold(cot[span(c, CHUNK), :].astype(F32))
 
-        loop(2 * rows // CHUNK, part)
+        loop(2 * rows // CHUNK, part, 4)
         for i in range(2):
             flip(cot.at[seq_rows(i), :], i, cot_t)
         flips["cot"] = swap_rows(cot_t, cot_r)
@@ -995,8 +1013,6 @@
     def vectors_done():
         vec_4.wait_recv()
         vec_o[...] = vs[3] + vr[3]
-
-    spans = [(0, 2 * quarter_h), (2 * quarter_h, quarter_h), (3 * quarter_h, quarter_h)]
 
     get_tok.wait()
     first_norm(0)
@@ -1034,12 +1050,16 @@
     out_near.wait_recv()
     get_up.wait()
     middle(0)
-    feed(0)
+    feed(0, 0)
+    feed(0, 1)
+    feed_back(0)
     middle(1)
-    feed(1)
-    flips["second"] = swap_rows(second_t, second_r)
+    feed(1, 0)
+    feed(1, 1)
     downs[0].prepare()
     downs[0].across()
+    feed_back(1)
+    flips["second"] = swap_rows(second_t, second_r)
     ups[0].beside()
     ups[1].beside()
     feed_out(0)
@@ -1064,12 +1084,12 @@
     send_first_back(0)
     proj_out.prepare()
     proj_out.across()
+    up_last.prepare()
+    up_last.across()
     back_own(1)
     forward_grads(1)
     downs[0].beyond()
     downs[1].beside()
-    up_last.prepare()
-    up_last.across()
     downs[2].beside()
     back_far(1)
     first_back(1)

time: 144 us -> 138 us (0.958)
  Pallas kernels: 143 us -> 137 us
    pallas_call x1, Pallas kernels: 138 us -> 132 us  [one_kernel(): pl.pallas_call(functools.partial(layer_kernel, n_dp), in_specs=[anywhere,...]
where the time goes in v4:
time: 138 us
  Pallas kernels  137 us (99%)
    pallas_call x1, Pallas kernels, one_kernel(): pl.pallas_call(functools.partial(layer_kernel, n_dp), in_specs=[anywhere,...  132 us
    pallas_call x1, Pallas kernels, split(): pl.pallas_call(functools.partial(split_kernel, parts), in_specs=[pl.Block...  4.6 us

profile of v4, /device:TPU:0, one launch (start us, length us, event | category | flops | bytes accessed | tf_op | source)
XLA Modules:
  0.0 137.6 jit_solution(5263681468059300991)
XLA Ops:
  0.7 132.2 %shard_map.254 = (bf16[512,1024]{1,0:T(8,128)(2,1)}, bf16[512,1024]{1,0:T(8,128)(2,1)}, f32[64,2048]{1,0:T(8,128)}, f32[64,2048]{1,0:T(8,128)}, f32[64,512]{1,0:...) custom-call(bf16[512,1024]{1,0:T(8,128)(2,1)} %bitcast.24, s32[2,256]{1,0:T(2,128)} %refs_1_.1, f32[1,1024]{1,0:T(1,128)} %bitcast.27, ...), custom_call_target="tpu_custom_call" | custom-call | tf_op jit(solution)/shard_map/pallas_call | solution.py:1154
  132.8 4.6 %shard_map.255 = (bf16[512,1024]{1,0:T(8,128)(2,1)}, bf16[512,1024]{1,0:T(8,128)(2,1)}, f32[64,2048]{1,0:T(8,128)}, f32[64,2048]{1,0:T(8,128)}, f32[64,512]{1,0:...) custom-call(s32[1]{0:T(128)} %bitcast.index_ref, ...), custom_call_target="tpu_custom_call" | custom-call | tf_op jit(solution)/shard_map/pallas_call | solution.py:1248

commit v5 on v4

--- a/solution.py
+++ b/solution.py
@@ -431,19 +431,14 @@
 
         loop(rows // CHUNK, norm, 4)
 
-    def keys_values(i):
-        k = dot(lnb[i], wqkv[1]).astype(LOW)
-        v = (dot(lnb[i], wqkv[2]) + qvb[1:2, :]).astype(LOW)
-        for part in range(2):
-            cols = slice(part * half_w, (part + 1) * half_w)
-            kv[i, 0, part, :, 0:half_w] = k[:, cols]
-            kv[i, 0, part, :, half_w:heads_w] = v[:, cols]
-
-    def send_keys(i):
-        for part in range(2):
-            kv_got[i][2][part] = copies.start(kv.at[i, 0, part], kv.at[i, 2, part], seq_peer[2])
-        for part in range(2):
-            kv_got[i][1][part] = copies.start(kv.at[i, 0, part], kv.at[i, 1, part], seq_peer[1])
+    def keys_values(i, part):
+        cols = slice(part * half_w, (part + 1) * half_w)
+        kv[i, 0, part, :, 0:half_w] = dot(lnb[i], wqkv[1, :, cols]).astype(LOW)
+        kv[i, 0, part, :, half_w:heads_w] = (dot(lnb[i], wqkv[2, :, cols]) + qvb[1:2, cols]).astype(LOW)
+
+    def send_keys(i, part):
+        for m in (2, 1):
+            kv_got[i][m][part] = copies.start(kv.at[i, 0, part], kv.at[i, m, part], seq_peer[m])
 
     def queries(i):
         q[seq_rows(i), :] = (dot(lnb[i], wqkv[0]) + qvb[0:1, :]).astype(LOW)
@@ -526,7 +521,7 @@
         segk[m] = segs[m].astype(F32).T
 
     own_heads = pl.ds(pl.multiple_of(h * heads_w, heads_w), heads_w)
-    attn_got = [None, None]
+    attn_got = [[], []]
 
     def forward_keys(i, part):
         kv_got[i][2][part].wait_recv()
@@ -540,15 +535,18 @@
         kv_got[i][3][part].wait_recv()
         attend_blocks(i, (2, 3), False, True, part * pairs // 2, (part + 1) * pairs // 2)
 
-    def send_heads(i):
-        mine = attn.at[seq_rows(i), own_heads]
-        attn_got[i] = copies.start(mine, mine, across)
-        heads_sent[i] = copies.start(mine, heads_r.at[seq_rows(i), :], seq_peer[1])
-
-    heads_sent = [None, None]
+    def send_heads(i, part):
+        to = pl.ds(pl.multiple_of(h * heads_w + part * half_w, half_w), half_w)
+        mine = attn.at[seq_rows(i), to]
+        attn_got[i].append(copies.start(mine, mine, across))
+        there = heads_r.at[seq_rows(i), part * half_w:(part + 1) * half_w]
+        heads_sent.append(copies.start(mine, there, seq_peer[1]))
+
+    heads_sent = []
 
     def middle(i):
-        attn_got[i].wait_recv()
+        for copy in attn_got[i]:
+            copy.wait_recv()
 
         def tile(j):
             at = span(j, WIDE)
@@ -824,10 +822,10 @@
 
     def hand_out(place, target, value):
         size = target.shape[1]
-        top, left = place // 2 * block, place % 2 * (width // 2)
+        top, left = place // 4 * block, place % 4 * (width // 4)
         mid[top:top + block, left:left + size] = value(slice(None))
         load(mid.at[top:top + block, left:left + size], target)
-        return place + size * 2 // width
+        return place + size * 4 // width
 
     class AcrossFirst:
         def __init__(self, piece, hold, offset, arrivals):
@@ -910,7 +908,7 @@
     flips = {}
     down_piece = lambda at, n: (cot_t, cot_r, act.at[:, at:at + n], act_r.at[:, at:at + n], n)
     up_piece = lambda at, n: (second_t, second_r, gh.at[:, at:at + n], gh_r.at[:, at:at + n], n)
-    proj_piece = lambda at: (first_t, first_r, dqkv.at[:, at], dqkv_r.at[:, at], heads_w)
+    proj_piece = lambda at, n: (first_t, first_r, dqkv.at[:, at], dqkv_r.at[:, at], n)
     quarter_h = hidden // 4
     halves_of = lambda got, at: [got[i][at // (2 * quarter_h)] for i in range(2)]
     from_cot = lambda at: lambda: flips["cot"] + halves_of(act_got, at)
@@ -940,20 +938,25 @@
         lambda: flips["gb"] + heads_sent,
     )
     proj_q = AcrossFirst(
-        proj_piece(q_cols),
+        proj_piece(q_cols, heads_w),
         down.at[0:rows, heads_w:2 * heads_w],
         base + heads_w,
         lambda: flips["first"] + dq_got,
     )
-    proj_k, proj_v = (
+    from_proj = lambda: flips["first"] + dkv_got
+    proj_k = AcrossFirst(
+        proj_piece(k_cols, heads_w), down.at[rows:2 * rows, 0:heads_w], base + 2 * heads_w, from_proj
+    )
+    v_halves = [slice(heads_w + c * half_w, heads_w + (c + 1) * half_w) for c in range(2)]
+    proj_v = [
         AcrossFirst(
-            proj_piece(cols),
-            down.at[rows:2 * rows, c * heads_w:(c + 1) * heads_w],
-            base + (2 + c) * heads_w,
-            lambda: flips["first"] + dkv_got,
+            proj_piece(slice(heads_w + at.start, heads_w + at.stop), half_w),
+            down.at[rows:2 * rows, at],
+            base + 2 * heads_w + at.start,
+            from_proj,
         )
-        for c, cols in enumerate((k_cols, v_cols))
-    )
+        for at in v_halves
+    ]
 
     def share_out():
         half = heads_w // 2
@@ -1017,14 +1020,18 @@
     get_tok.wait()
     first_norm(0)
     get_qkv.wait()
-    keys_values(0)
+    keys_values(0, 0)
     meet()
-    send_keys(0)
+    send_keys(0, 0)
+    keys_values(0, 1)
+    send_keys(0, 1)
     get_out, get_cot = load(outw_h, outw.at[own_out, :]), load(cot_h, cot)
     get_down, get_up = load(down_h, down), load(up_h, up)
     first_norm(1)
-    keys_values(1)
-    send_keys(1)
+    keys_values(1, 0)
+    send_keys(1, 0)
+    keys_values(1, 1)
+    send_keys(1, 1)
     queries(0)
     queries(1)
     flips["first"] = swap_rows(first_t, first_r)
@@ -1036,17 +1043,19 @@
     prepare_cot()
     forward_keys(0, 1)
     attend_far(0, 0)
+    send_heads(0, 0)
     attend_far(0, 1)
-    send_heads(0)
+    send_heads(0, 1)
     out_near = forward_out()
     get_down.wait()
     cot_down(0)
     forward_keys(1, 0)
     cot_down(1)
     attend_far(1, 0)
+    send_heads(1, 0)
     forward_keys(1, 1)
     attend_far(1, 1)
-    send_heads(1)
+    send_heads(1, 1)
     out_near.wait_recv()
     get_up.wait()
     middle(0)
@@ -1071,15 +1080,15 @@
     downs[1].prepare()
     downs[1].across()
     back_own(0)
+    ups[0].beyond()
     norm2_back(1)
     downs[0].beside()
     forward_grads(0)
     downs[2].prepare()
     downs[2].across()
     flip_branch()
-    ups[0].beyond()
+    back_far(0)
     ups[1].beyond()
-    back_far(0)
     first_back(0)
     send_first_back(0)
     proj_out.prepare()
@@ -1088,9 +1097,9 @@
     up_last.across()
     back_own(1)
     forward_grads(1)
-    downs[0].beyond()
     downs[1].beside()
     downs[2].beside()
+    downs[0].beyond()
     back_far(1)
     first_back(1)
     ln1_got = copies.start(vec.at[0:2], ln1_r, across)
@@ -1100,29 +1109,33 @@
     proj_q.across()
     proj_k.prepare()
     proj_k.across()
-    proj_v.prepare()
-    proj_v.across()
+    proj_v[0].prepare()
+    proj_v[0].across()
+    proj_v[1].prepare()
+    proj_v[1].across()
+    proj_out.beside()
+    norm1_back(0)
     downs[1].beyond()
     downs[2].beyond()
-    ups[0].across()
-    ups[1].across()
-    proj_out.beside()
-    norm1_back(0)
     finish_output(0)
     vec_1 = vectors()
     up_last.beside()
     proj_out.beyond()
     vec_2 = vectors_on(1, vec_1, seq_peer[2])
+    ups[0].across()
+    ups[1].across()
     proj_q.beside()
     up_last.beyond()
     norm1_back(1)
     proj_k.beside()
     proj_q.beyond()
-    proj_v.beside()
+    proj_v[0].beside()
     proj_k.beyond()
+    proj_v[1].beside()
+    proj_v[0].beyond()
     vec_3 = vectors_on(2, vec_2, beside)
     finish_output(1)
-    proj_v.beyond()
+    proj_v[1].beyond()
     vec_4 = vectors_on(3, vec_3, beyond)
     place = 0
     for group, (at, n) in zip(downs, spans): place = group.done(place, downg_h.at[:, at:at + n])
@@ -1130,7 +1143,7 @@
     place = proj_out.done(place, outg_h)
     place = proj_q.done(place, qkvg_h.at[0])
     place = proj_k.done(place, qkvg_h.at[1])
-    place = proj_v.done(place, qkvg_h.at[2])
+    for group, c in zip(proj_v, range(2)): place = group.done(place, qkvg_h.at[2, :, c * half_w:(c + 1) * half_w])
     vectors_done()
     copies.finish()
 

time: 138 us -> 133 us (0.964)
  Pallas kernels: 137 us -> 132 us
    pallas_call x1, Pallas kernels: 132 us -> 127 us  [one_kernel(): pl.pallas_call(functools.partial(layer_kernel, n_dp), in_specs=[anywhere,...]
where the time goes in v5:
time: 133 us
  Pallas kernels  132 us (99%)
    pallas_call x1, Pallas kernels, one_kernel(): pl.pallas_call(functools.partial(layer_kernel, n_dp), in_specs=[anywhere,...  127 us
    pallas_call x1, Pallas kernels, split(): pl.pallas_call(functools.partial(split_kernel, parts), in_specs=[pl.Block...  4.6 us

profile of v5, /device:TPU:0, one launch (start us, length us, event | category | flops | bytes accessed | tf_op | source)
XLA Modules:
  0.0 132.9 jit_solution(15988898921358858933)
XLA Ops:
  0.7 127.4 %shard_map.254 = (bf16[512,1024]{1,0:T(8,128)(2,1)}, bf16[512,1024]{1,0:T(8,128)(2,1)}, f32[64,2048]{1,0:T(8,128)}, f32[64,2048]{1,0:T(8,128)}, f32[64,512]{1,0:...) custom-call(bf16[512,1024]{1,0:T(8,128)(2,1)} %bitcast.24, s32[2,256]{1,0:T(2,128)} %refs_1_.1, f32[1,1024]{1,0:T(1,128)} %bitcast.27, ...), custom_call_target="tpu_custom_call" | custom-call | tf_op jit(solution)/shard_map/pallas_call | solution.py:1167
  128.1 4.6 %shard_map.255 = (bf16[512,1024]{1,0:T(8,128)(2,1)}, bf16[512,1024]{1,0:T(8,128)(2,1)}, f32[64,2048]{1,0:T(8,128)}, f32[64,2048]{1,0:T(8,128)}, f32[64,512]{1,0:...) custom-call(s32[1]{0:T(128)} %bitcast.index_ref, ...), custom_call_target="tpu_custom_call" | custom-call | tf_op jit(solution)/shard_map/pallas_call | solution.py:1261

commit v6 on v5

--- a/solution.py
+++ b/solution.py
@@ -1125,11 +1125,11 @@
     ups[0].across()
     ups[1].across()
     proj_q.beside()
-    up_last.beyond()
     norm1_back(1)
     proj_k.beside()
+    up_last.beyond()
+    proj_v[0].beside()
     proj_q.beyond()
-    proj_v[0].beside()
     proj_k.beyond()
     proj_v[1].beside()
     proj_v[0].beyond()

time: 133 us -> 135 us (1.015)
  Pallas kernels: 132 us -> 134 us
    pallas_call x1, Pallas kernels: 127 us -> 129 us  [one_kernel(): pl.pallas_call(functools.partial(layer_kernel, n_dp), in_specs=[anywhere,...]
where the time goes in v6:
time: 135 us; the launch traced here: 134 us
  Pallas kernels  134 us (99%)
    pallas_call x1, Pallas kernels, one_kernel(): pl.pallas_call(functools.partial(layer_kernel, n_dp), in_specs=[anywhere,...  129 us
    pallas_call x1, Pallas kernels, split(): pl.pallas_call(functools.partial(split_kernel, parts), in_specs=[pl.Block...  4.6 us

profile of v6, /device:TPU:0, one launch (start us, length us, event | category | flops | bytes accessed | tf_op | source)
XLA Modules:
  0.0 134.4 jit_solution(5223711247063096522)
XLA Ops:
  0.7 128.9 %shard_map.254 = (bf16[512,1024]{1,0:T(8,128)(2,1)}, bf16[512,1024]{1,0:T(8,128)(2,1)}, f32[64,2048]{1,0:T(8,128)}, f32[64,2048]{1,0:T(8,128)}, f32[64,512]{1,0:...) custom-call(bf16[512,1024]{1,0:T(8,128)(2,1)} %bitcast.24, s32[2,256]{1,0:T(2,128)} %refs_1_.1, f32[1,1024]{1,0:T(1,128)} %bitcast.27, ...), custom_call_target="tpu_custom_call" | custom-call | tf_op jit(solution)/shard_map/pallas_call | solution.py:1167
  129.6 4.6 %shard_map.255 = (bf16[512,1024]{1,0:T(8,128)(2,1)}, bf16[512,1024]{1,0:T(8,128)(2,1)}, f32[64,2048]{1,0:T(8,128)}, f32[64,2048]{1,0:T(8,128)}, f32[64,512]{1,0:...) custom-call(s32[1]{0:T(128)} %bitcast.index_ref, ...), custom_call_target="tpu_custom_call" | custom-call | tf_op jit(solution)/shard_map/pallas_call | solution.py:1261
